TPU v7x, 32 devices: a whole 2x2x4 slice. The times are simulated.
32 devices in a mesh: pix: 8 (over z, x), tm: 4 (over y, core).
Axes of the slice: x: 2, y: 2, z: 4, core: 2. Of those that a mesh axis runs over, the one named last changes fastest.
Arguments:
- query: bfloat16 [4, 8, 1024, 1152], P('tm', 'pix'), may hold values from -5 to 5, as said below
- key_in: bfloat16 [4, 8, 1024, 1152], P('tm', 'pix'), may hold values from -5 to 5, as said below
- value: bfloat16 [4, 8, 1024, 1152], P('tm', 'pix'), may hold values from -6 to 6
- mask: int32 [8, 8], replicated, may hold values from 0 to 1, as said below
- w_out: bfloat16 [1152, 1152], replicated, may hold values from -0.1875 to 0.1875
Outputs:
- result: bfloat16 [4, 8, 1024, 1152], P('tm', 'pix')
Inputs may be any that keep to these rules, and one draw needn't show every extreme that they name: `mask`: the diagonal is 1 everywhere; the table is a dilated pattern of block pairs with some further pairs set. `query`: entries of order one. `key_in`: entries of order one.
All inputs are finite; a program needn't handle non-finite values.
Results may differ from a plain program's by a relative error of at most 0.012.
Values may be sent and summed in bfloat16 or wider, within the bound.
No kernel may reach another device: no remote copies, remote signals or barrier semaphores. Data moves between devices by JAX's collectives and lax.ppermute only.
A program may use at most 192 MiB of HBM per device.

v0:
```python
import jax
import jax.numpy as jnp
from jax import lax
from jax.sharding import PartitionSpec as P

HDIM = 72


def block_table(first, count, blen, mask):
    nblk = mask.shape[0]
    blocks = (first + jnp.arange(count, dtype=jnp.int32)) // blen
    onehot = (blocks[:, None] == jnp.arange(nblk, dtype=jnp.int32)[None, :]).astype(jnp.float32)
    return onehot


def attend(carry, queries, q_first, keys, values, k_first, mask, blen):
    nq, width, feats = queries.shape
    nk = keys.shape[0]
    heads = feats // HDIM
    scale = 1.0 / HDIM**0.5
    q_hot = block_table(q_first, nq, blen, mask)
    k_hot = block_table(k_first, nk, blen, mask)
    allowed = jnp.dot(jnp.dot(q_hot, mask.astype(jnp.float32)), k_hot.T) > 0.5
    qh = queries.reshape(nq, width, heads, HDIM)
    kh = keys.reshape(nk, width, heads, HDIM)
    vh = values.reshape(nk, width, heads, HDIM)
    scores = jnp.einsum("iphd,jphd->phij", qh, kh, preferred_element_type=jnp.float32) * scale
    m_old, l_old, acc_old = carry
    m_new = jnp.maximum(m_old, jnp.max(jnp.where(allowed, scores, -1e30), axis=-1))
    expo = jnp.where(allowed, jnp.exp(scores - m_new[..., None]), 0.0)
    l_new = jnp.sum(expo, axis=-1)
    summed = jnp.einsum(
        "phij,jphd->iphd", expo.astype(jnp.bfloat16), vh, preferred_element_type=jnp.float32
    )
    return (m_new, l_new, summed)


def start_carry(count, width, feats):
    heads = feats // HDIM
    m_init = jnp.full((width, heads, count), -1e30, jnp.float32)
    l_init = jnp.zeros((width, heads, count), jnp.float32)
    acc_init = jnp.zeros((count, width, heads, HDIM), jnp.float32)
    return (m_init, l_init, acc_init)


def finish(carry, feats):
    m_last, l_last, acc_last = carry
    normed = acc_last / jnp.transpose(l_last, (2, 0, 1))[..., None]
    return normed.reshape(acc_last.shape[0], acc_last.shape[1], feats).astype(jnp.bfloat16)


def per_device(query, key_in, value, mask, w_out):
    feats = query.shape[3]
    n_time = lax.axis_size("tm")
    qx, kx, vx = (
        lax.all_to_all(query, "pix", split_axis=2, concat_axis=1, tiled=True),
        lax.all_to_all(key_in, "pix", split_axis=2, concat_axis=1, tiled=True),
        lax.all_to_all(value, "pix", split_axis=2, concat_axis=1, tiled=True),
    )
    group_frames = qx.shape[1]
    width = qx.shape[2]
    frames_all = group_frames * n_time
    blen = frames_all // mask.shape[0]
    queries = qx.reshape(group_frames, width, feats)
    q_first = lax.axis_index("tm") * group_frames
    kp = lax.all_gather(kx, "tm", axis=0, tiled=True)
    vp = lax.all_gather(vx, "tm", axis=0, tiled=True)
    count = kp.shape[0] * group_frames
    keys = kp.reshape(count, width, feats)
    values = vp.reshape(count, width, feats)
    carry = attend(
        start_carry(group_frames, width, feats),
        queries,
        q_first,
        keys,
        values,
        jnp.int32(0) * group_frames,
        mask,
        blen,
    )
    attended = finish(carry, feats).reshape(1, group_frames, width, feats)
    back = lax.all_to_all(attended, "pix", split_axis=1, concat_axis=2, tiled=True)
    rows = back.shape[1] * back.shape[2]
    projected = jnp.dot(back.reshape(rows, feats), w_out, preferred_element_type=jnp.float32)
    return projected.astype(jnp.bfloat16).reshape(back.shape)


def solution(mesh):
    placed = (
        P("tm", "pix", None, None),
        P("tm", "pix", None, None),
        P("tm", "pix", None, None),
        P(),
        P(),
    )
    return jax.shard_map(
        per_device,
        mesh=mesh,
        in_specs=placed,
        out_specs=P("tm", "pix", None, None),
        check_vma=False,
    )
```

profile of v0, /device:TPU:0, one launch (start us, length us, event | category | flops | bytes accessed | tf_op | source)
XLA Modules:
  0.0 516.2 jit_solution(7040138688606647934)
XLA Ops:
  6.5 0.0 copy-start
  6.5 0.0 all-gather.3.cloned.1.call-start
  6.5 7.6 %copy.43 = bf16[1,1,1024,1152]{3,1,0,2:T(2,128)(2,1)} copy(bf16[1,1,1024,1152]{3,2,1,0:T(8,128)(2,1)} %param.6) | data formatting | bytes 4718592 | tf_op args[1]
  14.1 0.5 broadcast.77
  14.6 16.3 %reduce.2 = bf16[1024,1152]{1,0:T(8,128)(2,1)} reduce(bf16[1024,1,1,1152]{3,2,1,0:T(2,128)(2,1)} %bitcast.34, bf16[]{:T(256)} %broadcast.77), dimensions={1,2}, to_apply=%bitcast.30.reduce_sub_computation | reduce | bytes 4718594
  30.9 6.0 %reshape.73 = bf16[8,2,73728]{2,1,0:T(2,128)(2,1)} reshape(bf16[1024,1152]{1,0:T(8,128)(2,1)} %reduce.2) | data formatting | bytes 4718592
  36.9 61.2 %all_to_all.42 = bf16[8,2,73728]{2,1,0:T(2,128)(2,1)} all-to-all(bf16[8,2,73728]{2,1,0:T(2,128)(2,1)} %reshape.73), channel_id=1, replica_groups=mesh['pix'=8,'tm'=4] {'pix'}, dimensions={0} | all-to-all | bytes 4718592 | tf_op jit(solution)/shard_map/all_to_all | solution.py:57
  98.1 7.0 %reshape.74 = bf16[1024,1,1,1152]{3,2,1,0:T(2,128)(2,1)} reshape(bf16[8,2,73728]{2,1,0:T(2,128)(2,1)} %all_to_all.42) | data formatting | bytes 4718592
  105.1 4.1 copy.33
  109.2 0.0 all-gather.3.cloned.1.call-update
  109.2 0.2 all-gather.5.cloned.1.call-start
  109.5 7.7 %copy.42 = bf16[1,1,1024,1152]{3,1,0,2:T(2,128)(2,1)} copy(bf16[1,1,1024,1152]{3,2,1,0:T(8,128)(2,1)} %param.7) | data formatting | bytes 4718592 | tf_op args[2]
  117.2 16.4 %reduce.4 = bf16[1024,1152]{1,0:T(8,128)(2,1)} reduce(bf16[1024,1,1,1152]{3,2,1,0:T(2,128)(2,1)} %bitcast.38, bf16[]{:T(256)} %broadcast.77), dimensions={1,2}, to_apply=%bitcast.29.reduce_sub_computation | reduce | bytes 4718594
  133.6 6.0 %reshape.77 = bf16[8,2,73728]{2,1,0:T(2,128)(2,1)} reshape(bf16[1024,1152]{1,0:T(8,128)(2,1)} %reduce.4) | data formatting | bytes 4718592
  139.5 57.3 %all_to_all.43 = bf16[8,2,73728]{2,1,0:T(2,128)(2,1)} all-to-all(bf16[8,2,73728]{2,1,0:T(2,128)(2,1)} %reshape.77), channel_id=1, replica_groups=mesh['pix'=8,'tm'=4] {'pix'}, dimensions={0} | all-to-all | bytes 4718592 | tf_op jit(solution)/shard_map/all_to_all | solution.py:58
  196.9 7.0 %reshape.78 = bf16[1024,1,1,1152]{3,2,1,0:T(2,128)(2,1)} reshape(bf16[8,2,73728]{2,1,0:T(2,128)(2,1)} %all_to_all.43) | data formatting | bytes 4718592
  203.8 4.1 copy.34
  207.9 0.0 all-gather.5.cloned.1.call-update
  207.9 7.7 %copy.44 = bf16[1,1,1024,1152]{3,1,0,2:T(2,128)(2,1)} copy(bf16[1,1,1024,1152]{3,2,1,0:T(8,128)(2,1)} %param.5) | data formatting | bytes 4718592 | tf_op args[0]
  215.6 16.4 %reduce.3 = bf16[1024,1152]{1,0:T(8,128)(2,1)} reduce(bf16[1024,1,1,1152]{3,2,1,0:T(2,128)(2,1)} %bitcast.37, bf16[]{:T(256)} %broadcast.77), dimensions={1,2}, to_apply=%bitcast.31.reduce_sub_computation | reduce | bytes 4718594
  232.1 0.0 copy-start.2
  232.1 6.0 %reshape.75 = bf16[8,2,73728]{2,1,0:T(2,128)(2,1)} reshape(bf16[1024,1152]{1,0:T(8,128)(2,1)} %reduce.3) | data formatting | bytes 4718592
  238.1 4.6 all-to-all-start
  242.7 0.0 copy-done.2
  242.7 0.3 fusion.17
  243.0 52.0 %all-to-all-done = bf16[8,2,73728]{2,1,0:T(2,128)(2,1)} async-done(((bf16[8,2,73728]{2,1,0:T(2,128)(2,1)}), bf16[8,2,73728]{2,1,0:T(2,128)(2,1)}, u32[]{:S(2)}, u32[]{:S(2)}) %all-to-all-start) | async-done | bytes 2359328 | tf_op jit(solution)/shard_map/all_to_all | solution.py:56
  295.0 7.0 %reshape.76 = bf16[1024,1,1,1152]{3,2,1,0:T(2,128)(2,1)} reshape(bf16[8,2,73728]{2,1,0:T(2,128)(2,1)} %all-to-all-done) | data formatting | bytes 4718592
  302.0 16.3 %bitcast_reduce_fusion = bf16[1024,1152]{1,0:T(8,128)(2,1)} fusion(bf16[1024,1,1,1152]{3,2,1,0:T(2,128)(2,1)} %reshape.76), kind=kLoop, calls=%fused_computation.34 | loop fusion | bytes 4718592 | tf_op jit(solution)/shard_map/all_to_all | solution.py:56
  318.4 9.6 %reshape.71 = bf16[8,128,16,72]{3,2,1,0:T(8,128)(2,1)} reshape(bf16[1024,1152]{1,0:T(8,128)(2,1)} %bitcast_reduce_fusion) | data formatting | bytes 4718592 | tf_op jit(solution)/shard_map/reshape;reshape | solution.py:24
  328.0 0.0 all-gather.3.cloned.1.call-done
  328.0 12.6 %copy.22 = bf16[4,8,128,1152]{2,3,1,0:T(8,128)(2,1)} copy(bf16[4,8,128,1152]{3,2,1,0:T(8,128)(2,1)} %all-gather.3.cloned.1.call-done) | data formatting | bytes 18874368 | tf_op jit(solution)/shard_map/all_gather | solution.py:66
  340.6 21.1 %copy.24 = bf16[32,128,16,72]{3,0,2,1:T(8,128)(2,1)} copy(bf16[32,128,16,72]{1,3,2,0:T(8,128)(2,1)} %bitcast.32) | data formatting | bytes 18874368 | tf_op jit(solution)/shard_map/reshape;reshape | solution.py:25
  361.7 16.0 %select_reduce_fusion = (f32[128,16,8]{2,1,0:T(8,128)}, f32[128,16,8,32]{3,2,1,0:T(8,128)}) fusion(pred[8,32]{1,0:T(8,128)(4,1)S(1)} %fusion.17, bf16[32,128,16,72]{3,0,2,1:T(8,128)(2,1)} %copy.24, bf16[8,128,16,72]{3,2,1,0:T(8,128)(2,1)} %reshape.71), kind=kOutput, calls=%fused_computation.3 | convolution fusion | flops 77053952 | bytes 13959424 | tf_op jit(solution)/shard_map/iphd,jphd->phij/dot_general | solution.py:27
  377.8 2.3 broadcast_maximum_fusion
  380.1 0.0 all-gather.5.cloned.1.call-done
  380.1 12.6 %copy.26 = bf16[4,8,128,1152]{2,3,1,0:T(8,128)(2,1)} copy(bf16[4,8,128,1152]{3,2,1,0:T(8,128)(2,1)} %all-gather.5.cloned.1.call-done) | data formatting | bytes 18874368 | tf_op jit(solution)/shard_map/all_gather | solution.py:67
  392.7 21.1 %copy.27 = bf16[32,128,16,72]{3,0,2,1:T(8,128)(2,1)} copy(bf16[32,128,16,72]{1,3,2,0:T(8,128)(2,1)} %bitcast.33) | data formatting | bytes 18874368 | tf_op jit(solution)/shard_map/reshape;reshape | solution.py:26
  413.8 0.0 copy-start.1
  413.8 7.5 %fusion.1 = f32[128,16,8]{2,1,0:T(8,128)S(1)} fusion(f32[128,16,8,32]{3,2,1,0:T(8,128)} %get-tuple-element.6, f32[128,16,8]{2,1,0:T(8,128)} %broadcast_maximum_fusion, pred[8,32]{1,0:T(8,128)(4,1)S(1)} %fusion.17), kind=kLoop, calls=%fused_computation.4 | loop fusion | flops 2080768 | bytes 2228480 | tf_op jit(solution)/shard_map/reduce_sum | solution.py:31
  421.3 0.0 copy-done.1
  421.3 13.1 %fusion = bf16[8,128,16,72]{3,0,2,1:T(8,128)(2,1)} fusion(f32[8,128,16]{0,2,1:T(8,128)S(1)} %bitcast.43, bf16[32,128,16,72]{3,0,2,1:T(8,128)(2,1)} %copy.27, f32[128,16,8,32]{3,2,1,0:T(8,128)} %get-tuple-element.6, f32[128,16,8]{2,1,0:T(8,128)S(1)} %copy-done.1, pred[8,32]{1,0:T(8,128)(4,1)S(1)} %fusion.17), kind=kOutput, calls=%fused_computation.1 | convolution fusion | flops 79953920 | bytes 14024960 | tf_op jit(solution)/shard_map/phij,jphd->iphd/dot_general | solution.py:32
  434.4 6.2 %copy.28 = bf16[8,128,16,72]{1,3,2,0:T(8,128)(2,1)} copy(bf16[8,128,16,72]{3,0,2,1:T(8,128)(2,1)} %fusion) | data formatting | bytes 4718592 | tf_op jit(solution)/shard_map/convert_element_type | solution.py:49
  440.6 57.8 %all_to_all.44 = bf16[1,8,128,1152]{2,3,0,1:T(8,128)(2,1)} all-to-all(bf16[1,8,128,1152]{2,3,0,1:T(8,128)(2,1)} %bitcast.41), channel_id=1, replica_groups=mesh['pix'=8,'tm'=4] {'pix'}, dimensions={1} | all-to-all | bytes 4718592 | tf_op jit(solution)/shard_map/all_to_all | solution.py:82
  498.5 4.4 copy.30
  502.8 0.0 copy-done
  502.8 6.6 %fusion.11 = bf16[1,1,1024,1152]{3,2,1,0:T(8,128)(2,1)} fusion(bf16[1024,1152]{1,0:T(8,128)(2,1)} %bitcast.42, bf16[1152,1152]{1,0:T(8,128)(2,1)S(1)} %copy-done), kind=kOutput, calls=%fused_computation.14 | convolution fusion | flops 2719088640 | bytes 7372800 | tf_op jit(solution)/shard_map/dot_general | solution.py:84
  (2 shorter events, 0.0 us)
Async XLA Ops:
  6.5 496.3 %copy-start = (bf16[1152,1152]{1,0:T(8,128)(2,1)S(1)}, bf16[1152,1152]{1,0:T(8,128)(2,1)}, u32[]{:S(2)}) copy-start(bf16[1152,1152]{1,0:T(8,128)(2,1)} %param.9) | copy-start | bytes 7962628
  6.5 321.5 %all-gather.3.cloned.1.call-start = ((), (), s32[]{:S(2)}) async-start(), calls=%async_computation.4 | async-start | bytes 11796480 | tf_op jit(solution)/shard_map/all_gather | solution.py:66
  109.2 270.8 %all-gather.5.cloned.1.call-start = ((), (), s32[]{:S(2)}) async-start(), calls=%async_computation.5 | async-start | bytes 11796480 | tf_op jit(solution)/shard_map/all_gather | solution.py:67
  232.1 10.7 %copy-start.2 = (s32[8,8]{1,0:T(8,128)S(1)}, s32[8,8]{1,0:T(8,128)}, u32[]{:S(2)}) copy-start(s32[8,8]{1,0:T(8,128)} %param.8) | copy-start | bytes 772
  238.1 57.0 %all-to-all-start = ((bf16[8,2,73728]{2,1,0:T(2,128)(2,1)}), bf16[8,2,73728]{2,1,0:T(2,128)(2,1)}, u32[]{:S(2)}, u32[]{:S(2)}) async-start(bf16[8,2,73728]{2,1,0:T(2,128)(2,1)} %reshape.75), calls=%async_computation | async-start | bytes 4718592 | tf_op jit(solution)/shard_map/all_to_all | solution.py:56
  413.8 7.5 %copy-start.1 = (f32[128,16,8]{2,1,0:T(8,128)S(1)}, f32[128,16,8]{2,1,0:T(8,128)}, u32[]{:S(2)}) copy-start(f32[128,16,8]{2,1,0:T(8,128)} %broadcast_maximum_fusion) | copy-start | bytes 196612
Sparse Core Ops, SparseCore 0:
  109.3 63.2 all-gather.2
  208.1 63.1 all-gather.4
where the time goes:
time: 520 us; the launch traced here: 516 us
  blocking collectives  176 us (34%)
  local copies, waits for them, and re-layouts  175 us (34%)
  other arithmetic  58.9 us (11%)
  waiting for transfers between devices  52 us (10%)
  matrix products  36 us (7%)
  between operations  13.5 us (3%)
    unnamed x18, local copies, waits for them, and re-layouts  70.5 us
    all_to_all x1, blocking collectives, per_device(): lax.all_to_all(key_in, 'pix', split_axis=2, concat_axis=1, tiled=True)  61.2 us
    all_to_all x1, blocking collectives, per_device(): lax.all_to_all(attended, 'pix', split_axis=1, concat_axis=2, tiled=True)  57.8 us
    all_to_all x1, blocking collectives, per_device(): lax.all_to_all(value, 'pix', split_axis=2, concat_axis=1, tiled=True)  57.3 us
    all_to_all x1, waiting for transfers between devices, per_device(): lax.all_to_all(query, 'pix', split_axis=2, concat_axis=1, tiled=True)  52 us
    unnamed x3, other arithmetic  49.1 us
    another operation x1, local copies, waits for them, and re-layouts, attend(): kh = keys.reshape(nk, width, heads, HDIM)  21.1 us
    another operation x1, local copies, waits for them, and re-layouts, attend(): vh = values.reshape(nk, width, heads, HDIM)  21.1 us
  transfers between devices with their start and end apart: 3, of which 1 were waited for; matrix products, arithmetic and copies ran while one was open for 30% of the time, Pallas kernels for 0%

commit v1 on v0

v1 whole, which is shorter than its diff:
```python
import functools
import math

import jax
import jax.numpy as jnp
from jax import lax
from jax.experimental import pallas as pl
from jax.experimental.pallas import tpu as pltpu
from jax.sharding import PartitionSpec as P

HDIM = 72
LANES = 128
SUB = 8


def attend_kernel(qkv_ref, bias_ref, w_ref, out_ref, acc_ref):
    frames, _, _, sub, feats = qkv_ref.shape
    rows = frames * sub
    scale = math.log2(math.e) / HDIM**0.5
    for head in range(feats // HDIM):
        low, high = head * HDIM, (head + 1) * HDIM
        start, stop = low // LANES * LANES, -(-high // LANES) * LANES
        lane = lax.broadcasted_iota(jnp.int32, (1, stop - start), 1) + start
        mine = (lane >= low) & (lane < high)
        q = qkv_ref[:, 0, 0, :, start:stop].reshape(rows, stop - start)
        k = qkv_ref[:, 0, 1, :, start:stop].reshape(rows, stop - start)
        v = qkv_ref[:, 0, 2, :, start:stop].reshape(rows, stop - start)
        q = jnp.where(mine, q, jnp.zeros_like(q))
        scores = lax.dot_general(q, k, (((1,), (1,)), ((), ())), preferred_element_type=jnp.float32)
        scores = scores * scale + bias_ref[...]
        expo = jnp.exp2(scores - jnp.max(scores, axis=1, keepdims=True))
        total = jnp.sum(expo, axis=1, keepdims=True)
        summed = jnp.dot(expo.astype(jnp.bfloat16), v, preferred_element_type=jnp.float32)
        acc_ref[:, start:stop] = jnp.where(mine, summed / total, acc_ref[:, start:stop])
    attended = acc_ref[...].astype(jnp.bfloat16)
    projected = jnp.dot(attended, w_ref[...], preferred_element_type=jnp.float32)
    out_ref[...] = projected.astype(jnp.bfloat16).reshape(out_ref.shape)


def attend(qkv, bias, w_out):
    frames, groups, _, sub, feats = qkv.shape
    rows = frames * sub
    return pl.pallas_call(
        attend_kernel,
        grid=(groups,),
        in_specs=[
            pl.BlockSpec((frames, 1, 3, sub, feats), lambda g: (0, g, 0, 0, 0)),
            pl.BlockSpec((rows, rows), lambda g: (0, 0)),
            pl.BlockSpec((feats, feats), lambda g: (0, 0)),
        ],
        out_specs=pl.BlockSpec((frames, 1, sub, feats), lambda g: (0, g, 0, 0)),
        out_shape=jax.ShapeDtypeStruct((frames, groups, sub, feats), jnp.bfloat16),
        scratch_shapes=[pltpu.VMEM((rows, feats), jnp.float32)],
        compiler_params=pltpu.CompilerParams(vmem_limit_bytes=48 * 2**20),
        cost_estimate=pl.CostEstimate(
            flops=groups * rows * feats * (feats + 4 * rows) * 2, bytes_accessed=groups * rows * feats * 8, transcendentals=0
        ),
    )(qkv, bias, w_out)


def bias_of(mask, frame_of_row, patch_of_row, blen):
    block = frame_of_row // blen
    allowed = (mask[block][:, block] > 0) & (patch_of_row[:, None] == patch_of_row[None, :])
    return jnp.where(allowed, 0.0, -1e30).astype(jnp.float32)


def plain(query, key_in, value, mask, w_out):
    axes = ("tm", "pix")
    _, _, patches, feats = query.shape
    frames = lax.axis_size(axes)
    width, heads = patches // frames, feats // HDIM
    moved = [
        lax.all_to_all(a.reshape(frames, width, feats), axes, split_axis=0, concat_axis=0, tiled=True)
        .reshape(frames, width, heads, HDIM)
        for a in (query, key_in, value)
    ]
    block = jnp.arange(frames, dtype=jnp.int32) // (frames // mask.shape[0])
    allowed = mask[block][:, block] > 0
    scores = jnp.einsum("iphd,jphd->phij", moved[0], moved[1], preferred_element_type=jnp.float32) / HDIM**0.5
    scores = jnp.where(allowed, scores, -1e30)
    expo = jnp.exp(scores - jnp.max(scores, axis=-1, keepdims=True))
    total = jnp.transpose(jnp.sum(expo, axis=-1), (2, 0, 1))[..., None]
    summed = jnp.einsum("phij,jphd->iphd", expo.astype(jnp.bfloat16), moved[2], preferred_element_type=jnp.float32)
    attended = (summed / total).astype(jnp.bfloat16).reshape(frames, width, feats)
    projected = jnp.dot(attended, w_out, preferred_element_type=jnp.float32).astype(jnp.bfloat16)
    back = lax.all_to_all(projected, axes, split_axis=0, concat_axis=0, tiled=True)
    return back.reshape(query.shape)


def per_device(query, key_in, value, mask, w_out):
    axes = ("tm", "pix")
    _, _, patches, feats = query.shape
    frames = lax.axis_size(axes)
    if patches % (frames * SUB) != 0:
        return plain(query, key_in, value, mask, w_out)
    groups = patches // (frames * SUB)
    row = jnp.arange(frames * SUB, dtype=jnp.int32)
    bias = bias_of(mask, row // SUB, row % SUB, frames // mask.shape[0])
    parts = [a.reshape(groups, frames, SUB, feats) for a in (query, key_in, value)]
    packed = jnp.stack(parts, axis=1).transpose(2, 0, 1, 3, 4)
    qkv = lax.all_to_all(packed, axes, split_axis=0, concat_axis=0, tiled=True)
    out = attend(qkv, bias, w_out)
    back = lax.all_to_all(out, axes, split_axis=0, concat_axis=0, tiled=True)
    return back.transpose(1, 0, 2, 3).reshape(query.shape)


def solution(mesh):
    placed = P("tm", "pix", None, None)
    return jax.shard_map(
        per_device, mesh=mesh, in_specs=(placed, placed, placed, P(), P()), out_specs=placed, check_vma=False
    )
```

time: 520 us -> 246 us (0.47)
  local copies, waits for them, and re-layouts: 175 us -> 3.49 us
  blocking collectives: 176 us -> 59.6 us
  waiting for transfers between devices: 52 us -> 155 us
  other arithmetic: 58.9 us -> 6.52 us
  matrix products: 36 us -> 0 us
  between operations: 13.5 us -> 0.07 us
  Pallas kernels: 0 us -> 13 us
    all_to_all x3 -> x1, blocking collectives: 176 us -> 59.6 us  [per_device(): back = lax.all_to_all(out, axes, split_axis=0, concat_axis=0, tiled=True)]
    all_to_all x1, waiting for transfers between devices: 52 us -> 155 us  [per_device(): qkv = lax.all_to_all(packed, axes, split_axis=0, concat_axis=0, tiled=True)]
    unnamed x18 -> x4, local copies, waits for them, and re-layouts: 70.5 us -> 0.01 us
    another operation x3 -> x0, local copies, waits for them, and re-layouts: 51.9 us -> none  [the longest x1 21.1 us: attend(): kh = keys.reshape(nk, width, heads, HDIM)]
    unnamed x3 -> x0, other arithmetic: 49.1 us -> none
    dot_general x4 -> x0, matrix products: 36 us -> none  [the longest x1 16 us: attend(): jnp.einsum('iphd,jphd->phij', qh, kh, preferred_element_type=jnp.float32)]
    all_gather x2 -> x0, local copies, waits for them, and re-layouts: 25.2 us -> none  [the longest x1 12.6 us: per_device(): kp = lax.all_gather(kx, 'tm', axis=0, tiled=True)]
    all_to_all x2 -> x0, local copies, waits for them, and re-layouts: 20.7 us -> none  [the longest x1 16.3 us: per_device(): lax.all_to_all(query, 'pix', split_axis=2, concat_axis=1, tiled=True)]
  transfers between devices with their start and end apart: 3 -> 1, of which waited for: 1 -> 1; matrix products, arithmetic and copies ran while one was open for 30% -> 1% of each run, Pallas kernels for 0% -> 0%
where the time goes in v1:
time: 246 us; the launch traced here: 245 us
  waiting for transfers between devices  155 us (63%)
  blocking collectives  59.6 us (24%)
  Pallas kernels  13 us (5%)
  starting transfers between devices  7.41 us (3%)
  other arithmetic  6.52 us (3%)
  local copies, waits for them, and re-layouts  3.49 us (1%)
    all_to_all x1, waiting for transfers between devices, per_device(): qkv = lax.all_to_all(packed, axes, split_axis=0, concat_axis=0, tiled=True)  155 us
    all_to_all x1, blocking collectives, per_device(): back = lax.all_to_all(out, axes, split_axis=0, concat_axis=0, tiled=True)  59.6 us
    pallas_call x1, Pallas kernels, attend(): pl.pallas_call(attend_kernel, grid=(groups,), in_specs=[pl.BlockSpec((fra...  13 us
    all_to_all x1, starting transfers between devices, per_device(): qkv = lax.all_to_all(packed, axes, split_axis=0, concat_axis=0, tiled=True)  7.41 us
    transpose x1, other arithmetic, per_device(): packed = jnp.stack(parts, axis=1).transpose(2, 0, 1, 3, 4)  6.4 us
  transfers between devices with their start and end apart: 1, of which 1 were waited for; matrix products, arithmetic and copies ran while one was open for 1% of the time, Pallas kernels for 0%

profile of v1, /device:TPU:0, one launch (start us, length us, event | category | flops | bytes accessed | tf_op | source)
XLA Modules:
  0.0 245.3 jit_solution(5224873875496665418)
XLA Ops:
  0.0 0.0 copy-start
  0.0 6.4 %copy_bitcast_fusion = bf16[32,4,3,8,1152]{4,3,2,1,0:T(8,128)(2,1)} fusion(bf16[4,1,32,8,1152]{4,3,2,0,1:T(8,128)(2,1)} %bitcast.13, bf16[4,1,32,8,1152]{4,3,2,0,1:T(8,128)(2,1)} %bitcast.14, bf16[4,1,32,8,1152]{4,3,2,0,1:T(8,128)(2,1)} %bitcast.15), kind=kLoop, calls=%fused_computation.3 | loop fusion | flops 7077888 | bytes 14155776 | tf_op jit(solution)/shard_map/transpose | solution.py:100
  6.4 7.4 %all-to-all-start = ((bf16[32,4,3,8,1152]{4,3,2,1,0:T(8,128)(2,1)}), bf16[32,4,3,8,1152]{4,3,2,1,0:T(8,128)(2,1)}, u32[]{:S(2)}, u32[]{:S(2)}) async-start(bf16[32,4,3,8,1152]{4,3,2,1,0:T(8,128)(2,1)} %copy_bitcast_fusion), calls=%async_computation | async-start | bytes 14155776 | tf_op jit(solution)/shard_map/all_to_all | solution.py:101
  13.9 0.0 copy-done
  13.9 0.0 copy-start.1
  13.9 0.7 gather_fusion
  14.6 0.1 copy.11
  14.7 1.0 gather_fusion.1
  15.6 0.1 copy.12
  15.8 0.1 fusion.bias_ref
  15.9 155.2 %all-to-all-done.qkv_ref = bf16[32,4,3,8,1152]{4,3,2,1,0:T(8,128)(2,1)} async-done(((bf16[32,4,3,8,1152]{4,3,2,1,0:T(8,128)(2,1)}), bf16[32,4,3,8,1152]{4,3,2,1,0:T(8,128)(2,1)}, u32[]{:S(2)}, u32[]{:S(2)}) %all-to-all-start) | async-done | bytes 7077920 | tf_op jit(solution)/shard_map/all_to_all | solution.py:101
  171.1 0.0 copy-done.1
  171.1 13.0 %shard_map.55 = bf16[32,4,8,1152]{3,2,1,0:T(8,128)(2,1)S(1)} custom-call(bf16[32,4,3,8,1152]{4,3,2,1,0:T(8,128)(2,1)} %all-to-all-done.qkv_ref, f32[256,256]{1,0:T(8,128)S(1)} %fusion.bias_ref, bf16[1152,1152]{1,0:T(8,128)(2,1)S(1)} %copy-done.1), custom_call_target="tpu_custom_call" | custom-call | flops 5133828096 | bytes 9437184 | tf_op jit(solution)/shard_map/pallas_call | solution.py:43
  184.1 59.6 %all_to_all.10 = bf16[32,4,8,1152]{3,2,1,0:T(8,128)(2,1)S(1)} all-to-all(bf16[32,4,8,1152]{3,2,1,0:T(8,128)(2,1)S(1)} %shard_map.55), channel_id=1, replica_groups=mesh['pix'=8,'tm'=4] {'tm','pix'}, dimensions={0} | all-to-all | bytes 4718592 | tf_op jit(solution)/shard_map/all_to_all | solution.py:103
  243.7 1.6 copy.13
  (3 shorter events, 0.0 us)
Async XLA Ops:
  0.0 13.9 %copy-start = (s32[8,8]{1,0:T(8,128)S(1)}, s32[8,8]{1,0:T(8,128)}, u32[]{:S(2)}) copy-start(s32[8,8]{1,0:T(8,128)} %param.8) | copy-start | bytes 772
  6.4 164.7 %all-to-all-start = ((bf16[32,4,3,8,1152]{4,3,2,1,0:T(8,128)(2,1)}), bf16[32,4,3,8,1152]{4,3,2,1,0:T(8,128)(2,1)}, u32[]{:S(2)}, u32[]{:S(2)}) async-start(bf16[32,4,3,8,1152]{4,3,2,1,0:T(8,128)(2,1)} %copy_bitcast_fusion), calls=%async_computation | async-start | bytes 14155776 | tf_op jit(solution)/shard_map/all_to_all | solution.py:101
  13.9 157.2 %copy-start.1 = (bf16[1152,1152]{1,0:T(8,128)(2,1)S(1)}, bf16[1152,1152]{1,0:T(8,128)(2,1)}, u32[]{:S(2)}) copy-start(bf16[1152,1152]{1,0:T(8,128)(2,1)} %w_ref.1) | copy-start | bytes 7962628

commit v2 on v1

v2 whole, which is shorter than its diff:
```python
import math

import jax
import jax.numpy as jnp
from jax import lax
from jax.experimental import pallas as pl
from jax.experimental.pallas import tpu as pltpu
from jax.sharding import PartitionSpec as P

HDIM = 72
LANES = 128
SUB = 8
HI = 4
AXES = ("tm", "pix")


def copies(pairs, sems):
    started = [pltpu.make_async_copy(src, dst, sems.at[i]) for i, (src, dst) in enumerate(pairs)]
    for c in started:
        c.start()
    for c in started:
        c.wait()


def mover(body, arrays, out_shapes, number, scalar):
    count = len(arrays)

    def kernel(z_ref, *refs):
        copies(body(z_ref[0], refs[:count], refs[count:-1]), refs[-1])

    return pl.pallas_call(
        kernel,
        grid_spec=pltpu.PrefetchScalarGridSpec(
            num_scalar_prefetch=1,
            in_specs=[pl.BlockSpec(memory_space=pl.ANY)] * count,
            out_specs=[pl.BlockSpec(memory_space=pltpu.VMEM)] * len(out_shapes),
            scratch_shapes=[pltpu.SemaphoreType.DMA((number,))],
        ),
        out_shape=[jax.ShapeDtypeStruct(s, jnp.bfloat16) for s in out_shapes],
        cost_estimate=pl.CostEstimate(flops=0, bytes_accessed=0, transcendentals=0),
    )(scalar.reshape(1), *arrays)


def attend_kernel(z_ref, *refs):
    slots, (bias_ref, w_ref, out_ref, acc_ref) = refs[:HI], refs[HI:]
    rows, feats = acc_ref.shape
    part = rows // HI
    scale = math.log2(math.e) / HDIM**0.5

    def load(which, start, stop):
        pieces = [s[:, 0, which, 0, :, start:stop].reshape(part, stop - start) for s in slots]
        return jnp.concatenate(pieces, axis=0)

    for head in range(feats // HDIM):
        low, high = head * HDIM, (head + 1) * HDIM
        start, stop = low // LANES * LANES, -(-high // LANES) * LANES
        lane = lax.broadcasted_iota(jnp.int32, (1, stop - start), 1) + start
        mine = (lane >= low) & (lane < high)
        q, k, v = (load(which, start, stop) for which in range(3))
        q = jnp.where(mine, q, jnp.zeros_like(q))
        scores = lax.dot_general(q, k, (((1,), (1,)), ((), ())), preferred_element_type=jnp.float32)
        scores = scores * scale + bias_ref[...]
        expo = jnp.exp2(scores - jnp.max(scores, axis=1, keepdims=True))
        share = 1.0 / jnp.sum(expo, axis=1, keepdims=True)
        summed = jnp.dot(expo.astype(jnp.bfloat16), v, preferred_element_type=jnp.float32)
        acc_ref[:, start:stop] = jnp.where(mine, summed * share, acc_ref[:, start:stop])
    attended = acc_ref[...].astype(jnp.bfloat16)
    projected = jnp.dot(attended, w_ref[...], preferred_element_type=jnp.float32).astype(jnp.bfloat16)
    for slot in range(HI):
        out_ref[:, slot, 0] = projected[slot * part : (slot + 1) * part].reshape(out_ref.shape[0], SUB, feats)


def attend(place, slots, bias, w_out):
    sources, _, _, groups, sub, feats = slots[0][0].shape
    rows = HI * sources * sub

    def spec(entry):
        if entry is None:
            return pl.BlockSpec((sources, 1, 3, 1, sub, feats), lambda g, z: (0, z[0], 0, g, 0, 0))
        return pl.BlockSpec((sources, 1, 3, 1, sub, feats), lambda g, z: (0, entry, 0, g, 0, 0))

    return pl.pallas_call(
        attend_kernel,
        grid_spec=pltpu.PrefetchScalarGridSpec(
            num_scalar_prefetch=1,
            grid=(groups,),
            in_specs=[spec(entry) for _, entry in slots]
            + [
                pl.BlockSpec((rows, rows), lambda g, z: (0, 0)),
                pl.BlockSpec((feats, feats), lambda g, z: (0, 0)),
            ],
            out_specs=pl.BlockSpec((sources, HI, 1, sub, feats), lambda g, z: (0, 0, g, 0, 0)),
            scratch_shapes=[pltpu.VMEM((rows, feats), jnp.float32)],
        ),
        out_shape=jax.ShapeDtypeStruct((sources, HI, groups, sub, feats), jnp.bfloat16),
        compiler_params=pltpu.CompilerParams(vmem_limit_bytes=48 * 2**20),
        cost_estimate=pl.CostEstimate(flops=0, bytes_accessed=0, transcendentals=0),
    )(place.reshape(1), *[a for a, _ in slots], bias, w_out)


def bias_of(mask, frame_of_row, patch_of_row, blen):
    block = frame_of_row // blen
    hot = (block[:, None] == jnp.arange(mask.shape[0], dtype=jnp.int32)).astype(jnp.float32)
    allowed = jnp.dot(jnp.dot(hot, mask.astype(jnp.float32)), hot.T) > 0.5
    return jnp.where(allowed & (patch_of_row[:, None] == patch_of_row[None, :]), 0.0, -1e30).astype(jnp.float32)


def plain(query, key_in, value, mask, w_out):
    _, _, patches, feats = query.shape
    frames = lax.axis_size(AXES)
    width, heads = patches // frames, feats // HDIM
    moved = [
        lax.all_to_all(a.reshape(frames, width, feats), AXES, split_axis=0, concat_axis=0, tiled=True)
        .reshape(frames, width, heads, HDIM)
        for a in (query, key_in, value)
    ]
    block = jnp.arange(frames, dtype=jnp.int32) // (frames // mask.shape[0])
    allowed = mask[block][:, block] > 0
    scores = jnp.einsum("iphd,jphd->phij", moved[0], moved[1], preferred_element_type=jnp.float32) / HDIM**0.5
    scores = jnp.where(allowed, scores, -1e30)
    expo = jnp.exp(scores - jnp.max(scores, axis=-1, keepdims=True))
    total = jnp.transpose(jnp.sum(expo, axis=-1), (2, 0, 1))[..., None]
    summed = jnp.einsum("phij,jphd->iphd", expo.astype(jnp.bfloat16), moved[2], preferred_element_type=jnp.float32)
    attended = (summed / total).astype(jnp.bfloat16).reshape(frames, width, feats)
    projected = jnp.dot(attended, w_out, preferred_element_type=jnp.float32).astype(jnp.bfloat16)
    back = lax.all_to_all(projected, AXES, split_axis=0, concat_axis=0, tiled=True)
    return back.reshape(query.shape)

def per_device(query, key_in, value, mask, w_out):
    _, _, patches, feats = query.shape
    n_tm, n_pix = lax.axis_size("tm"), lax.axis_size("pix")
    frames = n_tm * n_pix
    if n_pix % HI != 0 or patches != 4 * frames * SUB:
        return plain(query, key_in, value, mask, w_out)
    n_low = n_pix // HI
    plane = n_tm * n_low
    tall = 2 * SUB
    high = lax.axis_index("pix") // n_low
    teams = [[t * n_pix + z * n_low + x for t in range(n_tm) for x in range(n_low)] for z in range(HI)]
    order = [(p, t) for p in range(n_pix) for t in range(n_tm)]
    number = {device: i for i, device in enumerate(order)}
    tie = lax.optimization_barrier

    row = jnp.arange(HI * plane * SUB, dtype=jnp.int32)
    slot, source = row // (plane * SUB), row // SUB % plane
    frame = source // n_low * n_pix + (high ^ slot) * n_low + source % n_low
    bias = bias_of(mask, frame, row % SUB, frames // mask.shape[0])
    always = mask[0, 0] >= 0

    def region(f, *args):
        shapes = jax.eval_shape(f, *args)
        return lax.cond(always, f, lambda *_: jax.tree.map(lambda s: jnp.zeros(s.shape, s.dtype), shapes), *args)

    def along(a, k):
        pairs = [(number[(p, t)], number[((p // n_low ^ k) * n_low + p % n_low, t)]) for p, t in order]
        return lax.ppermute(a, ("pix", "tm"), pairs)

    def across(a):
        return lax.all_to_all(a, AXES, split_axis=0, concat_axis=0, tiled=True, axis_index_groups=teams)

    flat = [a.reshape(patches // tall, tall, feats) for a in (query, key_in, value)]
    piece = (plane, 3, tall, feats)
    whole = (plane, HI, 3, tall, feats)

    def cut(slots):
        def body(z, ins, outs):
            return [
                (a.at[pl.ds((z ^ k) * plane, plane)], out.at[:, t])
                for k, out in zip(slots, outs)
                for t, a in enumerate(ins)
            ]

        return lambda *flat: mover(body, flat, [piece] * len(slots), 3 * len(slots), high)

    far = cut((3, 2, 1))(*flat)
    far, flat = tie((far, flat))
    moved = [along(far[HI - 1 - k], k) for k in range(1, HI)]

    def pack(z, ins, outs):
        return [
            (a.at[pl.ds((HI + y) * plane, plane)], outs[0].at[:, y, t]) for y in range(HI) for t, a in enumerate(ins)
        ]

    def split(z, ins, outs):
        return [(ins[0].at[:, z ^ k], out) for k, out in enumerate(outs)]

    def start_second(*flat):
        [packed] = mover(pack, flat, [whole], 3 * HI, high)
        packed, flat = tie((packed, flat))
        return mover(split, [across(packed)], [piece] * HI, HI, high), cut((0,))(*flat)

    second, own = region(start_second, *flat)
    second, moved = tie((second, [*own, *moved]))
    second = [second[0]] + [along(second[k], k) for k in range(1, HI)]

    def gather(z, ins, outs):
        return [(a, outs[0].at[:, k]) for k, a in enumerate(ins)]

    def finish_first(moved, bias, w_out):
        [packed] = mover(gather, moved, [whole], HI, high)
        packed = across(packed).reshape(plane, HI, 3, 2, SUB, feats)
        return across(attend(high, [(packed, k) for k in range(HI)], bias, w_out))

    def finish_second(second, bias, w_out):
        second = [a.reshape(plane, 1, 3, 2, SUB, feats) for a in second]
        return across(attend(high, [(a, 0) for a in second], bias, w_out))

    def give_back(done):
        pieces = [done[:, k].reshape(plane * tall, feats) for k in range(HI)]
        return [pieces[0]] + [along(pieces[k], k) for k in range(1, HI)]

    done_first = region(finish_first, moved, bias, w_out)
    second, done_first = tie((second, done_first))
    back_first = give_back(done_first)
    done_second = region(finish_second, second, bias, w_out)
    back_first, done_second = tie((back_first, done_second))
    back_second = give_back(done_second)

    result = jnp.zeros((2 * HI, plane * tall, feats), jnp.bfloat16)
    for half, back in enumerate((back_first, back_second)):
        for k in range(HI):
            result = lax.dynamic_update_index_in_dim(result, back[k], half * HI + (high ^ k), 0)
    return result.reshape(query.shape)


def solution(mesh):
    placed = P("tm", "pix", None, None)
    return jax.shard_map(
        per_device, mesh=mesh, in_specs=(placed, placed, placed, P(), P()), out_specs=placed, check_vma=False
    )
```

time: 246 us -> 225 us (0.915); the launches traced: 245 us -> 222 us
  waiting for transfers between devices: 155 us -> 64.5 us
  starting transfers between devices: 7.41 us -> 39.7 us
  blocking collectives: 59.6 us -> 84 us
  Pallas kernels: 13 us -> 28.7 us
  other arithmetic: 6.52 us -> 0.02 us
    all_to_all x1, waiting for transfers between devices: 155 us -> 40.5 us  [across(): lax.all_to_all(a, AXES, split_axis=0, concat_axis=0, tiled=True, axis_ind...]
    ppermute x0 -> x12, starting transfers between devices: none -> 35.2 us  [along(): return lax.ppermute(a, ('pix', 'tm'), pairs)]
    all_to_all x1 -> x3, blocking collectives: 59.6 us -> 84 us  [across(): lax.all_to_all(a, AXES, split_axis=0, concat_axis=0, tiled=True, axis_ind...]
    ppermute x0 -> x12, waiting for transfers between devices: none -> 24 us  [along(): return lax.ppermute(a, ('pix', 'tm'), pairs)]
    pallas_call x1 -> x7, Pallas kernels: 13 us -> 28.7 us  [the longest x5 15.4 us: mover(): pl.pallas_call(kernel, grid_spec=pltpu.PrefetchScalarGridSpec(num_scalar_...]
    transpose x1 -> x0, other arithmetic: 6.4 us -> none  [per_device(): packed = jnp.stack(parts, axis=1).transpose(2, 0, 1, 3, 4)]
    all_to_all x1, starting transfers between devices: 7.41 us -> 4.5 us  [across(): lax.all_to_all(a, AXES, split_axis=0, concat_axis=0, tiled=True, axis_ind...]
  transfers between devices with their start and end apart: 1 -> 13, of which waited for: 1 -> 4; matrix products, arithmetic and copies ran while one was open for 1% -> 1% of each run, Pallas kernels for 0% -> 11%
where the time goes in v2:
time: 225 us; the launch traced here: 222 us
  blocking collectives  84 us (37%)
  waiting for transfers between devices  64.5 us (29%)
  starting transfers between devices  39.7 us (18%)
  Pallas kernels  28.7 us (13%)
  local copies, waits for them, and re-layouts  2.69 us (1%)
    all_to_all x3, blocking collectives, across(): lax.all_to_all(a, AXES, split_axis=0, concat_axis=0, tiled=True, axis_ind...  84 us
    all_to_all x1, waiting for transfers between devices, across(): lax.all_to_all(a, AXES, split_axis=0, concat_axis=0, tiled=True, axis_ind...  40.5 us
    ppermute x12, starting transfers between devices, along(): return lax.ppermute(a, ('pix', 'tm'), pairs)  35.2 us
    ppermute x12, waiting for transfers between devices, along(): return lax.ppermute(a, ('pix', 'tm'), pairs)  24 us
    pallas_call x5, Pallas kernels, mover(): pl.pallas_call(kernel, grid_spec=pltpu.PrefetchScalarGridSpec(num_scalar_...  15.4 us
    pallas_call x2, Pallas kernels, attend(): pl.pallas_call(attend_kernel, grid_spec=pltpu.PrefetchScalarGridSpec(num_...  13.4 us
    all_to_all x1, starting transfers between devices, across(): lax.all_to_all(a, AXES, split_axis=0, concat_axis=0, tiled=True, axis_ind...  4.5 us
  transfers between devices with their start and end apart: 13, of which 4 were waited for; matrix products, arithmetic and copies ran while one was open for 1% of the time, Pallas kernels for 11%

profile of v2, /device:TPU:0, one launch (start us, length us, event | category | flops | bytes accessed | tf_op | source)
XLA Modules:
  0.0 221.5 jit_solution(9507702797409880797)
XLA Ops:
  0.0 3.4 %shard_map.55 = (bf16[8,3,16,1152]{3,2,1,0:T(8,128)(2,1)}, bf16[8,3,16,1152]{3,2,1,0:T(8,128)(2,1)}, bf16[8,3,16,1152]{3,2,1,0:T(8,128)(2,1)}) custom-call(s32[1]{0:T(128)} %bitcast.9.z_ref, bf16[64,16,1152]{2,1,0:T(8,128)(2,1)} %bitcast.40, bf16[64,16,1152]{2,1,0:T(8,128)(2,1)} %bitcast.42, bf16[64,16,1152]{2,1,0:T(8,128)(2,1)} %bitcast.44), custom_call_target="tpu_custom_call" | custom-call | tf_op jit(solution)/shard_map/pallas_call | solution.py:31
  3.4 3.1 %collective-permute-start = (bf16[8,3,16,1152]{3,2,1,0:T(8,128)(2,1)}, bf16[8,3,16,1152]{3,2,1,0:T(8,128)(2,1)}, u32[]{:S(2)}, u32[]{:S(2)}) collective-permute-start(bf16[8,3,16,1152]{3,2,1,0:T(8,128)(2,1)} %get-tuple-element.116), channel_id=1, source_target_pairs={{0,8},{1,9},{2,10},{3,11},{4,12},{5,13},{6,14},{7,15},{8,0},{9,1},... | collective-permute-start | bytes 2654216 | tf_op jit(solution)/shard_map/ppermute | solution.py:156
  6.5 2.6 %collective-permute-start.1 = (bf16[8,3,16,1152]{3,2,1,0:T(8,128)(2,1)}, bf16[8,3,16,1152]{3,2,1,0:T(8,128)(2,1)}, u32[]{:S(2)}, u32[]{:S(2)}) collective-permute-start(bf16[8,3,16,1152]{3,2,1,0:T(8,128)(2,1)} %get-tuple-element.117), channel_id=1, source_target_pairs={{0,16},{1,17},{2,18},{3,19},{4,20},{5,21},{6,22},{7,23},{8,24},{9,... | collective-permute-start | bytes 2654216 | tf_op jit(solution)/shard_map/ppermute | solution.py:156
  9.1 0.0 collective-permute-start.2
  9.1 0.5 slice.27
  10.3 53.5 %conditional.3 = (bf16[8,3,16,1152]{3,2,1,0:T(8,128)(2,1)}, bf16[8,3,16,1152]{3,2,1,0:T(8,128)(2,1)}, bf16[8,3,16,1152]{3,2,1,0:T(8,128)(2,1)}, bf16[8,3,16,1152...) conditional(s32[]{:T(128)} %bitcast.8, () %tuple.30, (s32[]{:T(128)}, bf16[64,16,1152]{2,1,0:T(8,128)(2,1)S(1)}, ...), branch_computations={%region_0.1_spmd, %region_1.2_spmd} | conditional | bytes 10616904 | solution.py:152
  10.3 3.5 %branch_1_fun.6 = bf16[8,4,3,16,1152]{4,3,2,1,0:T(8,128)(2,1)} custom-call(s32[1]{0:T(128)} %bitcast.z_ref, bf16[64,16,1152]{2,1,0:T(8,128)(2,1)S(1)} %get-tuple-element.56.refs_0_, bf16[64,16,1152]{2,1,0:T(8,128)(2,1)} %get-tuple-element.57.refs_1_, bf16[64,16,1152]{2,1,0:T(8,128)(2,1)} %get-tuple-element.58.refs_2_), custom_call_target="tpu_custom_call" | custom-call | tf_op jit(solution)/shard_map/cond/branch_1_fun/pallas_call | solution.py:31
  13.8 4.5 %all-to-all-start = ((bf16[8,4,3,16,1152]{4,3,2,1,0:T(8,128)(2,1)}), bf16[8,4,3,16,1152]{4,3,2,1,0:T(8,128)(2,1)}, u32[]{:S(2)}, u32[]{:S(2)}) async-start(bf16[8,4,3,16,1152]{4,3,2,1,0:T(8,128)(2,1)} %branch_1_fun.6), calls=%async_computation | async-start | bytes 7077888 | tf_op jit(solution)/shard_map/cond/branch_1_fun/all_to_all | solution.py:159
  18.3 1.1 branch_1_fun.8
  19.5 40.5 %all-to-all-done.refs_0_ = bf16[8,4,3,16,1152]{4,3,2,1,0:T(8,128)(2,1)} async-done(((bf16[8,4,3,16,1152]{4,3,2,1,0:T(8,128)(2,1)}), bf16[8,4,3,16,1152]{4,3,2,1,0:T(8,128)(2,1)}, u32[]{:S(2)}, u32[]{:S(2)}) %all-to-all-start) | async-done | bytes 3538976 | tf_op jit(solution)/shard_map/cond/branch_1_fun/all_to_all | solution.py:159
  60.0 3.8 %branch_1_fun.7 = (bf16[8,3,16,1152]{3,2,1,0:T(8,128)(2,1)}, bf16[8,3,16,1152]{3,2,1,0:T(8,128)(2,1)}, bf16[8,3,16,1152]{3,2,1,0:T(8,128)(2,1)}, bf16[8,3,16,1152]{3,2,1,0:T(8,128)(2,1)}) custom-call(s32[1]{0:T(128)} %bitcast.z_ref, bf16[8,4,3,16,1152]{4,3,2,1,0:T(8,128)(2,1)} %all-to-all-done.refs_0_), custom_call_target="tpu_custom_call" | custom-call | tf_op jit(solution)/shard_map/cond/branch_1_fun/pallas_call | solution.py:31
  63.7 0.0 collective-permute-done
  63.8 4.4 %collective-permute-done.1 = bf16[8,3,16,1152]{3,2,1,0:T(8,128)(2,1)} collective-permute-done((bf16[8,3,16,1152]{3,2,1,0:T(8,128)(2,1)}, bf16[8,3,16,1152]{3,2,1,0:T(8,128)(2,1)}, u32[]{:S(2)}, u32[]{:S(2)}) %collective-permute-start.1) | collective-permute-done | bytes 884768 | tf_op jit(solution)/shard_map/ppermute | solution.py:156
  68.2 0.0 collective-permute-done.2
  68.2 18.1 %collective-permute-start.3 = (bf16[8,3,16,1152]{3,2,1,0:T(8,128)(2,1)}, bf16[8,3,16,1152]{3,2,1,0:T(8,128)(2,1)}, u32[]{:S(2)}, u32[]{:S(2)}) collective-permute-start(bf16[8,3,16,1152]{3,2,1,0:T(8,128)(2,1)} %get-tuple-element.120), channel_id=1, source_target_pairs={{0,8},{1,9},{2,10},{3,11},{4,12},{5,13},{6,14},{7,15},{8,0},{9,1},... | collective-permute-start | bytes 2654216 | tf_op jit(solution)/shard_map/ppermute | solution.py:156
  86.3 1.0 collective-permute-start.4
  87.3 1.5 collective-permute-start.5
  88.8 1.1 fusion.5
  89.9 73.6 %conditional.4 = (bf16[8,4,2,8,1152]{4,3,2,1,0:T(8,128)(2,1)S(1)}) conditional(s32[]{:T(128)} %bitcast.8, () %tuple.34, (s32[]{:T(128)}, bf16[8,3,16,1152]{3,2,1,0:T(8,128)(2,1)S(1)}, bf16[8,3,16,1152]{3,2,1,0:T(8,128)(2,1)}, bf16[8,3,16,1152]{3,2,1,0:T(8,128)(2,1)}, bf16[8,3,16,1152]{3,2,1,0:T(8,128)(2,1)}, /*index=5*/f32[256,256]{1,0:T(8,128)}, ...), branch_computations={%region_2.3_spmd, %region_3.4_spmd} | conditional | bytes 21102656 | solution.py:152
  89.9 3.6 %branch_1_fun.9 = bf16[8,4,3,16,1152]{4,3,2,1,0:T(8,128)(2,1)} custom-call(s32[1]{0:T(128)} %bitcast.1.z_ref, bf16[8,3,16,1152]{3,2,1,0:T(8,128)(2,1)S(1)} %get-tuple-element.60.refs_0_, bf16[8,3,16,1152]{3,2,1,0:T(8,128)(2,1)} %get-tuple-element.61.refs_1_, bf16[8,3,16,1152]{3,2,1,0:T(8,128)(2,1)} %get-tuple-element.62.refs_2_, ...), custom_call_target="tpu_custom_call" | custom-call | tf_op jit(solution)/shard_map/cond/branch_1_fun/pallas_call | solution.py:31
  93.4 0.0 copy-start.1
  93.4 45.7 %all_to_all.16 = bf16[8,4,3,16,1152]{4,3,2,1,0:T(8,128)(2,1)S(1)} all-to-all(bf16[8,4,3,16,1152]{4,3,2,1,0:T(8,128)(2,1)} %branch_1_fun.9), channel_id=1, replica_groups={{0,4,1,5,2,6,3,7},{8,12,9,13,10,14,11,15},{16,20,17,21,18,22,19,23},{24..., dimensions={0} | all-to-all | bytes 7077888 | tf_op jit(solution)/shard_map/cond/branch_1_fun/all_to_all | solution.py:159
  139.1 0.0 copy-done.1
  139.1 5.5 %branch_1_fun.10 = bf16[8,4,2,8,1152]{4,3,2,1,0:T(8,128)(2,1)S(1)} custom-call(s32[1]{0:T(128)} %bitcast.1.z_ref, bf16[8,4,3,2,8,1152]{5,4,3,2,1,0:T(8,128)(2,1)S(1)} %bitcast.36, bf16[8,4,3,2,8,1152]{5,4,3,2,1,0:T(8,128)(2,1)S(1)} %bitcast.37, bf16[8,4,3,2,8,1152]{5,4,3,2,1,0:T(8,128)(2,1)S(1)} %bitcast.38, bf16[8,4,3,2,8,1152]{5,4,3,2,1,0:T(8,128)(2,1)S(1)} %bitcast.39, ...), custom_call_target="tpu_custom_call" | custom-call | tf_op jit(solution)/shard_map/cond/branch_1_fun/pallas_call | solution.py:82
  144.7 18.8 %all_to_all.17 = bf16[8,4,2,8,1152]{4,3,2,1,0:T(8,128)(2,1)S(1)} all-to-all(bf16[8,4,2,8,1152]{4,3,2,1,0:T(8,128)(2,1)S(1)} %branch_1_fun.10), channel_id=1, replica_groups={{0,4,1,5,2,6,3,7},{8,12,9,13,10,14,11,15},{16,20,17,21,18,22,19,23},{24..., dimensions={0} | all-to-all | bytes 2359296 | tf_op jit(solution)/shard_map/cond/branch_1_fun/all_to_all | solution.py:159
  163.5 0.0 collective-permute-done.3
  163.5 0.0 collective-permute-done.4
  163.5 0.0 collective-permute-done.5
  163.5 0.1 fusion.21
  163.6 1.5 collective-permute-start.6
  165.1 1.5 collective-permute-start.7
  166.6 1.5 collective-permute-start.8
  168.1 27.3 %conditional.5 = (bf16[8,4,2,8,1152]{4,3,2,1,0:T(8,128)(2,1)S(1)}) conditional(s32[]{:T(128)} %bitcast.8, () %tuple.37, (s32[]{:T(128)}, bf16[8,3,16,1152]{3,2,1,0:T(8,128)(2,1)}, bf16[8,3,16,1152]{3,2,1,0:T(8,128)(2,1)}, bf16[8,3,16,1152]{3,2,1,0:T(8,128)(2,1)}, bf16[8,3,16,1152]{3,2,1,0:T(8,128)(2,1)}, /*index=5*/f32[256,256]{1,0:T(8,128)S(1)}, ...), branch_computations={%region_4.5_spmd, %region_5.6_spmd} | conditional | bytes 2359304 | solution.py:152
  168.1 7.8 %branch_1_fun.11 = bf16[8,4,2,8,1152]{4,3,2,1,0:T(8,128)(2,1)S(1)} custom-call(s32[1]{0:T(128)} %bitcast.3.z_ref, bf16[8,1,3,2,8,1152]{5,4,3,2,1,0:T(8,128)(2,1)} %bitcast.4.refs_0_, bf16[8,1,3,2,8,1152]{5,4,3,2,1,0:T(8,128)(2,1)} %bitcast.5.refs_1_, bf16[8,1,3,2,8,1152]{5,4,3,2,1,0:T(8,128)(2,1)} %bitcast.6.refs_2_, ...), custom_call_target="tpu_custom_call" | custom-call | tf_op jit(solution)/shard_map/cond/branch_1_fun/pallas_call | solution.py:82
  175.9 19.5 %all_to_all.18 = bf16[8,4,2,8,1152]{4,3,2,1,0:T(8,128)(2,1)S(1)} all-to-all(bf16[8,4,2,8,1152]{4,3,2,1,0:T(8,128)(2,1)S(1)} %branch_1_fun.11), channel_id=1, replica_groups={{0,4,1,5,2,6,3,7},{8,12,9,13,10,14,11,15},{16,20,17,21,18,22,19,23},{24..., dimensions={0} | all-to-all | bytes 2359296 | tf_op jit(solution)/shard_map/cond/branch_1_fun/all_to_all | solution.py:159
  195.4 0.0 collective-permute-done.6
  195.4 0.0 collective-permute-done.7
  195.4 0.0 collective-permute-done.8
  195.4 0.1 fusion.20
  195.5 1.1 collective-permute-start.9
  196.6 2.0 collective-permute-start.10
  198.6 1.4 collective-permute-start.11
  199.9 0.3 broadcast_in_dim.40
  200.4 9.8 %collective-permute-done.9 = bf16[128,1152]{1,0:T(8,128)(2,1)S(1)} collective-permute-done((bf16[128,1152]{1,0:T(8,128)(2,1)S(1)}, bf16[128,1152]{1,0:T(8,128)(2,1)S(1)}, u32[]{:S(2)}, u32[]{:S(2)}) %collective-permute-start.9) | collective-permute-done | bytes 294944 | tf_op jit(solution)/shard_map/ppermute | solution.py:156
  210.3 9.7 %collective-permute-done.10 = bf16[128,1152]{1,0:T(8,128)(2,1)S(1)} collective-permute-done((bf16[128,1152]{1,0:T(8,128)(2,1)S(1)}, bf16[128,1152]{1,0:T(8,128)(2,1)S(1)}, u32[]{:S(2)}, u32[]{:S(2)}) %collective-permute-start.10) | collective-permute-done | bytes 294944 | tf_op jit(solution)/shard_map/ppermute | solution.py:156
  220.0 0.0 collective-permute-done.11
  220.1 0.0 copy-start.2
  220.1 1.4 copy-done.2
  (17 shorter events, 0.3 us)
Async XLA Ops:
  0.0 9.1 %copy-start.5 = (s32[8,8]{1,0:T(8,128)S(1)}, s32[8,8]{1,0:T(8,128)}, u32[]{:S(2)}) copy-start(s32[8,8]{1,0:T(8,128)} %param.14) | copy-start | bytes 772
  0.0 10.2 %copy-start = (bf16[1,1,1024,1152]{3,2,1,0:T(8,128)(2,1)S(1)}, bf16[1,1,1024,1152]{3,2,1,0:T(8,128)(2,1)}, u32[]{:S(2)}) copy-start(bf16[1,1,1024,1152]{3,2,1,0:T(8,128)(2,1)} %param.11) | copy-start | bytes 7077892
  3.4 60.4 %collective-permute-start = (bf16[8,3,16,1152]{3,2,1,0:T(8,128)(2,1)}, bf16[8,3,16,1152]{3,2,1,0:T(8,128)(2,1)}, u32[]{:S(2)}, u32[]{:S(2)}) collective-permute-start(bf16[8,3,16,1152]{3,2,1,0:T(8,128)(2,1)} %get-tuple-element.116), channel_id=1, source_target_pairs={{0,8},{1,9},{2,10},{3,11},{4,12},{5,13},{6,14},{7,15},{8,0},{9,1},... | collective-permute-start | bytes 2654216 | tf_op jit(solution)/shard_map/ppermute | solution.py:156
  6.5 61.7 %collective-permute-start.1 = (bf16[8,3,16,1152]{3,2,1,0:T(8,128)(2,1)}, bf16[8,3,16,1152]{3,2,1,0:T(8,128)(2,1)}, u32[]{:S(2)}, u32[]{:S(2)}) collective-permute-start(bf16[8,3,16,1152]{3,2,1,0:T(8,128)(2,1)} %get-tuple-element.117), channel_id=1, source_target_pairs={{0,16},{1,17},{2,18},{3,19},{4,20},{5,21},{6,22},{7,23},{8,24},{9,... | collective-permute-start | bytes 2654216 | tf_op jit(solution)/shard_map/ppermute | solution.py:156
  9.1 59.1 %collective-permute-start.2 = (bf16[8,3,16,1152]{3,2,1,0:T(8,128)(2,1)}, bf16[8,3,16,1152]{3,2,1,0:T(8,128)(2,1)}, u32[]{:S(2)}, u32[]{:S(2)}) collective-permute-start(bf16[8,3,16,1152]{3,2,1,0:T(8,128)(2,1)} %get-tuple-element.118), channel_id=1, source_target_pairs={{0,24},{1,25},{2,26},{3,27},{4,28},{5,29},{6,30},{7,31},{8,16},{9,... | collective-permute-start | bytes 2654216 | tf_op jit(solution)/shard_map/ppermute | solution.py:156
  13.8 46.1 %all-to-all-start = ((bf16[8,4,3,16,1152]{4,3,2,1,0:T(8,128)(2,1)}), bf16[8,4,3,16,1152]{4,3,2,1,0:T(8,128)(2,1)}, u32[]{:S(2)}, u32[]{:S(2)}) async-start(bf16[8,4,3,16,1152]{4,3,2,1,0:T(8,128)(2,1)} %branch_1_fun.6), calls=%async_computation | async-start | bytes 7077888 | tf_op jit(solution)/shard_map/cond/branch_1_fun/all_to_all | solution.py:159
  68.2 95.3 %collective-permute-start.3 = (bf16[8,3,16,1152]{3,2,1,0:T(8,128)(2,1)}, bf16[8,3,16,1152]{3,2,1,0:T(8,128)(2,1)}, u32[]{:S(2)}, u32[]{:S(2)}) collective-permute-start(bf16[8,3,16,1152]{3,2,1,0:T(8,128)(2,1)} %get-tuple-element.120), channel_id=1, source_target_pairs={{0,8},{1,9},{2,10},{3,11},{4,12},{5,13},{6,14},{7,15},{8,0},{9,1},... | collective-permute-start | bytes 2654216 | tf_op jit(solution)/shard_map/ppermute | solution.py:156
  86.3 77.2 %collective-permute-start.4 = (bf16[8,3,16,1152]{3,2,1,0:T(8,128)(2,1)}, bf16[8,3,16,1152]{3,2,1,0:T(8,128)(2,1)}, u32[]{:S(2)}, u32[]{:S(2)}) collective-permute-start(bf16[8,3,16,1152]{3,2,1,0:T(8,128)(2,1)} %get-tuple-element.121), channel_id=1, source_target_pairs={{0,16},{1,17},{2,18},{3,19},{4,20},{5,21},{6,22},{7,23},{8,24},{9,... | collective-permute-start | bytes 2654216 | tf_op jit(solution)/shard_map/ppermute | solution.py:156
  87.3 76.2 %collective-permute-start.5 = (bf16[8,3,16,1152]{3,2,1,0:T(8,128)(2,1)}, bf16[8,3,16,1152]{3,2,1,0:T(8,128)(2,1)}, u32[]{:S(2)}, u32[]{:S(2)}) collective-permute-start(bf16[8,3,16,1152]{3,2,1,0:T(8,128)(2,1)} %get-tuple-element.122), channel_id=1, source_target_pairs={{0,24},{1,25},{2,26},{3,27},{4,28},{5,29},{6,30},{7,31},{8,16},{9,... | collective-permute-start | bytes 2654216 | tf_op jit(solution)/shard_map/ppermute | solution.py:156
  93.4 45.7 %copy-start.1 = (bf16[1152,1152]{1,0:T(8,128)(2,1)S(1)}, bf16[1152,1152]{1,0:T(8,128)(2,1)}, u32[]{:S(2)}) copy-start(bf16[1152,1152]{1,0:T(8,128)(2,1)} %get-tuple-element.65.refs_5_) | copy-start | bytes 7962628 | tf_op jit(solution)/shard_map/cond
  93.4 45.7 %copy-start.4 = (f32[256,256]{1,0:T(8,128)S(1)}, f32[256,256]{1,0:T(8,128)}, u32[]{:S(2)}) copy-start(f32[256,256]{1,0:T(8,128)} %get-tuple-element.64.refs_4_) | copy-start | bytes 786436 | tf_op jit(solution)/shard_map/cond
  163.5 4.6 %copy-start.3 = (f32[256,256]{1,0:T(8,128)S(1)}, f32[256,256]{1,0:T(8,128)}, u32[]{:S(2)}) copy-start(f32[256,256]{1,0:T(8,128)} %fusion.5) | copy-start | bytes 786436
  163.6 31.8 %collective-permute-start.6 = (bf16[128,1152]{1,0:T(8,128)(2,1)S(1)}, bf16[128,1152]{1,0:T(8,128)(2,1)S(1)}, u32[]{:S(2)}, u32[]{:S(2)}) collective-permute-start(bf16[128,1152]{1,0:T(8,128)(2,1)S(1)} %bitcast.50), channel_id=1, source_target_pairs={{0,8},{1,9},{2,10},{3,11},{4,12},{5,13},{6,14},{7,15},{8,0},{9,1},... | collective-permute-start | bytes 884744 | tf_op jit(solution)/shard_map/ppermute | solution.py:156
  165.1 30.3 %collective-permute-start.7 = (bf16[128,1152]{1,0:T(8,128)(2,1)S(1)}, bf16[128,1152]{1,0:T(8,128)(2,1)S(1)}, u32[]{:S(2)}, u32[]{:S(2)}) collective-permute-start(bf16[128,1152]{1,0:T(8,128)(2,1)S(1)} %bitcast.49), channel_id=1, source_target_pairs={{0,16},{1,17},{2,18},{3,19},{4,20},{5,21},{6,22},{7,23},{8,24},{9,... | collective-permute-start | bytes 884744 | tf_op jit(solution)/shard_map/ppermute | solution.py:156
  166.6 28.8 %collective-permute-start.8 = (bf16[128,1152]{1,0:T(8,128)(2,1)S(1)}, bf16[128,1152]{1,0:T(8,128)(2,1)S(1)}, u32[]{:S(2)}, u32[]{:S(2)}) collective-permute-start(bf16[128,1152]{1,0:T(8,128)(2,1)S(1)} %bitcast.48), channel_id=1, source_target_pairs={{0,24},{1,25},{2,26},{3,27},{4,28},{5,29},{6,30},{7,31},{8,16},{9,... | collective-permute-start | bytes 884744 | tf_op jit(solution)/shard_map/ppermute | solution.py:156
  195.5 14.8 %collective-permute-start.9 = (bf16[128,1152]{1,0:T(8,128)(2,1)S(1)}, bf16[128,1152]{1,0:T(8,128)(2,1)S(1)}, u32[]{:S(2)}, u32[]{:S(2)}) collective-permute-start(bf16[128,1152]{1,0:T(8,128)(2,1)S(1)} %bitcast.53), channel_id=1, source_target_pairs={{0,8},{1,9},{2,10},{3,11},{4,12},{5,13},{6,14},{7,15},{8,0},{9,1},... | collective-permute-start | bytes 884744 | tf_op jit(solution)/shard_map/ppermute | solution.py:156
  196.6 23.4 %collective-permute-start.10 = (bf16[128,1152]{1,0:T(8,128)(2,1)S(1)}, bf16[128,1152]{1,0:T(8,128)(2,1)S(1)}, u32[]{:S(2)}, u32[]{:S(2)}) collective-permute-start(bf16[128,1152]{1,0:T(8,128)(2,1)S(1)} %bitcast.52), channel_id=1, source_target_pairs={{0,16},{1,17},{2,18},{3,19},{4,20},{5,21},{6,22},{7,23},{8,24},{9,... | collective-permute-start | bytes 884744 | tf_op jit(solution)/shard_map/ppermute | solution.py:156
  198.6 21.5 %collective-permute-start.11 = (bf16[128,1152]{1,0:T(8,128)(2,1)S(1)}, bf16[128,1152]{1,0:T(8,128)(2,1)S(1)}, u32[]{:S(2)}, u32[]{:S(2)}) collective-permute-start(bf16[128,1152]{1,0:T(8,128)(2,1)S(1)} %bitcast.51), channel_id=1, source_target_pairs={{0,24},{1,25},{2,26},{3,27},{4,28},{5,29},{6,30},{7,31},{8,16},{9,... | collective-permute-start | bytes 884744 | tf_op jit(solution)/shard_map/ppermute | solution.py:156
  220.1 1.4 copy-start.2

commit v3 on v2

--- a/solution.py
+++ b/solution.py
@@ -11,30 +11,40 @@
 LANES = 128
 SUB = 8
 HI = 4
+NEAR = (0, 2, 3, 1)
 AXES = ("tm", "pix")
 
 
-def copies(pairs, sems):
-    started = [pltpu.make_async_copy(src, dst, sems.at[i]) for i, (src, dst) in enumerate(pairs)]
-    for c in started:
-        c.start()
-    for c in started:
-        c.wait()
-
-
 def mover(body, arrays, out_shapes, number, scalar):
-    count = len(arrays)
+    count, outs = len(arrays), len(out_shapes)
 
     def kernel(z_ref, *refs):
-        copies(body(z_ref[0], refs[:count], refs[count:-1]), refs[-1])
+        sems, out_sems = refs[-2:]
+        stages = refs[count + outs : count + 2 * outs]
+        arriving, slot = [], 0
+        for pairs in body(z_ref[0], refs[:count], stages):
+            arriving.append([pltpu.make_async_copy(a, b, sems.at[slot + i]) for i, (a, b) in enumerate(pairs)])
+            slot += len(pairs)
+        leaving = [
+            pltpu.make_async_copy(stages[i], refs[count + i], out_sems.at[i]) for i in range(outs)
+        ]
+        for copy in sum(arriving, []):
+            copy.start()
+        for copies, out in zip(arriving, leaving):
+            for copy in copies:
+                copy.wait()
+            out.start()
+        for out in leaving:
+            out.wait()
 
     return pl.pallas_call(
         kernel,
         grid_spec=pltpu.PrefetchScalarGridSpec(
             num_scalar_prefetch=1,
             in_specs=[pl.BlockSpec(memory_space=pl.ANY)] * count,
-            out_specs=[pl.BlockSpec(memory_space=pltpu.VMEM)] * len(out_shapes),
-            scratch_shapes=[pltpu.SemaphoreType.DMA((number,))],
+            out_specs=[pl.BlockSpec(memory_space=pl.ANY)] * outs,
+            scratch_shapes=[pltpu.VMEM(s, jnp.bfloat16) for s in out_shapes]
+            + [pltpu.SemaphoreType.DMA((number,)), pltpu.SemaphoreType.DMA((outs,))],
         ),
         out_shape=[jax.ShapeDtypeStruct(s, jnp.bfloat16) for s in out_shapes],
         cost_estimate=pl.CostEstimate(flops=0, bytes_accessed=0, transcendentals=0),
@@ -42,30 +52,55 @@
 
 
 def attend_kernel(z_ref, *refs):
-    slots, (bias_ref, w_ref, out_ref, acc_ref) = refs[:HI], refs[HI:]
+    slots, (bias_ref, w_hbm, out_ref, acc_ref, w_ref, w_sem) = refs[:HI], refs[HI:]
     rows, feats = acc_ref.shape
     part = rows // HI
     scale = math.log2(math.e) / HDIM**0.5
+    fetch = pltpu.make_async_copy(w_hbm, w_ref, w_sem)
+
+    @pl.when(pl.program_id(0) == 0)
+    def _():
+        fetch.start()
 
     def load(which, start, stop):
         pieces = [s[:, 0, which, 0, :, start:stop].reshape(part, stop - start) for s in slots]
         return jnp.concatenate(pieces, axis=0)
 
-    for head in range(feats // HDIM):
+    heads = feats // HDIM
+
+    def window(head):
         low, high = head * HDIM, (head + 1) * HDIM
         start, stop = low // LANES * LANES, -(-high // LANES) * LANES
         lane = lax.broadcasted_iota(jnp.int32, (1, stop - start), 1) + start
-        mine = (lane >= low) & (lane < high)
-        q, k, v = (load(which, start, stop) for which in range(3))
+        return start, stop, (lane >= low) & (lane < high)
+
+    def score(head):
+        start, stop, mine = window(head)
+        q, k = load(0, start, stop), load(1, start, stop)
         q = jnp.where(mine, q, jnp.zeros_like(q))
-        scores = lax.dot_general(q, k, (((1,), (1,)), ((), ())), preferred_element_type=jnp.float32)
+        return lax.dot_general(q, k, (((1,), (1,)), ((), ())), preferred_element_type=jnp.float32)
+
+    def weigh(scores):
         scores = scores * scale + bias_ref[...]
         expo = jnp.exp2(scores - jnp.max(scores, axis=1, keepdims=True))
-        share = 1.0 / jnp.sum(expo, axis=1, keepdims=True)
-        summed = jnp.dot(expo.astype(jnp.bfloat16), v, preferred_element_type=jnp.float32)
-        acc_ref[:, start:stop] = jnp.where(mine, summed * share, acc_ref[:, start:stop])
-    attended = acc_ref[...].astype(jnp.bfloat16)
-    projected = jnp.dot(attended, w_ref[...], preferred_element_type=jnp.float32).astype(jnp.bfloat16)
+        return expo.astype(jnp.bfloat16), 1.0 / jnp.sum(expo, axis=1, keepdims=True)
+
+    def blend(head, expo, share):
+        start, stop, mine = window(head)
+        summed = jnp.dot(expo, load(2, start, stop), preferred_element_type=jnp.float32)
+        acc_ref[:, start:stop] = jnp.where(mine, (summed * share).astype(jnp.bfloat16), acc_ref[:, start:stop])
+
+    scores = score(0)
+    for head in range(heads):
+        later = score(head + 1) if head + 1 < heads else None
+        expo, share = weigh(scores)
+        blend(head, expo, share)
+        scores = later
+    @pl.when(pl.program_id(0) == 0)
+    def _():
+        fetch.wait()
+
+    projected = jnp.dot(acc_ref[...], w_ref[...], preferred_element_type=jnp.float32).astype(jnp.bfloat16)
     for slot in range(HI):
         out_ref[:, slot, 0] = projected[slot * part : (slot + 1) * part].reshape(out_ref.shape[0], SUB, feats)
 
@@ -75,8 +110,6 @@
     rows = HI * sources * sub
 
     def spec(entry):
-        if entry is None:
-            return pl.BlockSpec((sources, 1, 3, 1, sub, feats), lambda g, z: (0, z[0], 0, g, 0, 0))
         return pl.BlockSpec((sources, 1, 3, 1, sub, feats), lambda g, z: (0, entry, 0, g, 0, 0))
 
     return pl.pallas_call(
@@ -85,12 +118,13 @@
             num_scalar_prefetch=1,
             grid=(groups,),
             in_specs=[spec(entry) for _, entry in slots]
-            + [
-                pl.BlockSpec((rows, rows), lambda g, z: (0, 0)),
-                pl.BlockSpec((feats, feats), lambda g, z: (0, 0)),
+            + [pl.BlockSpec((rows, rows), lambda g, z: (0, 0)), pl.BlockSpec(memory_space=pl.ANY)],
+            out_specs=pl.BlockSpec((sources, HI, 1, sub, feats), lambda g, z: (0, 0, g, 0, 0)),
+            scratch_shapes=[
+                pltpu.VMEM((rows, feats), jnp.bfloat16),
+                pltpu.VMEM((feats, feats), jnp.bfloat16),
+                pltpu.SemaphoreType.DMA,
             ],
-            out_specs=pl.BlockSpec((sources, HI, 1, sub, feats), lambda g, z: (0, 0, g, 0, 0)),
-            scratch_shapes=[pltpu.VMEM((rows, feats), jnp.float32)],
         ),
         out_shape=jax.ShapeDtypeStruct((sources, HI, groups, sub, feats), jnp.bfloat16),
         compiler_params=pltpu.CompilerParams(vmem_limit_bytes=48 * 2**20),
@@ -143,7 +177,7 @@
 
     row = jnp.arange(HI * plane * SUB, dtype=jnp.int32)
     slot, source = row // (plane * SUB), row // SUB % plane
-    frame = source // n_low * n_pix + (high ^ slot) * n_low + source % n_low
+    frame = source // n_low * n_pix + (high ^ sum(jnp.where(slot == s, k, 0) for s, k in enumerate(NEAR))) * n_low + source % n_low
     bias = bias_of(mask, frame, row % SUB, frames // mask.shape[0])
     always = mask[0, 0] >= 0
 
@@ -165,24 +199,23 @@
     def cut(slots):
         def body(z, ins, outs):
             return [
-                (a.at[pl.ds((z ^ k) * plane, plane)], out.at[:, t])
+                [(a.at[pl.ds((z ^ k) * plane, plane)], out.at[:, t]) for t, a in enumerate(ins)]
                 for k, out in zip(slots, outs)
-                for t, a in enumerate(ins)
             ]
 
         return lambda *flat: mover(body, flat, [piece] * len(slots), 3 * len(slots), high)
 
-    far = cut((3, 2, 1))(*flat)
+    far = cut(NEAR[1:])(*flat)
     far, flat = tie((far, flat))
-    moved = [along(far[HI - 1 - k], k) for k in range(1, HI)]
+    moved = [along(a, k) for a, k in zip(far, NEAR[1:])]
 
     def pack(z, ins, outs):
         return [
-            (a.at[pl.ds((HI + y) * plane, plane)], outs[0].at[:, y, t]) for y in range(HI) for t, a in enumerate(ins)
+            [(a.at[pl.ds((HI + y) * plane, plane)], outs[0].at[:, y, t]) for y in range(HI) for t, a in enumerate(ins)]
         ]
 
     def split(z, ins, outs):
-        return [(ins[0].at[:, z ^ k], out) for k, out in enumerate(outs)]
+        return [[(ins[0].at[:, z ^ k], out)] for k, out in zip(NEAR, outs)]
 
     def start_second(*flat):
         [packed] = mover(pack, flat, [whole], 3 * HI, high)
@@ -191,10 +224,10 @@
 
     second, own = region(start_second, *flat)
     second, moved = tie((second, [*own, *moved]))
-    second = [second[0]] + [along(second[k], k) for k in range(1, HI)]
+    second = [second[0], *[along(a, k) for a, k in zip(second[1:], NEAR[1:])]]
 
     def gather(z, ins, outs):
-        return [(a, outs[0].at[:, k]) for k, a in enumerate(ins)]
+        return [[(a, outs[0].at[:, k]) for k, a in enumerate(ins)]]
 
     def finish_first(moved, bias, w_out):
         [packed] = mover(gather, moved, [whole], HI, high)
@@ -207,10 +240,10 @@
 
     def give_back(done):
         pieces = [done[:, k].reshape(plane * tall, feats) for k in range(HI)]
-        return [pieces[0]] + [along(pieces[k], k) for k in range(1, HI)]
+        return [pieces[0], *[along(a, k) for a, k in zip(pieces[1:], NEAR[1:])]]
 
     done_first = region(finish_first, moved, bias, w_out)
-    second, done_first = tie((second, done_first))
+    second[0], done_first = tie((second[0], done_first))
     back_first = give_back(done_first)
     done_second = region(finish_second, second, bias, w_out)
     back_first, done_second = tie((back_first, done_second))
@@ -218,8 +251,8 @@
 
     result = jnp.zeros((2 * HI, plane * tall, feats), jnp.bfloat16)
     for half, back in enumerate((back_first, back_second)):
-        for k in range(HI):
-            result = lax.dynamic_update_index_in_dim(result, back[k], half * HI + (high ^ k), 0)
+        for k, piece in zip(NEAR, back):
+            result = lax.dynamic_update_index_in_dim(result, piece, half * HI + (high ^ k), 0)
     return result.reshape(query.shape)
 
 

time: 225 us -> 222 us (0.987)
  transfers between devices with their start and end apart: 13 -> 13, of which waited for: 4 -> 5; matrix products, arithmetic and copies ran while one was open for 1% -> 1% of each run, Pallas kernels for 11% -> 11%
where the time goes in v3:
time: 222 us; the launch traced here: 219 us
  blocking collectives  83.3 us (38%)
  waiting for transfers between devices  64.2 us (29%)
  starting transfers between devices  40.1 us (18%)
  Pallas kernels  27.2 us (12%)
  local copies, waits for them, and re-layouts  2.68 us (1%)
    all_to_all x3, blocking collectives, across(): lax.all_to_all(a, AXES, split_axis=0, concat_axis=0, tiled=True, axis_ind...  83.3 us
    all_to_all x1, waiting for transfers between devices, across(): lax.all_to_all(a, AXES, split_axis=0, concat_axis=0, tiled=True, axis_ind...  40.3 us
    ppermute x12, starting transfers between devices, along(): return lax.ppermute(a, ('pix', 'tm'), pairs)  35.6 us
    ppermute x12, waiting for transfers between devices, along(): return lax.ppermute(a, ('pix', 'tm'), pairs)  23.8 us
    pallas_call x5, Pallas kernels, mover(): pl.pallas_call(kernel, grid_spec=pltpu.PrefetchScalarGridSpec(num_scalar_...  14.3 us
    pallas_call x2, Pallas kernels, attend(): pl.pallas_call(attend_kernel, grid_spec=pltpu.PrefetchScalarGridSpec(num_...  12.9 us
    all_to_all x1, starting transfers between devices, across(): lax.all_to_all(a, AXES, split_axis=0, concat_axis=0, tiled=True, axis_ind...  4.5 us
  transfers between devices with their start and end apart: 13, of which 5 were waited for; matrix products, arithmetic and copies ran while one was open for 1% of the time, Pallas kernels for 11%

profile of v3, /device:TPU:0, one launch (start us, length us, event | category | flops | bytes accessed | tf_op | source)
XLA Modules:
  0.0 219.4 jit_solution(13285699224626982691)
XLA Ops:
  0.0 2.9 %shard_map.55 = (bf16[8,3,16,1152]{3,2,1,0:T(8,128)(2,1)}, bf16[8,3,16,1152]{3,2,1,0:T(8,128)(2,1)}, bf16[8,3,16,1152]{3,2,1,0:T(8,128)(2,1)}) custom-call(s32[1]{0:T(128)} %bitcast.9.z_ref, bf16[64,16,1152]{2,1,0:T(8,128)(2,1)} %bitcast.40, bf16[64,16,1152]{2,1,0:T(8,128)(2,1)} %bitcast.42, bf16[64,16,1152]{2,1,0:T(8,128)(2,1)} %bitcast.44), custom_call_target="tpu_custom_call" | custom-call | tf_op jit(solution)/shard_map/pallas_call | solution.py:40
  2.9 4.1 %collective-permute-start = (bf16[8,3,16,1152]{3,2,1,0:T(8,128)(2,1)}, bf16[8,3,16,1152]{3,2,1,0:T(8,128)(2,1)}, u32[]{:S(2)}, u32[]{:S(2)}) collective-permute-start(bf16[8,3,16,1152]{3,2,1,0:T(8,128)(2,1)} %get-tuple-element.113), channel_id=1, source_target_pairs={{0,16},{1,17},{2,18},{3,19},{4,20},{5,21},{6,22},{7,23},{8,24},{9,... | collective-permute-start | bytes 2654216 | tf_op jit(solution)/shard_map/ppermute | solution.py:190
  7.0 1.4 collective-permute-start.1
  8.4 0.2 collective-permute-start.2
  8.6 0.0 copy-done.5
  8.6 0.5 slice.27
  9.8 52.7 %conditional.3 = (bf16[8,3,16,1152]{3,2,1,0:T(8,128)(2,1)}, bf16[8,3,16,1152]{3,2,1,0:T(8,128)(2,1)}, bf16[8,3,16,1152]{3,2,1,0:T(8,128)(2,1)}, bf16[8,3,16,1152...) conditional(s32[]{:T(128)} %bitcast.8, () %tuple.30, (s32[]{:T(128)}, bf16[64,16,1152]{2,1,0:T(8,128)(2,1)S(1)}, ...), branch_computations={%region_0.1_spmd, %region_1.2_spmd} | conditional | bytes 10616904 | solution.py:186
  9.8 3.6 %branch_1_fun.6 = bf16[8,4,3,16,1152]{4,3,2,1,0:T(8,128)(2,1)} custom-call(s32[1]{0:T(128)} %bitcast.z_ref, bf16[64,16,1152]{2,1,0:T(8,128)(2,1)S(1)} %get-tuple-element.56.refs_0_, bf16[64,16,1152]{2,1,0:T(8,128)(2,1)} %get-tuple-element.57.refs_1_, bf16[64,16,1152]{2,1,0:T(8,128)(2,1)} %get-tuple-element.58.refs_2_), custom_call_target="tpu_custom_call" | custom-call | tf_op jit(solution)/shard_map/cond/branch_1_fun/pallas_call | solution.py:40
  13.3 4.5 %all-to-all-start = ((bf16[8,4,3,16,1152]{4,3,2,1,0:T(8,128)(2,1)}), bf16[8,4,3,16,1152]{4,3,2,1,0:T(8,128)(2,1)}, u32[]{:S(2)}, u32[]{:S(2)}) async-start(bf16[8,4,3,16,1152]{4,3,2,1,0:T(8,128)(2,1)} %branch_1_fun.6), calls=%async_computation | async-start | bytes 7077888 | tf_op jit(solution)/shard_map/cond/branch_1_fun/all_to_all | solution.py:193
  17.9 1.3 branch_1_fun.8
  19.2 40.3 %all-to-all-done.refs_0_ = bf16[8,4,3,16,1152]{4,3,2,1,0:T(8,128)(2,1)} async-done(((bf16[8,4,3,16,1152]{4,3,2,1,0:T(8,128)(2,1)}), bf16[8,4,3,16,1152]{4,3,2,1,0:T(8,128)(2,1)}, u32[]{:S(2)}, u32[]{:S(2)}) %all-to-all-start) | async-done | bytes 3538976 | tf_op jit(solution)/shard_map/cond/branch_1_fun/all_to_all | solution.py:193
  59.5 3.0 %branch_1_fun.7 = (bf16[8,3,16,1152]{3,2,1,0:T(8,128)(2,1)}, bf16[8,3,16,1152]{3,2,1,0:T(8,128)(2,1)}, bf16[8,3,16,1152]{3,2,1,0:T(8,128)(2,1)}, bf16[8,3,16,1152]{3,2,1,0:T(8,128)(2,1)}) custom-call(s32[1]{0:T(128)} %bitcast.z_ref, bf16[8,4,3,16,1152]{4,3,2,1,0:T(8,128)(2,1)} %all-to-all-done.refs_0_), custom_call_target="tpu_custom_call" | custom-call | tf_op jit(solution)/shard_map/cond/branch_1_fun/pallas_call | solution.py:40
  62.5 3.3 %collective-permute-done = bf16[8,3,16,1152]{3,2,1,0:T(8,128)(2,1)} collective-permute-done((bf16[8,3,16,1152]{3,2,1,0:T(8,128)(2,1)}, bf16[8,3,16,1152]{3,2,1,0:T(8,128)(2,1)}, u32[]{:S(2)}, u32[]{:S(2)}) %collective-permute-start) | collective-permute-done | bytes 884768 | tf_op jit(solution)/shard_map/ppermute | solution.py:190
  65.8 0.0 collective-permute-done.1
  65.8 0.5 collective-permute-done.2
  66.3 20.3 %collective-permute-start.6 = (bf16[8,3,16,1152]{3,2,1,0:T(8,128)(2,1)}, bf16[8,3,16,1152]{3,2,1,0:T(8,128)(2,1)}, u32[]{:S(2)}, u32[]{:S(2)}) collective-permute-start(bf16[8,3,16,1152]{3,2,1,0:T(8,128)(2,1)} %get-tuple-element.123), channel_id=1, source_target_pairs={{0,16},{1,17},{2,18},{3,19},{4,20},{5,21},{6,22},{7,23},{8,24},{9,... | collective-permute-start | bytes 2654216 | tf_op jit(solution)/shard_map/ppermute | solution.py:190
  86.6 0.5 collective-permute-start.7
  87.1 0.1 collective-permute-start.8
  87.2 1.1 fusion.5
  88.3 73.9 %conditional.4 = (bf16[8,4,2,8,1152]{4,3,2,1,0:T(8,128)(2,1)S(1)}) conditional(s32[]{:T(128)} %bitcast.8, () %tuple.34, (s32[]{:T(128)}, bf16[8,3,16,1152]{3,2,1,0:T(8,128)(2,1)S(1)}, bf16[8,3,16,1152]{3,2,1,0:T(8,128)(2,1)}, bf16[8,3,16,1152]{3,2,1,0:T(8,128)(2,1)}, bf16[8,3,16,1152]{3,2,1,0:T(8,128)(2,1)}, /*index=5*/f32[256,256]{1,0:T(8,128)}, ...), branch_computations={%region_2.3_spmd, %region_3.4_spmd} | conditional | bytes 21102656 | solution.py:186
  88.3 3.6 %branch_1_fun.9 = bf16[8,4,3,16,1152]{4,3,2,1,0:T(8,128)(2,1)} custom-call(s32[1]{0:T(128)} %bitcast.1.z_ref, bf16[8,3,16,1152]{3,2,1,0:T(8,128)(2,1)S(1)} %get-tuple-element.60.refs_0_, bf16[8,3,16,1152]{3,2,1,0:T(8,128)(2,1)} %get-tuple-element.61.refs_1_, bf16[8,3,16,1152]{3,2,1,0:T(8,128)(2,1)} %get-tuple-element.62.refs_2_, ...), custom_call_target="tpu_custom_call" | custom-call | tf_op jit(solution)/shard_map/cond/branch_1_fun/pallas_call | solution.py:40
  91.8 0.0 copy-start.1
  91.8 45.7 %all_to_all.16 = bf16[8,4,3,16,1152]{4,3,2,1,0:T(8,128)(2,1)S(1)} all-to-all(bf16[8,4,3,16,1152]{4,3,2,1,0:T(8,128)(2,1)} %branch_1_fun.9), channel_id=1, replica_groups={{0,4,1,5,2,6,3,7},{8,12,9,13,10,14,11,15},{16,20,17,21,18,22,19,23},{24..., dimensions={0} | all-to-all | bytes 7077888 | tf_op jit(solution)/shard_map/cond/branch_1_fun/all_to_all | solution.py:193
  137.5 5.8 %branch_1_fun.10 = bf16[8,4,2,8,1152]{4,3,2,1,0:T(8,128)(2,1)S(1)} custom-call(s32[1]{0:T(128)} %bitcast.1.z_ref, bf16[8,4,3,2,8,1152]{5,4,3,2,1,0:T(8,128)(2,1)S(1)} %bitcast.36, bf16[8,4,3,2,8,1152]{5,4,3,2,1,0:T(8,128)(2,1)S(1)} %bitcast.37, bf16[8,4,3,2,8,1152]{5,4,3,2,1,0:T(8,128)(2,1)S(1)} %bitcast.38, bf16[8,4,3,2,8,1152]{5,4,3,2,1,0:T(8,128)(2,1)S(1)} %bitcast.39, ...), custom_call_target="tpu_custom_call" | custom-call | tf_op jit(solution)/shard_map/cond/branch_1_fun/pallas_call | solution.py:115
  143.4 18.8 %all_to_all.17 = bf16[8,4,2,8,1152]{4,3,2,1,0:T(8,128)(2,1)S(1)} all-to-all(bf16[8,4,2,8,1152]{4,3,2,1,0:T(8,128)(2,1)S(1)} %branch_1_fun.10), channel_id=1, replica_groups={{0,4,1,5,2,6,3,7},{8,12,9,13,10,14,11,15},{16,20,17,21,18,22,19,23},{24..., dimensions={0} | all-to-all | bytes 2359296 | tf_op jit(solution)/shard_map/cond/branch_1_fun/all_to_all | solution.py:193
  162.2 0.1 fusion.23
  162.3 3.9 %collective-permute-start.3 = (bf16[128,1152]{1,0:T(8,128)(2,1)S(1)}, bf16[128,1152]{1,0:T(8,128)(2,1)S(1)}, u32[]{:S(2)}, u32[]{:S(2)}) collective-permute-start(bf16[128,1152]{1,0:T(8,128)(2,1)S(1)} %bitcast.50), channel_id=1, source_target_pairs={{0,16},{1,17},{2,18},{3,19},{4,20},{5,21},{6,22},{7,23},{8,24},{9,... | collective-permute-start | bytes 884744 | tf_op jit(solution)/shard_map/ppermute | solution.py:190
  166.2 0.4 collective-permute-start.4
  166.6 0.0 collective-permute-done.6
  166.6 0.2 collective-permute-start.5
  166.8 0.0 collective-permute-done.7
  166.8 0.0 collective-permute-done.8
  166.8 25.9 %conditional.5 = (bf16[8,4,2,8,1152]{4,3,2,1,0:T(8,128)(2,1)S(1)}) conditional(s32[]{:T(128)} %bitcast.8, () %tuple.37, (s32[]{:T(128)}, bf16[8,3,16,1152]{3,2,1,0:T(8,128)(2,1)}, bf16[8,3,16,1152]{3,2,1,0:T(8,128)(2,1)}, bf16[8,3,16,1152]{3,2,1,0:T(8,128)(2,1)}, bf16[8,3,16,1152]{3,2,1,0:T(8,128)(2,1)}, /*index=5*/f32[256,256]{1,0:T(8,128)S(1)}, ...), branch_computations={%region_4.5_spmd, %region_5.6_spmd} | conditional | bytes 2359304 | solution.py:186
  166.8 7.0 %branch_1_fun.11 = bf16[8,4,2,8,1152]{4,3,2,1,0:T(8,128)(2,1)S(1)} custom-call(s32[1]{0:T(128)} %bitcast.3.z_ref, bf16[8,1,3,2,8,1152]{5,4,3,2,1,0:T(8,128)(2,1)} %bitcast.4.refs_0_, bf16[8,1,3,2,8,1152]{5,4,3,2,1,0:T(8,128)(2,1)} %bitcast.5.refs_1_, bf16[8,1,3,2,8,1152]{5,4,3,2,1,0:T(8,128)(2,1)} %bitcast.6.refs_2_, ...), custom_call_target="tpu_custom_call" | custom-call | tf_op jit(solution)/shard_map/cond/branch_1_fun/pallas_call | solution.py:115
  173.9 18.8 %all_to_all.18 = bf16[8,4,2,8,1152]{4,3,2,1,0:T(8,128)(2,1)S(1)} all-to-all(bf16[8,4,2,8,1152]{4,3,2,1,0:T(8,128)(2,1)S(1)} %branch_1_fun.11), channel_id=1, replica_groups={{0,4,1,5,2,6,3,7},{8,12,9,13,10,14,11,15},{16,20,17,21,18,22,19,23},{24..., dimensions={0} | all-to-all | bytes 2359296 | tf_op jit(solution)/shard_map/cond/branch_1_fun/all_to_all | solution.py:193
  192.7 0.0 collective-permute-done.3
  192.7 0.0 collective-permute-done.4
  192.7 0.0 collective-permute-done.5
  192.7 0.1 fusion.22
  192.8 3.8 %collective-permute-start.9 = (bf16[128,1152]{1,0:T(8,128)(2,1)S(1)}, bf16[128,1152]{1,0:T(8,128)(2,1)S(1)}, u32[]{:S(2)}, u32[]{:S(2)}) collective-permute-start(bf16[128,1152]{1,0:T(8,128)(2,1)S(1)} %bitcast.53), channel_id=1, source_target_pairs={{0,16},{1,17},{2,18},{3,19},{4,20},{5,21},{6,22},{7,23},{8,24},{9,... | collective-permute-start | bytes 884744 | tf_op jit(solution)/shard_map/ppermute | solution.py:190
  196.6 0.4 collective-permute-start.10
  197.1 0.2 collective-permute-start.11
  197.3 0.3 broadcast_in_dim.50
  197.8 19.1 %collective-permute-done.9 = bf16[128,1152]{1,0:T(8,128)(2,1)S(1)} collective-permute-done((bf16[128,1152]{1,0:T(8,128)(2,1)S(1)}, bf16[128,1152]{1,0:T(8,128)(2,1)S(1)}, u32[]{:S(2)}, u32[]{:S(2)}) %collective-permute-start.9) | collective-permute-done | bytes 294944 | tf_op jit(solution)/shard_map/ppermute | solution.py:190
  216.9 0.0 collective-permute-done.10
  216.9 1.0 collective-permute-done.11
  218.0 0.0 copy-start.2
  218.0 1.4 copy-done.2
  (17 shorter events, 0.3 us)
Async XLA Ops:
  0.0 8.6 %copy-start.5 = (s32[8,8]{1,0:T(8,128)S(1)}, s32[8,8]{1,0:T(8,128)}, u32[]{:S(2)}) copy-start(s32[8,8]{1,0:T(8,128)} %param.14) | copy-start | bytes 772
  0.0 9.8 %copy-start = (bf16[1,1,1024,1152]{3,2,1,0:T(8,128)(2,1)S(1)}, bf16[1,1,1024,1152]{3,2,1,0:T(8,128)(2,1)}, u32[]{:S(2)}) copy-start(bf16[1,1,1024,1152]{3,2,1,0:T(8,128)(2,1)} %param.11) | copy-start | bytes 7077892
  2.9 62.9 %collective-permute-start = (bf16[8,3,16,1152]{3,2,1,0:T(8,128)(2,1)}, bf16[8,3,16,1152]{3,2,1,0:T(8,128)(2,1)}, u32[]{:S(2)}, u32[]{:S(2)}) collective-permute-start(bf16[8,3,16,1152]{3,2,1,0:T(8,128)(2,1)} %get-tuple-element.113), channel_id=1, source_target_pairs={{0,16},{1,17},{2,18},{3,19},{4,20},{5,21},{6,22},{7,23},{8,24},{9,... | collective-permute-start | bytes 2654216 | tf_op jit(solution)/shard_map/ppermute | solution.py:190
  7.0 58.8 %collective-permute-start.1 = (bf16[8,3,16,1152]{3,2,1,0:T(8,128)(2,1)}, bf16[8,3,16,1152]{3,2,1,0:T(8,128)(2,1)}, u32[]{:S(2)}, u32[]{:S(2)}) collective-permute-start(bf16[8,3,16,1152]{3,2,1,0:T(8,128)(2,1)} %get-tuple-element.114), channel_id=1, source_target_pairs={{0,24},{1,25},{2,26},{3,27},{4,28},{5,29},{6,30},{7,31},{8,16},{9,... | collective-permute-start | bytes 2654216 | tf_op jit(solution)/shard_map/ppermute | solution.py:190
  8.4 57.8 %collective-permute-start.2 = (bf16[8,3,16,1152]{3,2,1,0:T(8,128)(2,1)}, bf16[8,3,16,1152]{3,2,1,0:T(8,128)(2,1)}, u32[]{:S(2)}, u32[]{:S(2)}) collective-permute-start(bf16[8,3,16,1152]{3,2,1,0:T(8,128)(2,1)} %get-tuple-element.115), channel_id=1, source_target_pairs={{0,8},{1,9},{2,10},{3,11},{4,12},{5,13},{6,14},{7,15},{8,0},{9,1},... | collective-permute-start | bytes 2654216 | tf_op jit(solution)/shard_map/ppermute | solution.py:190
  13.3 46.1 %all-to-all-start = ((bf16[8,4,3,16,1152]{4,3,2,1,0:T(8,128)(2,1)}), bf16[8,4,3,16,1152]{4,3,2,1,0:T(8,128)(2,1)}, u32[]{:S(2)}, u32[]{:S(2)}) async-start(bf16[8,4,3,16,1152]{4,3,2,1,0:T(8,128)(2,1)} %branch_1_fun.6), calls=%async_computation | async-start | bytes 7077888 | tf_op jit(solution)/shard_map/cond/branch_1_fun/all_to_all | solution.py:193
  66.3 100.3 %collective-permute-start.6 = (bf16[8,3,16,1152]{3,2,1,0:T(8,128)(2,1)}, bf16[8,3,16,1152]{3,2,1,0:T(8,128)(2,1)}, u32[]{:S(2)}, u32[]{:S(2)}) collective-permute-start(bf16[8,3,16,1152]{3,2,1,0:T(8,128)(2,1)} %get-tuple-element.123), channel_id=1, source_target_pairs={{0,16},{1,17},{2,18},{3,19},{4,20},{5,21},{6,22},{7,23},{8,24},{9,... | collective-permute-start | bytes 2654216 | tf_op jit(solution)/shard_map/ppermute | solution.py:190
  86.6 80.2 %collective-permute-start.7 = (bf16[8,3,16,1152]{3,2,1,0:T(8,128)(2,1)}, bf16[8,3,16,1152]{3,2,1,0:T(8,128)(2,1)}, u32[]{:S(2)}, u32[]{:S(2)}) collective-permute-start(bf16[8,3,16,1152]{3,2,1,0:T(8,128)(2,1)} %get-tuple-element.124), channel_id=1, source_target_pairs={{0,24},{1,25},{2,26},{3,27},{4,28},{5,29},{6,30},{7,31},{8,16},{9,... | collective-permute-start | bytes 2654216 | tf_op jit(solution)/shard_map/ppermute | solution.py:190
  87.1 79.7 %collective-permute-start.8 = (bf16[8,3,16,1152]{3,2,1,0:T(8,128)(2,1)}, bf16[8,3,16,1152]{3,2,1,0:T(8,128)(2,1)}, u32[]{:S(2)}, u32[]{:S(2)}) collective-permute-start(bf16[8,3,16,1152]{3,2,1,0:T(8,128)(2,1)} %get-tuple-element.125), channel_id=1, source_target_pairs={{0,8},{1,9},{2,10},{3,11},{4,12},{5,13},{6,14},{7,15},{8,0},{9,1},... | collective-permute-start | bytes 2654216 | tf_op jit(solution)/shard_map/ppermute | solution.py:190
  91.8 45.7 %copy-start.1 = (bf16[1152,1152]{1,0:T(8,128)(2,1)S(1)}, bf16[1152,1152]{1,0:T(8,128)(2,1)}, u32[]{:S(2)}) copy-start(bf16[1152,1152]{1,0:T(8,128)(2,1)} %get-tuple-element.65.refs_5_) | copy-start | bytes 7962628 | tf_op jit(solution)/shard_map/cond
  91.8 45.7 %copy-start.4 = (f32[256,256]{1,0:T(8,128)S(1)}, f32[256,256]{1,0:T(8,128)}, u32[]{:S(2)}) copy-start(f32[256,256]{1,0:T(8,128)} %get-tuple-element.64.refs_4_) | copy-start | bytes 786436 | tf_op jit(solution)/shard_map/cond
  162.2 4.6 %copy-start.3 = (f32[256,256]{1,0:T(8,128)S(1)}, f32[256,256]{1,0:T(8,128)}, u32[]{:S(2)}) copy-start(f32[256,256]{1,0:T(8,128)} %fusion.5) | copy-start | bytes 786436
  162.3 30.4 %collective-permute-start.3 = (bf16[128,1152]{1,0:T(8,128)(2,1)S(1)}, bf16[128,1152]{1,0:T(8,128)(2,1)S(1)}, u32[]{:S(2)}, u32[]{:S(2)}) collective-permute-start(bf16[128,1152]{1,0:T(8,128)(2,1)S(1)} %bitcast.50), channel_id=1, source_target_pairs={{0,16},{1,17},{2,18},{3,19},{4,20},{5,21},{6,22},{7,23},{8,24},{9,... | collective-permute-start | bytes 884744 | tf_op jit(solution)/shard_map/ppermute | solution.py:190
  166.2 26.6 %collective-permute-start.4 = (bf16[128,1152]{1,0:T(8,128)(2,1)S(1)}, bf16[128,1152]{1,0:T(8,128)(2,1)S(1)}, u32[]{:S(2)}, u32[]{:S(2)}) collective-permute-start(bf16[128,1152]{1,0:T(8,128)(2,1)S(1)} %bitcast.49), channel_id=1, source_target_pairs={{0,24},{1,25},{2,26},{3,27},{4,28},{5,29},{6,30},{7,31},{8,16},{9,... | collective-permute-start | bytes 884744 | tf_op jit(solution)/shard_map/ppermute | solution.py:190
  166.6 26.1 %collective-permute-start.5 = (bf16[128,1152]{1,0:T(8,128)(2,1)S(1)}, bf16[128,1152]{1,0:T(8,128)(2,1)S(1)}, u32[]{:S(2)}, u32[]{:S(2)}) collective-permute-start(bf16[128,1152]{1,0:T(8,128)(2,1)S(1)} %bitcast.48), channel_id=1, source_target_pairs={{0,8},{1,9},{2,10},{3,11},{4,12},{5,13},{6,14},{7,15},{8,0},{9,1},... | collective-permute-start | bytes 884744 | tf_op jit(solution)/shard_map/ppermute | solution.py:190
  192.8 24.0 %collective-permute-start.9 = (bf16[128,1152]{1,0:T(8,128)(2,1)S(1)}, bf16[128,1152]{1,0:T(8,128)(2,1)S(1)}, u32[]{:S(2)}, u32[]{:S(2)}) collective-permute-start(bf16[128,1152]{1,0:T(8,128)(2,1)S(1)} %bitcast.53), channel_id=1, source_target_pairs={{0,16},{1,17},{2,18},{3,19},{4,20},{5,21},{6,22},{7,23},{8,24},{9,... | collective-permute-start | bytes 884744 | tf_op jit(solution)/shard_map/ppermute | solution.py:190
  196.6 20.3 %collective-permute-start.10 = (bf16[128,1152]{1,0:T(8,128)(2,1)S(1)}, bf16[128,1152]{1,0:T(8,128)(2,1)S(1)}, u32[]{:S(2)}, u32[]{:S(2)}) collective-permute-start(bf16[128,1152]{1,0:T(8,128)(2,1)S(1)} %bitcast.52), channel_id=1, source_target_pairs={{0,24},{1,25},{2,26},{3,27},{4,28},{5,29},{6,30},{7,31},{8,16},{9,... | collective-permute-start | bytes 884744 | tf_op jit(solution)/shard_map/ppermute | solution.py:190
  197.1 20.9 %collective-permute-start.11 = (bf16[128,1152]{1,0:T(8,128)(2,1)S(1)}, bf16[128,1152]{1,0:T(8,128)(2,1)S(1)}, u32[]{:S(2)}, u32[]{:S(2)}) collective-permute-start(bf16[128,1152]{1,0:T(8,128)(2,1)S(1)} %bitcast.51), channel_id=1, source_target_pairs={{0,8},{1,9},{2,10},{3,11},{4,12},{5,13},{6,14},{7,15},{8,0},{9,1},... | collective-permute-start | bytes 884744 | tf_op jit(solution)/shard_map/ppermute | solution.py:190
  218.0 1.4 copy-start.2

commit v4 on v3

--- a/solution.py
+++ b/solution.py
@@ -1,3 +1,4 @@
+import functools
 import math
 
 import jax
@@ -15,19 +16,19 @@
 AXES = ("tm", "pix")
 
 
-def mover(body, arrays, out_shapes, number, scalar):
+def mover(body, arrays, out_shapes, number, scalar, stage_shapes=None, place=None, aliases=None):
     count, outs = len(arrays), len(out_shapes)
+    stage_shapes = stage_shapes or out_shapes
+    place = place or (lambda out_refs: out_refs)
 
     def kernel(z_ref, *refs):
         sems, out_sems = refs[-2:]
-        stages = refs[count + outs : count + 2 * outs]
+        stages, targets = refs[count + outs : -2], place(refs[count : count + outs])
         arriving, slot = [], 0
         for pairs in body(z_ref[0], refs[:count], stages):
             arriving.append([pltpu.make_async_copy(a, b, sems.at[slot + i]) for i, (a, b) in enumerate(pairs)])
             slot += len(pairs)
-        leaving = [
-            pltpu.make_async_copy(stages[i], refs[count + i], out_sems.at[i]) for i in range(outs)
-        ]
+        leaving = [pltpu.make_async_copy(a, b, out_sems.at[i]) for i, (a, b) in enumerate(zip(stages, targets))]
         for copy in sum(arriving, []):
             copy.start()
         for copies, out in zip(arriving, leaving):
@@ -43,15 +44,16 @@
             num_scalar_prefetch=1,
             in_specs=[pl.BlockSpec(memory_space=pl.ANY)] * count,
             out_specs=[pl.BlockSpec(memory_space=pl.ANY)] * outs,
-            scratch_shapes=[pltpu.VMEM(s, jnp.bfloat16) for s in out_shapes]
-            + [pltpu.SemaphoreType.DMA((number,)), pltpu.SemaphoreType.DMA((outs,))],
+            scratch_shapes=[pltpu.VMEM(s, jnp.bfloat16) for s in stage_shapes]
+            + [pltpu.SemaphoreType.DMA((number,)), pltpu.SemaphoreType.DMA((len(stage_shapes),))],
         ),
         out_shape=[jax.ShapeDtypeStruct(s, jnp.bfloat16) for s in out_shapes],
+        input_output_aliases=aliases or {},
         cost_estimate=pl.CostEstimate(flops=0, bytes_accessed=0, transcendentals=0),
     )(scalar.reshape(1), *arrays)
 
 
-def attend_kernel(z_ref, *refs):
+def attend_kernel(by_frame, z_ref, *refs):
     slots, (bias_ref, w_hbm, out_ref, acc_ref, w_ref, w_sem) = refs[:HI], refs[HI:]
     rows, feats = acc_ref.shape
     part = rows // HI
@@ -101,32 +103,39 @@
         fetch.wait()
 
     projected = jnp.dot(acc_ref[...], w_ref[...], preferred_element_type=jnp.float32).astype(jnp.bfloat16)
-    for slot in range(HI):
-        out_ref[:, slot, 0] = projected[slot * part : (slot + 1) * part].reshape(out_ref.shape[0], SUB, feats)
-
-
-def attend(place, slots, bias, w_out):
+    for slot, k in enumerate(NEAR):
+        own = projected[slot * part : (slot + 1) * part]
+        if by_frame:
+            out_ref[:, z_ref[0] ^ k, :, 0] = own.reshape(out_ref.shape[0], out_ref.shape[2], SUB, feats)
+        else:
+            out_ref[:, slot, 0] = own.reshape(out_ref.shape[0], SUB, feats)
+
+
+def attend(place, slots, bias, w_out, outer=None):
     sources, _, _, groups, sub, feats = slots[0][0].shape
     rows = HI * sources * sub
 
+    shape = (sources, HI) if outer is None else (outer, HI, sources // outer)
+    zeros = (0,) * len(shape)
+
     def spec(entry):
         return pl.BlockSpec((sources, 1, 3, 1, sub, feats), lambda g, z: (0, entry, 0, g, 0, 0))
 
     return pl.pallas_call(
-        attend_kernel,
+        functools.partial(attend_kernel, outer is not None),
         grid_spec=pltpu.PrefetchScalarGridSpec(
             num_scalar_prefetch=1,
             grid=(groups,),
             in_specs=[spec(entry) for _, entry in slots]
             + [pl.BlockSpec((rows, rows), lambda g, z: (0, 0)), pl.BlockSpec(memory_space=pl.ANY)],
-            out_specs=pl.BlockSpec((sources, HI, 1, sub, feats), lambda g, z: (0, 0, g, 0, 0)),
+            out_specs=pl.BlockSpec((*shape, 1, sub, feats), lambda g, z: (*zeros, g, 0, 0)),
             scratch_shapes=[
                 pltpu.VMEM((rows, feats), jnp.bfloat16),
                 pltpu.VMEM((feats, feats), jnp.bfloat16),
                 pltpu.SemaphoreType.DMA,
             ],
         ),
-        out_shape=jax.ShapeDtypeStruct((sources, HI, groups, sub, feats), jnp.bfloat16),
+        out_shape=jax.ShapeDtypeStruct((*shape, groups, sub, feats), jnp.bfloat16),
         compiler_params=pltpu.CompilerParams(vmem_limit_bytes=48 * 2**20),
         cost_estimate=pl.CostEstimate(flops=0, bytes_accessed=0, transcendentals=0),
     )(place.reshape(1), *[a for a, _ in slots], bias, w_out)
@@ -178,7 +187,7 @@
     row = jnp.arange(HI * plane * SUB, dtype=jnp.int32)
     slot, source = row // (plane * SUB), row // SUB % plane
     frame = source // n_low * n_pix + (high ^ sum(jnp.where(slot == s, k, 0) for s, k in enumerate(NEAR))) * n_low + source % n_low
-    bias = bias_of(mask, frame, row % SUB, frames // mask.shape[0])
+    blen = frames // mask.shape[0]
     always = mask[0, 0] >= 0
 
     def region(f, *args):
@@ -211,48 +220,57 @@
 
     def pack(z, ins, outs):
         return [
-            [(a.at[pl.ds((HI + y) * plane, plane)], outs[0].at[:, y, t]) for y in range(HI) for t, a in enumerate(ins)]
+            [(a.at[1, :, y], outs[0].at[:, :, y, t]) for y in range(HI) for t, a in enumerate(ins)]
         ]
 
     def split(z, ins, outs):
         return [[(ins[0].at[:, z ^ k], out)] for k, out in zip(NEAR, outs)]
 
     def start_second(*flat):
-        [packed] = mover(pack, flat, [whole], 3 * HI, high)
-        packed, flat = tie((packed, flat))
-        return mover(split, [across(packed)], [piece] * HI, HI, high), cut((0,))(*flat)
-
-    second, own = region(start_second, *flat)
-    second, moved = tie((second, [*own, *moved]))
+        owned = [a.reshape(2, n_tm, HI, n_low, tall, feats) for a in flat]
+        [packed] = mover(pack, owned, [(n_tm, n_low, *whole[1:])], 3 * HI, high)
+        packed, flat = tie((packed.reshape(whole), flat))
+        bias = bias_of(mask, frame, row % SUB, blen)
+        return mover(split, [across(packed)], [piece] * HI, HI, high), cut((0,))(*flat), bias
+
+    second, own, bias = region(start_second, *flat)
+    late = NEAR.index(3)
+    slots = [s for s in range(HI) if s != late]
+
+    def each(z, ins, stages):
+        return [[(a, stage)] for a, stage in zip(ins, stages)]
+
+    def early_place(outs):
+        return [outs[0].at[:, s] for s in slots]
+
+    early = [[*own, *moved][s] for s in slots]
+    packed = mover(each, early, [whole], HI - 1, high, [piece] * (HI - 1), early_place)
+    second, packed, last = tie((second, packed, moved[late - 1]))
     second = [second[0], *[along(a, k) for a, k in zip(second[1:], NEAR[1:])]]
-
-    def gather(z, ins, outs):
-        return [[(a, outs[0].at[:, k]) for k, a in enumerate(ins)]]
-
-    def finish_first(moved, bias, w_out):
-        [packed] = mover(gather, moved, [whole], HI, high)
+    [packed] = mover(each, [last, *packed], [whole], 1, high, [piece], lambda outs: [outs[0].at[:, late]], {2: 0})
+
+    def finish_first(packed, bias, w_out):
         packed = across(packed).reshape(plane, HI, 3, 2, SUB, feats)
         return across(attend(high, [(packed, k) for k in range(HI)], bias, w_out))
 
     def finish_second(second, bias, w_out):
         second = [a.reshape(plane, 1, 3, 2, SUB, feats) for a in second]
-        return across(attend(high, [(a, 0) for a in second], bias, w_out))
+        out = attend(high, [(a, 0) for a in second], bias, w_out, n_tm)
+        return lax.all_to_all(out.reshape(frames, tall, feats), AXES, split_axis=0, concat_axis=0, tiled=True)
 
     def give_back(done):
         pieces = [done[:, k].reshape(plane * tall, feats) for k in range(HI)]
         return [pieces[0], *[along(a, k) for a, k in zip(pieces[1:], NEAR[1:])]]
 
-    done_first = region(finish_first, moved, bias, w_out)
+    done_first = region(finish_first, packed, bias, w_out)
     second[0], done_first = tie((second[0], done_first))
     back_first = give_back(done_first)
     done_second = region(finish_second, second, bias, w_out)
     back_first, done_second = tie((back_first, done_second))
-    back_second = give_back(done_second)
-
     result = jnp.zeros((2 * HI, plane * tall, feats), jnp.bfloat16)
-    for half, back in enumerate((back_first, back_second)):
-        for k, piece in zip(NEAR, back):
-            result = lax.dynamic_update_index_in_dim(result, piece, half * HI + (high ^ k), 0)
+    for k, piece in zip(NEAR, back_first):
+        result = lax.dynamic_update_index_in_dim(result, piece, high ^ k, 0)
+    result = lax.dynamic_update_slice(result, done_second.reshape(HI, plane * tall, feats), (HI, 0, 0))
     return result.reshape(query.shape)
 
 

time: 222 us -> 219 us (0.986); the launches traced: 219 us -> 219 us
  blocking collectives: 83.3 us -> 111 us
  waiting for transfers between devices: 64.2 us -> 40.5 us
  starting transfers between devices: 40.1 us -> 35.6 us
    all_to_all x0 -> x1, blocking collectives: none -> 46.3 us  [finish_second(): lax.all_to_all(out.reshape(frames, tall, feats), AXES, split_axis=0, conc...]
    ppermute x12 -> x9, waiting for transfers between devices: 23.8 us -> 0.58 us  [along(): return lax.ppermute(a, ('pix', 'tm'), pairs)]
    all_to_all x3 -> x2, blocking collectives: 83.3 us -> 64.3 us  [across(): lax.all_to_all(a, AXES, split_axis=0, concat_axis=0, tiled=True, axis_ind...]
    ppermute x12 -> x9, starting transfers between devices: 35.6 us -> 31.1 us  [along(): return lax.ppermute(a, ('pix', 'tm'), pairs)]
    pallas_call x5 -> x6, Pallas kernels: 14.3 us -> 13.9 us  [mover(): pl.pallas_call(kernel, grid_spec=pltpu.PrefetchScalarGridSpec(num_scalar_...]
  transfers between devices with their start and end apart: 13 -> 10, of which waited for: 5 -> 2; matrix products, arithmetic and copies ran while one was open for 1% -> 0% of each run, Pallas kernels for 11% -> 11%
where the time goes in v4:
time: 219 us
  blocking collectives  111 us (51%)
  waiting for transfers between devices  40.5 us (18%)
  starting transfers between devices  35.6 us (16%)
  Pallas kernels  26.8 us (12%)
  local copies, waits for them, and re-layouts  3.71 us (2%)
    all_to_all x2, blocking collectives, across(): lax.all_to_all(a, AXES, split_axis=0, concat_axis=0, tiled=True, axis_ind...  64.3 us
    all_to_all x1, blocking collectives, finish_second(): lax.all_to_all(out.reshape(frames, tall, feats), AXES, split_axis=0, conc...  46.3 us
    all_to_all x1, waiting for transfers between devices, across(): lax.all_to_all(a, AXES, split_axis=0, concat_axis=0, tiled=True, axis_ind...  39.9 us
    ppermute x9, starting transfers between devices, along(): return lax.ppermute(a, ('pix', 'tm'), pairs)  31.1 us
    pallas_call x6, Pallas kernels, mover(): pl.pallas_call(kernel, grid_spec=pltpu.PrefetchScalarGridSpec(num_scalar_...  13.9 us
    pallas_call x2, Pallas kernels, attend(): pl.pallas_call(functools.partial(attend_kernel, outer is not None), grid_...  12.9 us
    all_to_all x1, starting transfers between devices, across(): lax.all_to_all(a, AXES, split_axis=0, concat_axis=0, tiled=True, axis_ind...  4.51 us
  transfers between devices with their start and end apart: 10, of which 2 were waited for; matrix products, arithmetic and copies ran while one was open for 0% of the time, Pallas kernels for 11%

profile of v4, /device:TPU:0, one launch (start us, length us, event | category | flops | bytes accessed | tf_op | source)
XLA Modules:
  0.0 218.6 jit_solution(4051170971030344823)
XLA Ops:
  0.0 2.9 %shard_map.55 = (bf16[8,3,16,1152]{3,2,1,0:T(8,128)(2,1)}, bf16[8,3,16,1152]{3,2,1,0:T(8,128)(2,1)}, bf16[8,3,16,1152]{3,2,1,0:T(8,128)(2,1)}) custom-call(s32[1]{0:T(128)} %bitcast.14.z_ref, bf16[64,16,1152]{2,1,0:T(8,128)(2,1)} %bitcast.39, bf16[64,16,1152]{2,1,0:T(8,128)(2,1)} %bitcast.42, bf16[64,16,1152]{2,1,0:T(8,128)(2,1)} %bitcast.45), custom_call_target="tpu_custom_call" | custom-call | tf_op jit(solution)/shard_map/pallas_call | solution.py:41
  2.9 4.1 %collective-permute-start = (bf16[8,3,16,1152]{3,2,1,0:T(8,128)(2,1)}, bf16[8,3,16,1152]{3,2,1,0:T(8,128)(2,1)}, u32[]{:S(2)}, u32[]{:S(2)}) collective-permute-start(bf16[8,3,16,1152]{3,2,1,0:T(8,128)(2,1)} %get-tuple-element.221), channel_id=1, source_target_pairs={{0,16},{1,17},{2,18},{3,19},{4,20},{5,21},{6,22},{7,23},{8,24},{9,... | collective-permute-start | bytes 2654216 | tf_op jit(solution)/shard_map/ppermute | solution.py:199
  7.0 1.6 collective-permute-start.1
  8.6 0.0 collective-permute-start.2
  8.6 0.0 copy-done.7
  8.6 0.6 slice.15
  10.0 0.0 copy-done
  10.0 52.8 %conditional.3 = (bf16[8,3,16,1152]{3,2,1,0:T(8,128)(2,1)}, bf16[8,3,16,1152]{3,2,1,0:T(8,128)(2,1)}, bf16[8,3,16,1152]{3,2,1,0:T(8,128)(2,1)}, bf16[8,3,16,1152...) conditional(s32[]{:T(128)} %bitcast.13, () %tuple.38, (s32[]{:T(128)}, ...), branch_computations={%region_0.1_spmd, %region_1.2_spmd} | conditional | flops 1365312 | bytes 10893916 | solution.py:195
  10.0 3.6 %branch_1_fun.5 = bf16[4,2,4,3,16,1152]{5,4,3,2,1,0:T(8,128)(2,1)} custom-call(s32[1]{0:T(128)} %bitcast.z_ref, bf16[2,4,4,2,16,1152]{5,4,3,2,1,0:T(8,128)(2,1)S(1)} %bitcast.41, bf16[2,4,4,2,16,1152]{5,4,3,2,1,0:T(8,128)(2,1)} %bitcast.44, bf16[2,4,4,2,16,1152]{5,4,3,2,1,0:T(8,128)(2,1)} %bitcast.47), custom_call_target="tpu_custom_call" | custom-call | tf_op jit(solution)/shard_map/cond/branch_1_fun/pallas_call | solution.py:41
  13.6 4.5 %all-to-all-start.3 = ((bf16[8,4,3,16,1152]{4,3,2,1,0:T(8,128)(2,1)}), bf16[8,4,3,16,1152]{4,3,2,1,0:T(8,128)(2,1)}, u32[]{:S(2)}, u32[]{:S(2)}) async-start(bf16[8,4,3,16,1152]{4,3,2,1,0:T(8,128)(2,1)} %bitcast.48), calls=%async_computation.3 | async-start | bytes 7077888 | tf_op jit(solution)/shard_map/cond/branch_1_fun/all_to_all | solution.py:202
  18.1 1.3 branch_1_fun.7
  19.5 0.4 fusion.5
  19.8 39.9 %all-to-all-done.3.refs_0_ = bf16[8,4,3,16,1152]{4,3,2,1,0:T(8,128)(2,1)} async-done(((bf16[8,4,3,16,1152]{4,3,2,1,0:T(8,128)(2,1)}), bf16[8,4,3,16,1152]{4,3,2,1,0:T(8,128)(2,1)}, u32[]{:S(2)}, u32[]{:S(2)}) %all-to-all-start.3) | async-done | bytes 3538976 | tf_op jit(solution)/shard_map/cond/branch_1_fun/all_to_all | solution.py:202
  59.7 3.0 %branch_1_fun.6 = (bf16[8,3,16,1152]{3,2,1,0:T(8,128)(2,1)}, bf16[8,3,16,1152]{3,2,1,0:T(8,128)(2,1)}, bf16[8,3,16,1152]{3,2,1,0:T(8,128)(2,1)}, bf16[8,3,16,1152]{3,2,1,0:T(8,128)(2,1)}) custom-call(s32[1]{0:T(128)} %bitcast.z_ref, bf16[8,4,3,16,1152]{4,3,2,1,0:T(8,128)(2,1)} %all-to-all-done.3.refs_0_), custom_call_target="tpu_custom_call" | custom-call | tf_op jit(solution)/shard_map/cond/branch_1_fun/pallas_call | solution.py:41
  62.8 0.0 copy-start.2
  62.8 0.0 collective-permute-done.refs_1_
  62.8 0.0 collective-permute-done.1.refs_2_
  62.8 0.9 copy-done.2
  63.7 0.1 copy-done.3
  63.8 1.8 shard_map.56.refs_1_
  65.6 0.6 collective-permute-done.2.refs_0_
  66.2 20.3 %collective-permute-start.6 = (bf16[8,3,16,1152]{3,2,1,0:T(8,128)(2,1)}, bf16[8,3,16,1152]{3,2,1,0:T(8,128)(2,1)}, u32[]{:S(2)}, u32[]{:S(2)}) collective-permute-start(bf16[8,3,16,1152]{3,2,1,0:T(8,128)(2,1)} %get-tuple-element.230), channel_id=1, source_target_pairs={{0,16},{1,17},{2,18},{3,19},{4,20},{5,21},{6,22},{7,23},{8,24},{9,... | collective-permute-start | bytes 2654216 | tf_op jit(solution)/shard_map/ppermute | solution.py:199
  86.5 0.4 collective-permute-start.7
  86.9 0.1 collective-permute-start.8
  87.1 1.2 shard_map.57
  88.3 70.2 %conditional.4 = (bf16[8,4,2,8,1152]{4,3,2,1,0:T(8,128)(2,1)S(1)}) conditional(s32[]{:T(128)} %bitcast.13, () %tuple.42, (s32[]{:T(128)}, bf16[8,4,3,16,1152]{4,3,2,1,0:T(8,128)(2,1)S(1)}, f32[256,256]{1,0:T(8,128)}, bf16[1152,1152]{1,0:T(8,128)(2,1)}) %tuple.63), branch_computations={%region_2.3_spmd, %region_3.4_spmd} | conditional | bytes 21102656 | solution.py:195
  88.3 0.0 copy-start.1
  88.4 45.5 %all_to_all.16 = bf16[8,4,3,16,1152]{4,3,2,1,0:T(8,128)(2,1)S(1)} all-to-all(bf16[8,4,3,16,1152]{4,3,2,1,0:T(8,128)(2,1)S(1)} %get-tuple-element.172), channel_id=1, replica_groups={{0,4,1,5,2,6,3,7},{8,12,9,13,10,14,11,15},{16,20,17,21,18,22,19,23},{24..., dimensions={0} | all-to-all | bytes 7077888 | tf_op jit(solution)/shard_map/cond/branch_1_fun/all_to_all | solution.py:202
  133.8 0.0 copy-done.1
  133.8 5.8 %branch_1_fun.8 = bf16[8,4,2,8,1152]{4,3,2,1,0:T(8,128)(2,1)S(1)} custom-call(s32[1]{0:T(128)} %bitcast.5.z_ref, bf16[8,4,3,2,8,1152]{5,4,3,2,1,0:T(8,128)(2,1)S(1)} %bitcast.34, bf16[8,4,3,2,8,1152]{5,4,3,2,1,0:T(8,128)(2,1)S(1)} %bitcast.35, bf16[8,4,3,2,8,1152]{5,4,3,2,1,0:T(8,128)(2,1)S(1)} %bitcast.36, bf16[8,4,3,2,8,1152]{5,4,3,2,1,0:T(8,128)(2,1)S(1)} %bitcast.37, ...), custom_call_target="tpu_custom_call" | custom-call | tf_op jit(solution)/shard_map/cond/branch_1_fun/pallas_call | solution.py:124
  139.7 18.8 %all_to_all.17 = bf16[8,4,2,8,1152]{4,3,2,1,0:T(8,128)(2,1)S(1)} all-to-all(bf16[8,4,2,8,1152]{4,3,2,1,0:T(8,128)(2,1)S(1)} %branch_1_fun.8), channel_id=1, replica_groups={{0,4,1,5,2,6,3,7},{8,12,9,13,10,14,11,15},{16,20,17,21,18,22,19,23},{24..., dimensions={0} | all-to-all | bytes 2359296 | tf_op jit(solution)/shard_map/cond/branch_1_fun/all_to_all | solution.py:202
  158.5 0.1 fusion.21
  158.6 3.9 %collective-permute-start.3 = (bf16[128,1152]{1,0:T(8,128)(2,1)S(1)}, bf16[128,1152]{1,0:T(8,128)(2,1)S(1)}, u32[]{:S(2)}, u32[]{:S(2)}) collective-permute-start(bf16[128,1152]{1,0:T(8,128)(2,1)S(1)} %bitcast.53), channel_id=1, source_target_pairs={{0,16},{1,17},{2,18},{3,19},{4,20},{5,21},{6,22},{7,23},{8,24},{9,... | collective-permute-start | bytes 884744 | tf_op jit(solution)/shard_map/ppermute | solution.py:199
  162.5 0.4 collective-permute-start.4
  162.9 0.0 collective-permute-done.6
  162.9 0.2 collective-permute-start.5
  163.1 0.0 collective-permute-done.7
  163.1 0.0 collective-permute-done.8
  163.1 53.5 %conditional.5 = (bf16[32,16,1152]{2,1,0:T(8,128)(2,1)S(1)}) conditional(s32[]{:T(128)} %bitcast.13, () %tuple.45, (s32[]{:T(128)}, bf16[8,3,16,1152]{3,2,1,0:T(8,128)(2,1)}, bf16[8,3,16,1152]{3,2,1,0:T(8,128)(2,1)}, bf16[8,3,16,1152]{3,2,1,0:T(8,128)(2,1)}, bf16[8,3,16,1152]{3,2,1,0:T(8,128)(2,1)}, /*index=5*/f32[256,256]{1,0:T(8,128)S(1)}, ...), branch_computations={%region_4.5_spmd, %region_5.6_spmd} | conditional | bytes 2359304 | solution.py:195
  163.1 7.1 %branch_1_fun.9 = bf16[4,4,2,2,8,1152]{5,4,3,2,1,0:T(8,128)(2,1)S(1)} custom-call(s32[1]{0:T(128)} %bitcast.7.z_ref, bf16[8,1,3,2,8,1152]{5,4,3,2,1,0:T(8,128)(2,1)} %bitcast.8.refs_0_, bf16[8,1,3,2,8,1152]{5,4,3,2,1,0:T(8,128)(2,1)} %bitcast.9.refs_1_, bf16[8,1,3,2,8,1152]{5,4,3,2,1,0:T(8,128)(2,1)} %bitcast.10.refs_2_, ...), custom_call_target="tpu_custom_call" | custom-call | tf_op jit(solution)/shard_map/cond/branch_1_fun/pallas_call | solution.py:124
  170.2 46.3 %all_to_all.18 = bf16[32,16,1152]{2,1,0:T(8,128)(2,1)S(1)} all-to-all(bf16[32,16,1152]{2,1,0:T(8,128)(2,1)S(1)} %bitcast.38), channel_id=1, replica_groups=mesh['pix'=8,'tm'=4] {'tm','pix'}, dimensions={0} | all-to-all | bytes 2359296 | tf_op jit(solution)/shard_map/cond/branch_1_fun/all_to_all | solution.py:259
  216.6 0.0 collective-permute-done.3
  216.6 0.0 collective-permute-done.4
  216.6 0.0 collective-permute-done.5
  216.6 0.3 broadcast_in_dim.38
  217.1 0.2 bitcast_dynamic-update-slice_fusion
  217.2 0.0 copy-start.6
  217.2 1.4 copy-done.6
  (19 shorter events, 0.2 us)
Async XLA Ops:
  0.0 8.6 %copy-start.7 = (s32[8,8]{1,0:T(8,128)S(1)}, s32[8,8]{1,0:T(8,128)}, u32[]{:S(2)}) copy-start(s32[8,8]{1,0:T(8,128)} %param.14) | copy-start | bytes 772
  0.0 10.0 %copy-start = (bf16[1,1,1024,1152]{3,2,1,0:T(8,128)(2,1)S(1)}, bf16[1,1,1024,1152]{3,2,1,0:T(8,128)(2,1)}, u32[]{:S(2)}) copy-start(bf16[1,1,1024,1152]{3,2,1,0:T(8,128)(2,1)} %param.11) | copy-start | bytes 7077892
  2.9 59.9 %collective-permute-start = (bf16[8,3,16,1152]{3,2,1,0:T(8,128)(2,1)}, bf16[8,3,16,1152]{3,2,1,0:T(8,128)(2,1)}, u32[]{:S(2)}, u32[]{:S(2)}) collective-permute-start(bf16[8,3,16,1152]{3,2,1,0:T(8,128)(2,1)} %get-tuple-element.221), channel_id=1, source_target_pairs={{0,16},{1,17},{2,18},{3,19},{4,20},{5,21},{6,22},{7,23},{8,24},{9,... | collective-permute-start | bytes 2654216 | tf_op jit(solution)/shard_map/ppermute | solution.py:199
  7.0 55.8 %collective-permute-start.1 = (bf16[8,3,16,1152]{3,2,1,0:T(8,128)(2,1)}, bf16[8,3,16,1152]{3,2,1,0:T(8,128)(2,1)}, u32[]{:S(2)}, u32[]{:S(2)}) collective-permute-start(bf16[8,3,16,1152]{3,2,1,0:T(8,128)(2,1)} %get-tuple-element.222), channel_id=1, source_target_pairs={{0,8},{1,9},{2,10},{3,11},{4,12},{5,13},{6,14},{7,15},{8,0},{9,1},... | collective-permute-start | bytes 2654216 | tf_op jit(solution)/shard_map/ppermute | solution.py:199
  8.6 57.6 %collective-permute-start.2 = (bf16[8,3,16,1152]{3,2,1,0:T(8,128)(2,1)}, bf16[8,3,16,1152]{3,2,1,0:T(8,128)(2,1)}, u32[]{:S(2)}, u32[]{:S(2)}) collective-permute-start(bf16[8,3,16,1152]{3,2,1,0:T(8,128)(2,1)} %get-tuple-element.223), channel_id=1, source_target_pairs={{0,24},{1,25},{2,26},{3,27},{4,28},{5,29},{6,30},{7,31},{8,16},{9,... | collective-permute-start | bytes 2654216 | tf_op jit(solution)/shard_map/ppermute | solution.py:199
  13.6 46.1 %all-to-all-start.3 = ((bf16[8,4,3,16,1152]{4,3,2,1,0:T(8,128)(2,1)}), bf16[8,4,3,16,1152]{4,3,2,1,0:T(8,128)(2,1)}, u32[]{:S(2)}, u32[]{:S(2)}) async-start(bf16[8,4,3,16,1152]{4,3,2,1,0:T(8,128)(2,1)} %bitcast.48), calls=%async_computation.3 | async-start | bytes 7077888 | tf_op jit(solution)/shard_map/cond/branch_1_fun/all_to_all | solution.py:202
  62.8 0.9 copy-start.2
  62.8 1.0 copy-start.3
  66.2 96.7 %collective-permute-start.6 = (bf16[8,3,16,1152]{3,2,1,0:T(8,128)(2,1)}, bf16[8,3,16,1152]{3,2,1,0:T(8,128)(2,1)}, u32[]{:S(2)}, u32[]{:S(2)}) collective-permute-start(bf16[8,3,16,1152]{3,2,1,0:T(8,128)(2,1)} %get-tuple-element.230), channel_id=1, source_target_pairs={{0,16},{1,17},{2,18},{3,19},{4,20},{5,21},{6,22},{7,23},{8,24},{9,... | collective-permute-start | bytes 2654216 | tf_op jit(solution)/shard_map/ppermute | solution.py:199
  86.5 76.6 %collective-permute-start.7 = (bf16[8,3,16,1152]{3,2,1,0:T(8,128)(2,1)}, bf16[8,3,16,1152]{3,2,1,0:T(8,128)(2,1)}, u32[]{:S(2)}, u32[]{:S(2)}) collective-permute-start(bf16[8,3,16,1152]{3,2,1,0:T(8,128)(2,1)} %get-tuple-element.231), channel_id=1, source_target_pairs={{0,24},{1,25},{2,26},{3,27},{4,28},{5,29},{6,30},{7,31},{8,16},{9,... | collective-permute-start | bytes 2654216 | tf_op jit(solution)/shard_map/ppermute | solution.py:199
  86.9 76.2 %collective-permute-start.8 = (bf16[8,3,16,1152]{3,2,1,0:T(8,128)(2,1)}, bf16[8,3,16,1152]{3,2,1,0:T(8,128)(2,1)}, u32[]{:S(2)}, u32[]{:S(2)}) collective-permute-start(bf16[8,3,16,1152]{3,2,1,0:T(8,128)(2,1)} %get-tuple-element.232), channel_id=1, source_target_pairs={{0,8},{1,9},{2,10},{3,11},{4,12},{5,13},{6,14},{7,15},{8,0},{9,1},... | collective-permute-start | bytes 2654216 | tf_op jit(solution)/shard_map/ppermute | solution.py:199
  88.3 45.5 %copy-start.1 = (bf16[1152,1152]{1,0:T(8,128)(2,1)S(1)}, bf16[1152,1152]{1,0:T(8,128)(2,1)}, u32[]{:S(2)}) copy-start(bf16[1152,1152]{1,0:T(8,128)(2,1)} %get-tuple-element.174.refs_5_) | copy-start | bytes 7962628 | tf_op jit(solution)/shard_map/cond
  88.3 45.5 %copy-start.5 = (f32[256,256]{1,0:T(8,128)S(1)}, f32[256,256]{1,0:T(8,128)}, u32[]{:S(2)}) copy-start(f32[256,256]{1,0:T(8,128)} %get-tuple-element.173.refs_4_) | copy-start | bytes 786436 | tf_op jit(solution)/shard_map/cond
  158.5 4.6 %copy-start.4 = (f32[256,256]{1,0:T(8,128)S(1)}, f32[256,256]{1,0:T(8,128)}, u32[]{:S(2)}) copy-start(f32[256,256]{1,0:T(8,128)} %copy-done.3) | copy-start | bytes 786436
  158.6 58.0 %collective-permute-start.3 = (bf16[128,1152]{1,0:T(8,128)(2,1)S(1)}, bf16[128,1152]{1,0:T(8,128)(2,1)S(1)}, u32[]{:S(2)}, u32[]{:S(2)}) collective-permute-start(bf16[128,1152]{1,0:T(8,128)(2,1)S(1)} %bitcast.53), channel_id=1, source_target_pairs={{0,16},{1,17},{2,18},{3,19},{4,20},{5,21},{6,22},{7,23},{8,24},{9,... | collective-permute-start | bytes 884744 | tf_op jit(solution)/shard_map/ppermute | solution.py:199
  162.5 54.1 %collective-permute-start.4 = (bf16[128,1152]{1,0:T(8,128)(2,1)S(1)}, bf16[128,1152]{1,0:T(8,128)(2,1)S(1)}, u32[]{:S(2)}, u32[]{:S(2)}) collective-permute-start(bf16[128,1152]{1,0:T(8,128)(2,1)S(1)} %bitcast.52), channel_id=1, source_target_pairs={{0,24},{1,25},{2,26},{3,27},{4,28},{5,29},{6,30},{7,31},{8,16},{9,... | collective-permute-start | bytes 884744 | tf_op jit(solution)/shard_map/ppermute | solution.py:199
  162.9 53.7 %collective-permute-start.5 = (bf16[128,1152]{1,0:T(8,128)(2,1)S(1)}, bf16[128,1152]{1,0:T(8,128)(2,1)S(1)}, u32[]{:S(2)}, u32[]{:S(2)}) collective-permute-start(bf16[128,1152]{1,0:T(8,128)(2,1)S(1)} %bitcast.51), channel_id=1, source_target_pairs={{0,8},{1,9},{2,10},{3,11},{4,12},{5,13},{6,14},{7,15},{8,0},{9,1},... | collective-permute-start | bytes 884744 | tf_op jit(solution)/shard_map/ppermute | solution.py:199
  217.2 1.4 copy-start.6

commit v5 on v4

--- a/solution.py
+++ b/solution.py
@@ -12,7 +12,7 @@
 LANES = 128
 SUB = 8
 HI = 4
-NEAR = (0, 2, 3, 1)
+NEAR = (0, 3, 2, 1)
 AXES = ("tm", "pix")
 
 
@@ -234,7 +234,7 @@
         return mover(split, [across(packed)], [piece] * HI, HI, high), cut((0,))(*flat), bias
 
     second, own, bias = region(start_second, *flat)
-    late = NEAR.index(3)
+    late = NEAR.index(2)
     slots = [s for s in range(HI) if s != late]
 
     def each(z, ins, stages):

time: 219 us -> 215 us (0.982)
  waiting for transfers between devices: 40.5 us -> 58.4 us
  starting transfers between devices: 35.6 us -> 19.1 us
  blocking collectives: 111 us -> 105 us
    ppermute x9, waiting for transfers between devices: 0.58 us -> 18.5 us  [along(): return lax.ppermute(a, ('pix', 'tm'), pairs)]
    ppermute x9, starting transfers between devices: 31.1 us -> 14.6 us  [along(): return lax.ppermute(a, ('pix', 'tm'), pairs)]
    all_to_all x1, blocking collectives: 46.3 us -> 41.1 us  [finish_second(): lax.all_to_all(out.reshape(frames, tall, feats), AXES, split_axis=0, conc...]
  transfers between devices with their start and end apart: 10 -> 10, of which waited for: 2 -> 2; matrix products, arithmetic and copies ran while one was open for 0% -> 1% of each run, Pallas kernels for 11% -> 11%
where the time goes in v5:
time: 215 us
  blocking collectives  105 us (49%)
  waiting for transfers between devices  58.4 us (27%)
  Pallas kernels  26.8 us (12%)
  starting transfers between devices  19.1 us (9%)
  local copies, waits for them, and re-layouts  3.71 us (2%)
    all_to_all x2, blocking collectives, across(): lax.all_to_all(a, AXES, split_axis=0, concat_axis=0, tiled=True, axis_ind...  64.3 us
    all_to_all x1, blocking collectives, finish_second(): lax.all_to_all(out.reshape(frames, tall, feats), AXES, split_axis=0, conc...  41.1 us
    all_to_all x1, waiting for transfers between devices, across(): lax.all_to_all(a, AXES, split_axis=0, concat_axis=0, tiled=True, axis_ind...  39.9 us
    ppermute x9, waiting for transfers between devices, along(): return lax.ppermute(a, ('pix', 'tm'), pairs)  18.5 us
    ppermute x9, starting transfers between devices, along(): return lax.ppermute(a, ('pix', 'tm'), pairs)  14.6 us
    pallas_call x6, Pallas kernels, mover(): pl.pallas_call(kernel, grid_spec=pltpu.PrefetchScalarGridSpec(num_scalar_...  13.9 us
    pallas_call x2, Pallas kernels, attend(): pl.pallas_call(functools.partial(attend_kernel, outer is not None), grid_...  12.9 us
    all_to_all x1, starting transfers between devices, across(): lax.all_to_all(a, AXES, split_axis=0, concat_axis=0, tiled=True, axis_ind...  4.51 us
  transfers between devices with their start and end apart: 10, of which 2 were waited for; matrix products, arithmetic and copies ran while one was open for 1% of the time, Pallas kernels for 11%

profile of v5, /device:TPU:0, one launch (start us, length us, event | category | flops | bytes accessed | tf_op | source)
XLA Modules:
  0.0 214.7 jit_solution(15200297747522396422)
XLA Ops:
  0.0 2.9 %shard_map.55 = (bf16[8,3,16,1152]{3,2,1,0:T(8,128)(2,1)}, bf16[8,3,16,1152]{3,2,1,0:T(8,128)(2,1)}, bf16[8,3,16,1152]{3,2,1,0:T(8,128)(2,1)}) custom-call(s32[1]{0:T(128)} %bitcast.14.z_ref, bf16[64,16,1152]{2,1,0:T(8,128)(2,1)} %bitcast.39, bf16[64,16,1152]{2,1,0:T(8,128)(2,1)} %bitcast.42, bf16[64,16,1152]{2,1,0:T(8,128)(2,1)} %bitcast.45), custom_call_target="tpu_custom_call" | custom-call | tf_op jit(solution)/shard_map/pallas_call | solution.py:41
  2.9 5.1 %collective-permute-start = (bf16[8,3,16,1152]{3,2,1,0:T(8,128)(2,1)}, bf16[8,3,16,1152]{3,2,1,0:T(8,128)(2,1)}, u32[]{:S(2)}, u32[]{:S(2)}) collective-permute-start(bf16[8,3,16,1152]{3,2,1,0:T(8,128)(2,1)} %get-tuple-element.221), channel_id=1, source_target_pairs={{0,24},{1,25},{2,26},{3,27},{4,28},{5,29},{6,30},{7,31},{8,16},{9,... | collective-permute-start | bytes 2654216 | tf_op jit(solution)/shard_map/ppermute | solution.py:199
  8.0 0.0 collective-permute-start.1
  8.0 0.6 collective-permute-start.2
  8.7 0.0 copy-done.7
  8.7 0.6 slice.15
  10.0 52.8 %conditional.3 = (bf16[8,3,16,1152]{3,2,1,0:T(8,128)(2,1)}, bf16[8,3,16,1152]{3,2,1,0:T(8,128)(2,1)}, bf16[8,3,16,1152]{3,2,1,0:T(8,128)(2,1)}, bf16[8,3,16,1152...) conditional(s32[]{:T(128)} %bitcast.13, () %tuple.38, (s32[]{:T(128)}, ...), branch_computations={%region_0.1_spmd, %region_1.2_spmd} | conditional | flops 1365312 | bytes 10893916 | solution.py:195
  10.1 3.6 %branch_1_fun.5 = bf16[4,2,4,3,16,1152]{5,4,3,2,1,0:T(8,128)(2,1)} custom-call(s32[1]{0:T(128)} %bitcast.z_ref, bf16[2,4,4,2,16,1152]{5,4,3,2,1,0:T(8,128)(2,1)S(1)} %bitcast.41, bf16[2,4,4,2,16,1152]{5,4,3,2,1,0:T(8,128)(2,1)} %bitcast.44, bf16[2,4,4,2,16,1152]{5,4,3,2,1,0:T(8,128)(2,1)} %bitcast.47), custom_call_target="tpu_custom_call" | custom-call | tf_op jit(solution)/shard_map/cond/branch_1_fun/pallas_call | solution.py:41
  13.6 4.5 %all-to-all-start.3 = ((bf16[8,4,3,16,1152]{4,3,2,1,0:T(8,128)(2,1)}), bf16[8,4,3,16,1152]{4,3,2,1,0:T(8,128)(2,1)}, u32[]{:S(2)}, u32[]{:S(2)}) async-start(bf16[8,4,3,16,1152]{4,3,2,1,0:T(8,128)(2,1)} %bitcast.48), calls=%async_computation.3 | async-start | bytes 7077888 | tf_op jit(solution)/shard_map/cond/branch_1_fun/all_to_all | solution.py:202
  18.1 1.3 branch_1_fun.7
  19.5 0.4 fusion.5
  19.8 39.9 %all-to-all-done.3.refs_0_ = bf16[8,4,3,16,1152]{4,3,2,1,0:T(8,128)(2,1)} async-done(((bf16[8,4,3,16,1152]{4,3,2,1,0:T(8,128)(2,1)}), bf16[8,4,3,16,1152]{4,3,2,1,0:T(8,128)(2,1)}, u32[]{:S(2)}, u32[]{:S(2)}) %all-to-all-start.3) | async-done | bytes 3538976 | tf_op jit(solution)/shard_map/cond/branch_1_fun/all_to_all | solution.py:202
  59.8 3.0 %branch_1_fun.6 = (bf16[8,3,16,1152]{3,2,1,0:T(8,128)(2,1)}, bf16[8,3,16,1152]{3,2,1,0:T(8,128)(2,1)}, bf16[8,3,16,1152]{3,2,1,0:T(8,128)(2,1)}, bf16[8,3,16,1152]{3,2,1,0:T(8,128)(2,1)}) custom-call(s32[1]{0:T(128)} %bitcast.z_ref, bf16[8,4,3,16,1152]{4,3,2,1,0:T(8,128)(2,1)} %all-to-all-done.3.refs_0_), custom_call_target="tpu_custom_call" | custom-call | tf_op jit(solution)/shard_map/cond/branch_1_fun/pallas_call | solution.py:41
  62.8 0.0 copy-start.2
  62.8 0.0 copy-start.3
  62.8 0.0 collective-permute-done.refs_1_
  62.8 0.0 collective-permute-done.1.refs_2_
  62.8 0.9 copy-done.2
  63.7 0.1 copy-done.3
  63.8 1.8 shard_map.56.refs_1_
  65.7 18.4 %collective-permute-done.2.refs_0_ = bf16[8,3,16,1152]{3,2,1,0:T(8,128)(2,1)} collective-permute-done((bf16[8,3,16,1152]{3,2,1,0:T(8,128)(2,1)}, bf16[8,3,16,1152]{3,2,1,0:T(8,128)(2,1)}, u32[]{:S(2)}, u32[]{:S(2)}) %collective-permute-start.2) | collective-permute-done | bytes 884768 | tf_op jit(solution)/shard_map/ppermute | solution.py:199
  84.1 2.5 %collective-permute-start.6 = (bf16[8,3,16,1152]{3,2,1,0:T(8,128)(2,1)}, bf16[8,3,16,1152]{3,2,1,0:T(8,128)(2,1)}, u32[]{:S(2)}, u32[]{:S(2)}) collective-permute-start(bf16[8,3,16,1152]{3,2,1,0:T(8,128)(2,1)} %get-tuple-element.230), channel_id=1, source_target_pairs={{0,24},{1,25},{2,26},{3,27},{4,28},{5,29},{6,30},{7,31},{8,16},{9,... | collective-permute-start | bytes 2654216 | tf_op jit(solution)/shard_map/ppermute | solution.py:199
  86.5 0.0 collective-permute-start.7
  86.5 1.9 collective-permute-start.8
  88.5 1.2 shard_map.57
  89.7 70.2 %conditional.4 = (bf16[8,4,2,8,1152]{4,3,2,1,0:T(8,128)(2,1)S(1)}) conditional(s32[]{:T(128)} %bitcast.13, () %tuple.42, (s32[]{:T(128)}, bf16[8,4,3,16,1152]{4,3,2,1,0:T(8,128)(2,1)S(1)}, f32[256,256]{1,0:T(8,128)}, bf16[1152,1152]{1,0:T(8,128)(2,1)}) %tuple.63), branch_computations={%region_2.3_spmd, %region_3.4_spmd} | conditional | bytes 21102656 | solution.py:195
  89.8 0.0 copy-start.1
  89.8 0.0 copy-start.5
  89.8 45.5 %all_to_all.16 = bf16[8,4,3,16,1152]{4,3,2,1,0:T(8,128)(2,1)S(1)} all-to-all(bf16[8,4,3,16,1152]{4,3,2,1,0:T(8,128)(2,1)S(1)} %get-tuple-element.172), channel_id=1, replica_groups={{0,4,1,5,2,6,3,7},{8,12,9,13,10,14,11,15},{16,20,17,21,18,22,19,23},{24..., dimensions={0} | all-to-all | bytes 7077888 | tf_op jit(solution)/shard_map/cond/branch_1_fun/all_to_all | solution.py:202
  135.3 5.8 %branch_1_fun.8 = bf16[8,4,2,8,1152]{4,3,2,1,0:T(8,128)(2,1)S(1)} custom-call(s32[1]{0:T(128)} %bitcast.5.z_ref, bf16[8,4,3,2,8,1152]{5,4,3,2,1,0:T(8,128)(2,1)S(1)} %bitcast.34, bf16[8,4,3,2,8,1152]{5,4,3,2,1,0:T(8,128)(2,1)S(1)} %bitcast.35, bf16[8,4,3,2,8,1152]{5,4,3,2,1,0:T(8,128)(2,1)S(1)} %bitcast.36, bf16[8,4,3,2,8,1152]{5,4,3,2,1,0:T(8,128)(2,1)S(1)} %bitcast.37, ...), custom_call_target="tpu_custom_call" | custom-call | tf_op jit(solution)/shard_map/cond/branch_1_fun/pallas_call | solution.py:124
  141.1 18.8 %all_to_all.17 = bf16[8,4,2,8,1152]{4,3,2,1,0:T(8,128)(2,1)S(1)} all-to-all(bf16[8,4,2,8,1152]{4,3,2,1,0:T(8,128)(2,1)S(1)} %branch_1_fun.8), channel_id=1, replica_groups={{0,4,1,5,2,6,3,7},{8,12,9,13,10,14,11,15},{16,20,17,21,18,22,19,23},{24..., dimensions={0} | all-to-all | bytes 2359296 | tf_op jit(solution)/shard_map/cond/branch_1_fun/all_to_all | solution.py:202
  159.9 0.1 fusion.21
  160.0 2.5 %collective-permute-start.3 = (bf16[128,1152]{1,0:T(8,128)(2,1)S(1)}, bf16[128,1152]{1,0:T(8,128)(2,1)S(1)}, u32[]{:S(2)}, u32[]{:S(2)}) collective-permute-start(bf16[128,1152]{1,0:T(8,128)(2,1)S(1)} %bitcast.53), channel_id=1, source_target_pairs={{0,24},{1,25},{2,26},{3,27},{4,28},{5,29},{6,30},{7,31},{8,16},{9,... | collective-permute-start | bytes 884744 | tf_op jit(solution)/shard_map/ppermute | solution.py:199
  162.5 0.0 collective-permute-start.4
  162.5 0.0 collective-permute-done.6
  162.5 1.9 collective-permute-start.5
  164.5 0.0 collective-permute-done.7
  164.5 0.0 collective-permute-done.8
  164.5 48.2 %conditional.5 = (bf16[32,16,1152]{2,1,0:T(8,128)(2,1)S(1)}) conditional(s32[]{:T(128)} %bitcast.13, () %tuple.45, (s32[]{:T(128)}, bf16[8,3,16,1152]{3,2,1,0:T(8,128)(2,1)}, bf16[8,3,16,1152]{3,2,1,0:T(8,128)(2,1)}, bf16[8,3,16,1152]{3,2,1,0:T(8,128)(2,1)}, bf16[8,3,16,1152]{3,2,1,0:T(8,128)(2,1)}, /*index=5*/f32[256,256]{1,0:T(8,128)S(1)}, ...), branch_computations={%region_4.5_spmd, %region_5.6_spmd} | conditional | bytes 2359304 | solution.py:195
  164.5 7.1 %branch_1_fun.9 = bf16[4,4,2,2,8,1152]{5,4,3,2,1,0:T(8,128)(2,1)S(1)} custom-call(s32[1]{0:T(128)} %bitcast.7.z_ref, bf16[8,1,3,2,8,1152]{5,4,3,2,1,0:T(8,128)(2,1)} %bitcast.8.refs_0_, bf16[8,1,3,2,8,1152]{5,4,3,2,1,0:T(8,128)(2,1)} %bitcast.9.refs_1_, bf16[8,1,3,2,8,1152]{5,4,3,2,1,0:T(8,128)(2,1)} %bitcast.10.refs_2_, ...), custom_call_target="tpu_custom_call" | custom-call | tf_op jit(solution)/shard_map/cond/branch_1_fun/pallas_call | solution.py:124
  171.6 41.1 %all_to_all.18 = bf16[32,16,1152]{2,1,0:T(8,128)(2,1)S(1)} all-to-all(bf16[32,16,1152]{2,1,0:T(8,128)(2,1)S(1)} %bitcast.38), channel_id=1, replica_groups=mesh['pix'=8,'tm'=4] {'tm','pix'}, dimensions={0} | all-to-all | bytes 2359296 | tf_op jit(solution)/shard_map/cond/branch_1_fun/all_to_all | solution.py:259
  212.7 0.0 collective-permute-done.3
  212.7 0.0 collective-permute-done.4
  212.7 0.0 collective-permute-done.5
  212.7 0.3 broadcast_in_dim.38
  213.2 0.2 bitcast_dynamic-update-slice_fusion
  213.3 0.0 copy-start.6
  213.4 1.4 copy-done.6
  (19 shorter events, 0.2 us)
Async XLA Ops:
  0.0 8.7 %copy-start.7 = (s32[8,8]{1,0:T(8,128)S(1)}, s32[8,8]{1,0:T(8,128)}, u32[]{:S(2)}) copy-start(s32[8,8]{1,0:T(8,128)} %param.14) | copy-start | bytes 772
  0.0 10.0 %copy-start = (bf16[1,1,1024,1152]{3,2,1,0:T(8,128)(2,1)S(1)}, bf16[1,1,1024,1152]{3,2,1,0:T(8,128)(2,1)}, u32[]{:S(2)}) copy-start(bf16[1,1,1024,1152]{3,2,1,0:T(8,128)(2,1)} %param.11) | copy-start | bytes 7077892
  2.9 59.9 %collective-permute-start = (bf16[8,3,16,1152]{3,2,1,0:T(8,128)(2,1)}, bf16[8,3,16,1152]{3,2,1,0:T(8,128)(2,1)}, u32[]{:S(2)}, u32[]{:S(2)}) collective-permute-start(bf16[8,3,16,1152]{3,2,1,0:T(8,128)(2,1)} %get-tuple-element.221), channel_id=1, source_target_pairs={{0,24},{1,25},{2,26},{3,27},{4,28},{5,29},{6,30},{7,31},{8,16},{9,... | collective-permute-start | bytes 2654216 | tf_op jit(solution)/shard_map/ppermute | solution.py:199
  8.0 54.8 %collective-permute-start.1 = (bf16[8,3,16,1152]{3,2,1,0:T(8,128)(2,1)}, bf16[8,3,16,1152]{3,2,1,0:T(8,128)(2,1)}, u32[]{:S(2)}, u32[]{:S(2)}) collective-permute-start(bf16[8,3,16,1152]{3,2,1,0:T(8,128)(2,1)} %get-tuple-element.222), channel_id=1, source_target_pairs={{0,8},{1,9},{2,10},{3,11},{4,12},{5,13},{6,14},{7,15},{8,0},{9,1},... | collective-permute-start | bytes 2654216 | tf_op jit(solution)/shard_map/ppermute | solution.py:199
  8.0 76.1 %collective-permute-start.2 = (bf16[8,3,16,1152]{3,2,1,0:T(8,128)(2,1)}, bf16[8,3,16,1152]{3,2,1,0:T(8,128)(2,1)}, u32[]{:S(2)}, u32[]{:S(2)}) collective-permute-start(bf16[8,3,16,1152]{3,2,1,0:T(8,128)(2,1)} %get-tuple-element.223), channel_id=1, source_target_pairs={{0,16},{1,17},{2,18},{3,19},{4,20},{5,21},{6,22},{7,23},{8,24},{9,... | collective-permute-start | bytes 2654216 | tf_op jit(solution)/shard_map/ppermute | solution.py:199
  13.6 46.1 %all-to-all-start.3 = ((bf16[8,4,3,16,1152]{4,3,2,1,0:T(8,128)(2,1)}), bf16[8,4,3,16,1152]{4,3,2,1,0:T(8,128)(2,1)}, u32[]{:S(2)}, u32[]{:S(2)}) async-start(bf16[8,4,3,16,1152]{4,3,2,1,0:T(8,128)(2,1)} %bitcast.48), calls=%async_computation.3 | async-start | bytes 7077888 | tf_op jit(solution)/shard_map/cond/branch_1_fun/all_to_all | solution.py:202
  62.8 0.9 copy-start.2
  62.8 1.0 copy-start.3
  84.1 78.4 %collective-permute-start.6 = (bf16[8,3,16,1152]{3,2,1,0:T(8,128)(2,1)}, bf16[8,3,16,1152]{3,2,1,0:T(8,128)(2,1)}, u32[]{:S(2)}, u32[]{:S(2)}) collective-permute-start(bf16[8,3,16,1152]{3,2,1,0:T(8,128)(2,1)} %get-tuple-element.230), channel_id=1, source_target_pairs={{0,24},{1,25},{2,26},{3,27},{4,28},{5,29},{6,30},{7,31},{8,16},{9,... | collective-permute-start | bytes 2654216 | tf_op jit(solution)/shard_map/ppermute | solution.py:199
  86.5 77.9 %collective-permute-start.7 = (bf16[8,3,16,1152]{3,2,1,0:T(8,128)(2,1)}, bf16[8,3,16,1152]{3,2,1,0:T(8,128)(2,1)}, u32[]{:S(2)}, u32[]{:S(2)}) collective-permute-start(bf16[8,3,16,1152]{3,2,1,0:T(8,128)(2,1)} %get-tuple-element.231), channel_id=1, source_target_pairs={{0,16},{1,17},{2,18},{3,19},{4,20},{5,21},{6,22},{7,23},{8,24},{9,... | collective-permute-start | bytes 2654216 | tf_op jit(solution)/shard_map/ppermute | solution.py:199
  86.5 77.9 %collective-permute-start.8 = (bf16[8,3,16,1152]{3,2,1,0:T(8,128)(2,1)}, bf16[8,3,16,1152]{3,2,1,0:T(8,128)(2,1)}, u32[]{:S(2)}, u32[]{:S(2)}) collective-permute-start(bf16[8,3,16,1152]{3,2,1,0:T(8,128)(2,1)} %get-tuple-element.232), channel_id=1, source_target_pairs={{0,8},{1,9},{2,10},{3,11},{4,12},{5,13},{6,14},{7,15},{8,0},{9,1},... | collective-permute-start | bytes 2654216 | tf_op jit(solution)/shard_map/ppermute | solution.py:199
  89.8 45.5 %copy-start.1 = (bf16[1152,1152]{1,0:T(8,128)(2,1)S(1)}, bf16[1152,1152]{1,0:T(8,128)(2,1)}, u32[]{:S(2)}) copy-start(bf16[1152,1152]{1,0:T(8,128)(2,1)} %get-tuple-element.174.refs_5_) | copy-start | bytes 7962628 | tf_op jit(solution)/shard_map/cond
  89.8 45.5 %copy-start.5 = (f32[256,256]{1,0:T(8,128)S(1)}, f32[256,256]{1,0:T(8,128)}, u32[]{:S(2)}) copy-start(f32[256,256]{1,0:T(8,128)} %get-tuple-element.173.refs_4_) | copy-start | bytes 786436 | tf_op jit(solution)/shard_map/cond
  159.9 4.6 %copy-start.4 = (f32[256,256]{1,0:T(8,128)S(1)}, f32[256,256]{1,0:T(8,128)}, u32[]{:S(2)}) copy-start(f32[256,256]{1,0:T(8,128)} %copy-done.3) | copy-start | bytes 786436
  160.0 52.7 %collective-permute-start.3 = (bf16[128,1152]{1,0:T(8,128)(2,1)S(1)}, bf16[128,1152]{1,0:T(8,128)(2,1)S(1)}, u32[]{:S(2)}, u32[]{:S(2)}) collective-permute-start(bf16[128,1152]{1,0:T(8,128)(2,1)S(1)} %bitcast.53), channel_id=1, source_target_pairs={{0,24},{1,25},{2,26},{3,27},{4,28},{5,29},{6,30},{7,31},{8,16},{9,... | collective-permute-start | bytes 884744 | tf_op jit(solution)/shard_map/ppermute | solution.py:199
  162.5 50.2 %collective-permute-start.4 = (bf16[128,1152]{1,0:T(8,128)(2,1)S(1)}, bf16[128,1152]{1,0:T(8,128)(2,1)S(1)}, u32[]{:S(2)}, u32[]{:S(2)}) collective-permute-start(bf16[128,1152]{1,0:T(8,128)(2,1)S(1)} %bitcast.52), channel_id=1, source_target_pairs={{0,16},{1,17},{2,18},{3,19},{4,20},{5,21},{6,22},{7,23},{8,24},{9,... | collective-permute-start | bytes 884744 | tf_op jit(solution)/shard_map/ppermute | solution.py:199
  162.5 50.2 %collective-permute-start.5 = (bf16[128,1152]{1,0:T(8,128)(2,1)S(1)}, bf16[128,1152]{1,0:T(8,128)(2,1)S(1)}, u32[]{:S(2)}, u32[]{:S(2)}) collective-permute-start(bf16[128,1152]{1,0:T(8,128)(2,1)S(1)} %bitcast.51), channel_id=1, source_target_pairs={{0,8},{1,9},{2,10},{3,11},{4,12},{5,13},{6,14},{7,15},{8,0},{9,1},... | collective-permute-start | bytes 884744 | tf_op jit(solution)/shard_map/ppermute | solution.py:199
  213.3 1.4 copy-start.6

commit v6 on v5

--- a/solution.py
+++ b/solution.py
@@ -263,14 +263,14 @@
         return [pieces[0], *[along(a, k) for a, k in zip(pieces[1:], NEAR[1:])]]
 
     done_first = region(finish_first, packed, bias, w_out)
-    second[0], done_first = tie((second[0], done_first))
+    second, done_first = tie((second, done_first))
     back_first = give_back(done_first)
     done_second = region(finish_second, second, bias, w_out)
     back_first, done_second = tie((back_first, done_second))
-    result = jnp.zeros((2 * HI, plane * tall, feats), jnp.bfloat16)
-    for k, piece in zip(NEAR, back_first):
-        result = lax.dynamic_update_index_in_dim(result, piece, high ^ k, 0)
-    result = lax.dynamic_update_slice(result, done_second.reshape(HI, plane * tall, feats), (HI, 0, 0))
+    upper = jnp.zeros((HI, plane * tall, feats), jnp.bfloat16)
+    for k, back in zip(NEAR, back_first):
+        upper = lax.dynamic_update_index_in_dim(upper, back, high ^ k, 0)
+    result = jnp.concatenate([upper, done_second.reshape(HI, plane * tall, feats)], axis=0)
     return result.reshape(query.shape)
 
 

time: 215 us -> 215 us (level)
  transfers between devices with their start and end apart: 10 -> 10, of which waited for: 2 -> 3; matrix products, arithmetic and copies ran while one was open for 1% -> 0% of each run, Pallas kernels for 11% -> 11%
where the time goes in v6:
time: 215 us
  blocking collectives  104 us (48%)
  waiting for transfers between devices  59.5 us (28%)
  Pallas kernels  26.8 us (12%)
  starting transfers between devices  19.1 us (9%)
    all_to_all x2, blocking collectives, across(): lax.all_to_all(a, AXES, split_axis=0, concat_axis=0, tiled=True, axis_ind...  64.3 us
    all_to_all x1, blocking collectives, finish_second(): lax.all_to_all(out.reshape(frames, tall, feats), AXES, split_axis=0, conc...  40.1 us
    all_to_all x1, waiting for transfers between devices, across(): lax.all_to_all(a, AXES, split_axis=0, concat_axis=0, tiled=True, axis_ind...  39.9 us
    ppermute x9, waiting for transfers between devices, along(): return lax.ppermute(a, ('pix', 'tm'), pairs)  19.6 us
    ppermute x9, starting transfers between devices, along(): return lax.ppermute(a, ('pix', 'tm'), pairs)  14.6 us
    pallas_call x6, Pallas kernels, mover(): pl.pallas_call(kernel, grid_spec=pltpu.PrefetchScalarGridSpec(num_scalar_...  13.9 us
    pallas_call x2, Pallas kernels, attend(): pl.pallas_call(functools.partial(attend_kernel, outer is not None), grid_...  12.9 us
    all_to_all x1, starting transfers between devices, across(): lax.all_to_all(a, AXES, split_axis=0, concat_axis=0, tiled=True, axis_ind...  4.51 us
  transfers between devices with their start and end apart: 10, of which 3 were waited for; matrix products, arithmetic and copies ran while one was open for 0% of the time, Pallas kernels for 11%

profile of v6, /device:TPU:0, one launch (start us, length us, event | category | flops | bytes accessed | tf_op | source)
XLA Modules:
  0.0 214.7 jit_solution(17519816573591094184)
XLA Ops:
  0.0 3.0 %shard_map.55 = (bf16[8,3,16,1152]{3,2,1,0:T(8,128)(2,1)}, bf16[8,3,16,1152]{3,2,1,0:T(8,128)(2,1)}, bf16[8,3,16,1152]{3,2,1,0:T(8,128)(2,1)}) custom-call(s32[1]{0:T(128)} %bitcast.14.z_ref, bf16[64,16,1152]{2,1,0:T(8,128)(2,1)} %bitcast.37, bf16[64,16,1152]{2,1,0:T(8,128)(2,1)} %bitcast.40, bf16[64,16,1152]{2,1,0:T(8,128)(2,1)} %bitcast.43), custom_call_target="tpu_custom_call" | custom-call | tf_op jit(solution)/shard_map/pallas_call | solution.py:41
  3.0 5.1 %collective-permute-start = (bf16[8,3,16,1152]{3,2,1,0:T(8,128)(2,1)}, bf16[8,3,16,1152]{3,2,1,0:T(8,128)(2,1)}, u32[]{:S(2)}, u32[]{:S(2)}) collective-permute-start(bf16[8,3,16,1152]{3,2,1,0:T(8,128)(2,1)} %get-tuple-element.224), channel_id=1, source_target_pairs={{0,24},{1,25},{2,26},{3,27},{4,28},{5,29},{6,30},{7,31},{8,16},{9,... | collective-permute-start | bytes 2654216 | tf_op jit(solution)/shard_map/ppermute | solution.py:199
  8.1 0.0 collective-permute-start.1
  8.1 0.6 collective-permute-start.2
  8.7 0.0 copy-done.6
  8.8 0.5 slice.15
  10.0 0.0 copy-done
  10.0 52.7 %conditional.3 = (bf16[8,3,16,1152]{3,2,1,0:T(8,128)(2,1)}, bf16[8,3,16,1152]{3,2,1,0:T(8,128)(2,1)}, bf16[8,3,16,1152]{3,2,1,0:T(8,128)(2,1)}, bf16[8,3,16,1152...) conditional(s32[]{:T(128)} %bitcast.13, () %tuple.38, (s32[]{:T(128)}, ...), branch_computations={%region_0.1_spmd, %region_1.2_spmd} | conditional | flops 1365312 | bytes 10893916 | solution.py:195
  10.0 3.5 %branch_1_fun.5 = bf16[4,2,4,3,16,1152]{5,4,3,2,1,0:T(8,128)(2,1)} custom-call(s32[1]{0:T(128)} %bitcast.z_ref, bf16[2,4,4,2,16,1152]{5,4,3,2,1,0:T(8,128)(2,1)S(1)} %bitcast.39, bf16[2,4,4,2,16,1152]{5,4,3,2,1,0:T(8,128)(2,1)} %bitcast.42, bf16[2,4,4,2,16,1152]{5,4,3,2,1,0:T(8,128)(2,1)} %bitcast.45), custom_call_target="tpu_custom_call" | custom-call | tf_op jit(solution)/shard_map/cond/branch_1_fun/pallas_call | solution.py:41
  13.6 4.5 %all-to-all-start.3 = ((bf16[8,4,3,16,1152]{4,3,2,1,0:T(8,128)(2,1)}), bf16[8,4,3,16,1152]{4,3,2,1,0:T(8,128)(2,1)}, u32[]{:S(2)}, u32[]{:S(2)}) async-start(bf16[8,4,3,16,1152]{4,3,2,1,0:T(8,128)(2,1)} %bitcast.46), calls=%async_computation.3 | async-start | bytes 7077888 | tf_op jit(solution)/shard_map/cond/branch_1_fun/all_to_all | solution.py:202
  18.1 1.3 branch_1_fun.7
  19.4 0.4 fusion.5
  19.8 39.9 %all-to-all-done.3.refs_0_ = bf16[8,4,3,16,1152]{4,3,2,1,0:T(8,128)(2,1)} async-done(((bf16[8,4,3,16,1152]{4,3,2,1,0:T(8,128)(2,1)}), bf16[8,4,3,16,1152]{4,3,2,1,0:T(8,128)(2,1)}, u32[]{:S(2)}, u32[]{:S(2)}) %all-to-all-start.3) | async-done | bytes 3538976 | tf_op jit(solution)/shard_map/cond/branch_1_fun/all_to_all | solution.py:202
  59.7 3.0 %branch_1_fun.6 = (bf16[8,3,16,1152]{3,2,1,0:T(8,128)(2,1)}, bf16[8,3,16,1152]{3,2,1,0:T(8,128)(2,1)}, bf16[8,3,16,1152]{3,2,1,0:T(8,128)(2,1)}, bf16[8,3,16,1152]{3,2,1,0:T(8,128)(2,1)}) custom-call(s32[1]{0:T(128)} %bitcast.z_ref, bf16[8,4,3,16,1152]{4,3,2,1,0:T(8,128)(2,1)} %all-to-all-done.3.refs_0_), custom_call_target="tpu_custom_call" | custom-call | tf_op jit(solution)/shard_map/cond/branch_1_fun/pallas_call | solution.py:41
  62.7 0.0 copy-start.2
  62.8 0.0 copy-start.3
  62.8 0.0 collective-permute-done.refs_1_
  62.8 0.0 collective-permute-done.1.refs_2_
  62.8 0.9 copy-done.2
  63.7 0.1 copy-done.3
  63.8 1.8 shard_map.56.refs_1_
  65.6 18.5 %collective-permute-done.2.refs_0_ = bf16[8,3,16,1152]{3,2,1,0:T(8,128)(2,1)} collective-permute-done((bf16[8,3,16,1152]{3,2,1,0:T(8,128)(2,1)}, bf16[8,3,16,1152]{3,2,1,0:T(8,128)(2,1)}, u32[]{:S(2)}, u32[]{:S(2)}) %collective-permute-start.2) | collective-permute-done | bytes 884768 | tf_op jit(solution)/shard_map/ppermute | solution.py:199
  84.1 2.5 %collective-permute-start.3 = (bf16[8,3,16,1152]{3,2,1,0:T(8,128)(2,1)}, bf16[8,3,16,1152]{3,2,1,0:T(8,128)(2,1)}, u32[]{:S(2)}, u32[]{:S(2)}) collective-permute-start(bf16[8,3,16,1152]{3,2,1,0:T(8,128)(2,1)} %get-tuple-element.228), channel_id=1, source_target_pairs={{0,24},{1,25},{2,26},{3,27},{4,28},{5,29},{6,30},{7,31},{8,16},{9,... | collective-permute-start | bytes 2654216 | tf_op jit(solution)/shard_map/ppermute | solution.py:199
  86.6 0.0 collective-permute-start.4
  86.6 1.9 collective-permute-start.5
  88.5 1.2 shard_map.57
  89.7 70.2 %conditional.4 = (bf16[8,4,2,8,1152]{4,3,2,1,0:T(8,128)(2,1)S(1)}) conditional(s32[]{:T(128)} %bitcast.13, () %tuple.42, (s32[]{:T(128)}, bf16[8,4,3,16,1152]{4,3,2,1,0:T(8,128)(2,1)S(1)}, f32[256,256]{1,0:T(8,128)}, bf16[1152,1152]{1,0:T(8,128)(2,1)}) %tuple.63), branch_computations={%region_2.3_spmd, %region_3.4_spmd} | conditional | bytes 21102656 | solution.py:195
  89.8 0.0 copy-start.1
  89.8 0.0 copy-start.5
  89.8 45.5 %all_to_all.16 = bf16[8,4,3,16,1152]{4,3,2,1,0:T(8,128)(2,1)S(1)} all-to-all(bf16[8,4,3,16,1152]{4,3,2,1,0:T(8,128)(2,1)S(1)} %get-tuple-element.172), channel_id=1, replica_groups={{0,4,1,5,2,6,3,7},{8,12,9,13,10,14,11,15},{16,20,17,21,18,22,19,23},{24..., dimensions={0} | all-to-all | bytes 7077888 | tf_op jit(solution)/shard_map/cond/branch_1_fun/all_to_all | solution.py:202
  135.3 0.0 copy-done.5
  135.3 5.8 %branch_1_fun.8 = bf16[8,4,2,8,1152]{4,3,2,1,0:T(8,128)(2,1)S(1)} custom-call(s32[1]{0:T(128)} %bitcast.5.z_ref, bf16[8,4,3,2,8,1152]{5,4,3,2,1,0:T(8,128)(2,1)S(1)} %bitcast.32, bf16[8,4,3,2,8,1152]{5,4,3,2,1,0:T(8,128)(2,1)S(1)} %bitcast.33, bf16[8,4,3,2,8,1152]{5,4,3,2,1,0:T(8,128)(2,1)S(1)} %bitcast.34, bf16[8,4,3,2,8,1152]{5,4,3,2,1,0:T(8,128)(2,1)S(1)} %bitcast.35, ...), custom_call_target="tpu_custom_call" | custom-call | tf_op jit(solution)/shard_map/cond/branch_1_fun/pallas_call | solution.py:124
  141.1 18.8 %all_to_all.17 = bf16[8,4,2,8,1152]{4,3,2,1,0:T(8,128)(2,1)S(1)} all-to-all(bf16[8,4,2,8,1152]{4,3,2,1,0:T(8,128)(2,1)S(1)} %branch_1_fun.8), channel_id=1, replica_groups={{0,4,1,5,2,6,3,7},{8,12,9,13,10,14,11,15},{16,20,17,21,18,22,19,23},{24..., dimensions={0} | all-to-all | bytes 2359296 | tf_op jit(solution)/shard_map/cond/branch_1_fun/all_to_all | solution.py:202
  159.9 0.0 collective-permute-done.3
  159.9 1.0 collective-permute-done.4
  160.9 0.0 collective-permute-done.5
  161.0 0.1 fusion.21
  161.0 1.6 collective-permute-start.6
  162.6 0.0 collective-permute-start.7
  162.6 2.9 %collective-permute-start.8 = (bf16[128,1152]{1,0:T(8,128)(2,1)S(1)}, bf16[128,1152]{1,0:T(8,128)(2,1)S(1)}, u32[]{:S(2)}, u32[]{:S(2)}) collective-permute-start(bf16[128,1152]{1,0:T(8,128)(2,1)S(1)} %bitcast.49), channel_id=1, source_target_pairs={{0,8},{1,9},{2,10},{3,11},{4,12},{5,13},{6,14},{7,15},{8,0},{9,1},... | collective-permute-start | bytes 884744 | tf_op jit(solution)/shard_map/ppermute | solution.py:199
  165.5 47.2 %conditional.5 = (bf16[32,16,1152]{2,1,0:T(8,128)(2,1)S(1)}) conditional(s32[]{:T(128)} %bitcast.13, () %tuple.45, (s32[]{:T(128)}, bf16[8,3,16,1152]{3,2,1,0:T(8,128)(2,1)}, bf16[8,3,16,1152]{3,2,1,0:T(8,128)(2,1)}, bf16[8,3,16,1152]{3,2,1,0:T(8,128)(2,1)}, bf16[8,3,16,1152]{3,2,1,0:T(8,128)(2,1)}, /*index=5*/f32[256,256]{1,0:T(8,128)S(1)}, ...), branch_computations={%region_4.5_spmd, %region_5.6_spmd} | conditional | bytes 2359304 | solution.py:195
  165.5 7.1 %branch_1_fun.9 = bf16[4,4,2,2,8,1152]{5,4,3,2,1,0:T(8,128)(2,1)S(1)} custom-call(s32[1]{0:T(128)} %bitcast.7.z_ref, bf16[8,1,3,2,8,1152]{5,4,3,2,1,0:T(8,128)(2,1)} %bitcast.8.refs_0_, bf16[8,1,3,2,8,1152]{5,4,3,2,1,0:T(8,128)(2,1)} %bitcast.9.refs_1_, bf16[8,1,3,2,8,1152]{5,4,3,2,1,0:T(8,128)(2,1)} %bitcast.10.refs_2_, ...), custom_call_target="tpu_custom_call" | custom-call | tf_op jit(solution)/shard_map/cond/branch_1_fun/pallas_call | solution.py:124
  172.6 40.1 %all_to_all.18 = bf16[32,16,1152]{2,1,0:T(8,128)(2,1)S(1)} all-to-all(bf16[32,16,1152]{2,1,0:T(8,128)(2,1)S(1)} %bitcast.36), channel_id=1, replica_groups=mesh['pix'=8,'tm'=4] {'tm','pix'}, dimensions={0} | all-to-all | bytes 2359296 | tf_op jit(solution)/shard_map/cond/branch_1_fun/all_to_all | solution.py:259
  212.7 0.0 collective-permute-done.6
  212.7 0.0 collective-permute-done.7
  212.7 0.0 collective-permute-done.8
  212.7 0.1 broadcast_in_dim.38
  213.0 1.6 pad_maximum_fusion
  (17 shorter events, 0.2 us)
Async XLA Ops:
  0.0 8.8 %copy-start.6 = (s32[8,8]{1,0:T(8,128)S(1)}, s32[8,8]{1,0:T(8,128)}, u32[]{:S(2)}) copy-start(s32[8,8]{1,0:T(8,128)} %param.14) | copy-start | bytes 772
  0.0 10.0 %copy-start = (bf16[1,1,1024,1152]{3,2,1,0:T(8,128)(2,1)S(1)}, bf16[1,1,1024,1152]{3,2,1,0:T(8,128)(2,1)}, u32[]{:S(2)}) copy-start(bf16[1,1,1024,1152]{3,2,1,0:T(8,128)(2,1)} %param.11) | copy-start | bytes 7077892
  3.0 59.8 %collective-permute-start = (bf16[8,3,16,1152]{3,2,1,0:T(8,128)(2,1)}, bf16[8,3,16,1152]{3,2,1,0:T(8,128)(2,1)}, u32[]{:S(2)}, u32[]{:S(2)}) collective-permute-start(bf16[8,3,16,1152]{3,2,1,0:T(8,128)(2,1)} %get-tuple-element.224), channel_id=1, source_target_pairs={{0,24},{1,25},{2,26},{3,27},{4,28},{5,29},{6,30},{7,31},{8,16},{9,... | collective-permute-start | bytes 2654216 | tf_op jit(solution)/shard_map/ppermute | solution.py:199
  8.1 54.7 %collective-permute-start.1 = (bf16[8,3,16,1152]{3,2,1,0:T(8,128)(2,1)}, bf16[8,3,16,1152]{3,2,1,0:T(8,128)(2,1)}, u32[]{:S(2)}, u32[]{:S(2)}) collective-permute-start(bf16[8,3,16,1152]{3,2,1,0:T(8,128)(2,1)} %get-tuple-element.225), channel_id=1, source_target_pairs={{0,8},{1,9},{2,10},{3,11},{4,12},{5,13},{6,14},{7,15},{8,0},{9,1},... | collective-permute-start | bytes 2654216 | tf_op jit(solution)/shard_map/ppermute | solution.py:199
  8.1 76.0 %collective-permute-start.2 = (bf16[8,3,16,1152]{3,2,1,0:T(8,128)(2,1)}, bf16[8,3,16,1152]{3,2,1,0:T(8,128)(2,1)}, u32[]{:S(2)}, u32[]{:S(2)}) collective-permute-start(bf16[8,3,16,1152]{3,2,1,0:T(8,128)(2,1)} %get-tuple-element.226), channel_id=1, source_target_pairs={{0,16},{1,17},{2,18},{3,19},{4,20},{5,21},{6,22},{7,23},{8,24},{9,... | collective-permute-start | bytes 2654216 | tf_op jit(solution)/shard_map/ppermute | solution.py:199
  13.6 46.1 %all-to-all-start.3 = ((bf16[8,4,3,16,1152]{4,3,2,1,0:T(8,128)(2,1)}), bf16[8,4,3,16,1152]{4,3,2,1,0:T(8,128)(2,1)}, u32[]{:S(2)}, u32[]{:S(2)}) async-start(bf16[8,4,3,16,1152]{4,3,2,1,0:T(8,128)(2,1)} %bitcast.46), calls=%async_computation.3 | async-start | bytes 7077888 | tf_op jit(solution)/shard_map/cond/branch_1_fun/all_to_all | solution.py:202
  62.7 0.9 copy-start.2
  62.8 1.0 copy-start.3
  84.1 75.8 %collective-permute-start.3 = (bf16[8,3,16,1152]{3,2,1,0:T(8,128)(2,1)}, bf16[8,3,16,1152]{3,2,1,0:T(8,128)(2,1)}, u32[]{:S(2)}, u32[]{:S(2)}) collective-permute-start(bf16[8,3,16,1152]{3,2,1,0:T(8,128)(2,1)} %get-tuple-element.228), channel_id=1, source_target_pairs={{0,24},{1,25},{2,26},{3,27},{4,28},{5,29},{6,30},{7,31},{8,16},{9,... | collective-permute-start | bytes 2654216 | tf_op jit(solution)/shard_map/ppermute | solution.py:199
  86.6 74.3 %collective-permute-start.4 = (bf16[8,3,16,1152]{3,2,1,0:T(8,128)(2,1)}, bf16[8,3,16,1152]{3,2,1,0:T(8,128)(2,1)}, u32[]{:S(2)}, u32[]{:S(2)}) collective-permute-start(bf16[8,3,16,1152]{3,2,1,0:T(8,128)(2,1)} %get-tuple-element.229), channel_id=1, source_target_pairs={{0,16},{1,17},{2,18},{3,19},{4,20},{5,21},{6,22},{7,23},{8,24},{9,... | collective-permute-start | bytes 2654216 | tf_op jit(solution)/shard_map/ppermute | solution.py:199
  86.6 74.3 %collective-permute-start.5 = (bf16[8,3,16,1152]{3,2,1,0:T(8,128)(2,1)}, bf16[8,3,16,1152]{3,2,1,0:T(8,128)(2,1)}, u32[]{:S(2)}, u32[]{:S(2)}) collective-permute-start(bf16[8,3,16,1152]{3,2,1,0:T(8,128)(2,1)} %get-tuple-element.230), channel_id=1, source_target_pairs={{0,8},{1,9},{2,10},{3,11},{4,12},{5,13},{6,14},{7,15},{8,0},{9,1},... | collective-permute-start | bytes 2654216 | tf_op jit(solution)/shard_map/ppermute | solution.py:199
  89.8 45.5 %copy-start.1 = (bf16[1152,1152]{1,0:T(8,128)(2,1)S(1)}, bf16[1152,1152]{1,0:T(8,128)(2,1)}, u32[]{:S(2)}) copy-start(bf16[1152,1152]{1,0:T(8,128)(2,1)} %get-tuple-element.174.refs_5_) | copy-start | bytes 7962628 | tf_op jit(solution)/shard_map/cond
  89.8 45.5 %copy-start.5 = (f32[256,256]{1,0:T(8,128)S(1)}, f32[256,256]{1,0:T(8,128)}, u32[]{:S(2)}) copy-start(f32[256,256]{1,0:T(8,128)} %get-tuple-element.173.refs_4_) | copy-start | bytes 786436 | tf_op jit(solution)/shard_map/cond
  159.9 5.6 %copy-start.4 = (f32[256,256]{1,0:T(8,128)S(1)}, f32[256,256]{1,0:T(8,128)}, u32[]{:S(2)}) copy-start(f32[256,256]{1,0:T(8,128)} %copy-done.3) | copy-start | bytes 786436
  161.0 51.7 %collective-permute-start.6 = (bf16[128,1152]{1,0:T(8,128)(2,1)S(1)}, bf16[128,1152]{1,0:T(8,128)(2,1)S(1)}, u32[]{:S(2)}, u32[]{:S(2)}) collective-permute-start(bf16[128,1152]{1,0:T(8,128)(2,1)S(1)} %bitcast.51), channel_id=1, source_target_pairs={{0,24},{1,25},{2,26},{3,27},{4,28},{5,29},{6,30},{7,31},{8,16},{9,... | collective-permute-start | bytes 884744 | tf_op jit(solution)/shard_map/ppermute | solution.py:199
  162.6 50.1 %collective-permute-start.7 = (bf16[128,1152]{1,0:T(8,128)(2,1)S(1)}, bf16[128,1152]{1,0:T(8,128)(2,1)S(1)}, u32[]{:S(2)}, u32[]{:S(2)}) collective-permute-start(bf16[128,1152]{1,0:T(8,128)(2,1)S(1)} %bitcast.50), channel_id=1, source_target_pairs={{0,16},{1,17},{2,18},{3,19},{4,20},{5,21},{6,22},{7,23},{8,24},{9,... | collective-permute-start | bytes 884744 | tf_op jit(solution)/shard_map/ppermute | solution.py:199
  162.6 50.1 %collective-permute-start.8 = (bf16[128,1152]{1,0:T(8,128)(2,1)S(1)}, bf16[128,1152]{1,0:T(8,128)(2,1)S(1)}, u32[]{:S(2)}, u32[]{:S(2)}) collective-permute-start(bf16[128,1152]{1,0:T(8,128)(2,1)S(1)} %bitcast.49), channel_id=1, source_target_pairs={{0,8},{1,9},{2,10},{3,11},{4,12},{5,13},{6,14},{7,15},{8,0},{9,1},... | collective-permute-start | bytes 884744 | tf_op jit(solution)/shard_map/ppermute | solution.py:199

commit v7 on v6

--- a/solution.py
+++ b/solution.py
@@ -12,7 +12,7 @@
 LANES = 128
 SUB = 8
 HI = 4
-NEAR = (0, 3, 2, 1)
+NEAR = (0, 3, 1, 2)
 AXES = ("tm", "pix")
 
 

time: 215 us -> 215 us (level)
  no operation moved by 1% of the time
where the time goes in v7:
time: 215 us
  blocking collectives  104 us (48%)
  waiting for transfers between devices  59.5 us (28%)
  Pallas kernels  26.8 us (12%)
  starting transfers between devices  19.1 us (9%)
    all_to_all x2, blocking collectives, across(): lax.all_to_all(a, AXES, split_axis=0, concat_axis=0, tiled=True, axis_ind...  64.3 us
    all_to_all x1, blocking collectives, finish_second(): lax.all_to_all(out.reshape(frames, tall, feats), AXES, split_axis=0, conc...  40.1 us
    all_to_all x1, waiting for transfers between devices, across(): lax.all_to_all(a, AXES, split_axis=0, concat_axis=0, tiled=True, axis_ind...  39.9 us
    ppermute x9, waiting for transfers between devices, along(): return lax.ppermute(a, ('pix', 'tm'), pairs)  19.6 us
    ppermute x9, starting transfers between devices, along(): return lax.ppermute(a, ('pix', 'tm'), pairs)  14.6 us
    pallas_call x6, Pallas kernels, mover(): pl.pallas_call(kernel, grid_spec=pltpu.PrefetchScalarGridSpec(num_scalar_...  13.9 us
    pallas_call x2, Pallas kernels, attend(): pl.pallas_call(functools.partial(attend_kernel, outer is not None), grid_...  12.9 us
    all_to_all x1, starting transfers between devices, across(): lax.all_to_all(a, AXES, split_axis=0, concat_axis=0, tiled=True, axis_ind...  4.51 us
  transfers between devices with their start and end apart: 10, of which 3 were waited for; matrix products, arithmetic and copies ran while one was open for 0% of the time, Pallas kernels for 11%

profile of v7, /device:TPU:0, one launch (start us, length us, event | category | flops | bytes accessed | tf_op | source)
XLA Modules:
  0.0 214.7 jit_solution(10316817449232209893)
XLA Ops:
  0.0 3.0 %shard_map.55 = (bf16[8,3,16,1152]{3,2,1,0:T(8,128)(2,1)}, bf16[8,3,16,1152]{3,2,1,0:T(8,128)(2,1)}, bf16[8,3,16,1152]{3,2,1,0:T(8,128)(2,1)}) custom-call(s32[1]{0:T(128)} %bitcast.14.z_ref, bf16[64,16,1152]{2,1,0:T(8,128)(2,1)} %bitcast.37, bf16[64,16,1152]{2,1,0:T(8,128)(2,1)} %bitcast.40, bf16[64,16,1152]{2,1,0:T(8,128)(2,1)} %bitcast.43), custom_call_target="tpu_custom_call" | custom-call | tf_op jit(solution)/shard_map/pallas_call | solution.py:41
  3.0 5.1 %collective-permute-start = (bf16[8,3,16,1152]{3,2,1,0:T(8,128)(2,1)}, bf16[8,3,16,1152]{3,2,1,0:T(8,128)(2,1)}, u32[]{:S(2)}, u32[]{:S(2)}) collective-permute-start(bf16[8,3,16,1152]{3,2,1,0:T(8,128)(2,1)} %get-tuple-element.224), channel_id=1, source_target_pairs={{0,24},{1,25},{2,26},{3,27},{4,28},{5,29},{6,30},{7,31},{8,16},{9,... | collective-permute-start | bytes 2654216 | tf_op jit(solution)/shard_map/ppermute | solution.py:199
  8.1 0.0 collective-permute-start.1
  8.1 0.6 collective-permute-start.2
  8.7 0.0 copy-done.6
  8.8 0.5 slice.15
  10.0 0.0 copy-done
  10.0 52.7 %conditional.3 = (bf16[8,3,16,1152]{3,2,1,0:T(8,128)(2,1)}, bf16[8,3,16,1152]{3,2,1,0:T(8,128)(2,1)}, bf16[8,3,16,1152]{3,2,1,0:T(8,128)(2,1)}, bf16[8,3,16,1152...) conditional(s32[]{:T(128)} %bitcast.13, () %tuple.38, (s32[]{:T(128)}, ...), branch_computations={%region_0.1_spmd, %region_1.2_spmd} | conditional | flops 1365312 | bytes 10893916 | solution.py:195
  10.0 3.5 %branch_1_fun.5 = bf16[4,2,4,3,16,1152]{5,4,3,2,1,0:T(8,128)(2,1)} custom-call(s32[1]{0:T(128)} %bitcast.z_ref, bf16[2,4,4,2,16,1152]{5,4,3,2,1,0:T(8,128)(2,1)S(1)} %bitcast.39, bf16[2,4,4,2,16,1152]{5,4,3,2,1,0:T(8,128)(2,1)} %bitcast.42, bf16[2,4,4,2,16,1152]{5,4,3,2,1,0:T(8,128)(2,1)} %bitcast.45), custom_call_target="tpu_custom_call" | custom-call | tf_op jit(solution)/shard_map/cond/branch_1_fun/pallas_call | solution.py:41
  13.6 4.5 %all-to-all-start.3 = ((bf16[8,4,3,16,1152]{4,3,2,1,0:T(8,128)(2,1)}), bf16[8,4,3,16,1152]{4,3,2,1,0:T(8,128)(2,1)}, u32[]{:S(2)}, u32[]{:S(2)}) async-start(bf16[8,4,3,16,1152]{4,3,2,1,0:T(8,128)(2,1)} %bitcast.46), calls=%async_computation.3 | async-start | bytes 7077888 | tf_op jit(solution)/shard_map/cond/branch_1_fun/all_to_all | solution.py:202
  18.1 1.3 branch_1_fun.7
  19.4 0.4 fusion.5
  19.8 39.9 %all-to-all-done.3.refs_0_ = bf16[8,4,3,16,1152]{4,3,2,1,0:T(8,128)(2,1)} async-done(((bf16[8,4,3,16,1152]{4,3,2,1,0:T(8,128)(2,1)}), bf16[8,4,3,16,1152]{4,3,2,1,0:T(8,128)(2,1)}, u32[]{:S(2)}, u32[]{:S(2)}) %all-to-all-start.3) | async-done | bytes 3538976 | tf_op jit(solution)/shard_map/cond/branch_1_fun/all_to_all | solution.py:202
  59.7 3.0 %branch_1_fun.6 = (bf16[8,3,16,1152]{3,2,1,0:T(8,128)(2,1)}, bf16[8,3,16,1152]{3,2,1,0:T(8,128)(2,1)}, bf16[8,3,16,1152]{3,2,1,0:T(8,128)(2,1)}, bf16[8,3,16,1152]{3,2,1,0:T(8,128)(2,1)}) custom-call(s32[1]{0:T(128)} %bitcast.z_ref, bf16[8,4,3,16,1152]{4,3,2,1,0:T(8,128)(2,1)} %all-to-all-done.3.refs_0_), custom_call_target="tpu_custom_call" | custom-call | tf_op jit(solution)/shard_map/cond/branch_1_fun/pallas_call | solution.py:41
  62.7 0.0 copy-start.2
  62.8 0.0 copy-start.3
  62.8 0.0 collective-permute-done.refs_1_
  62.8 0.0 collective-permute-done.1.refs_2_
  62.8 0.9 copy-done.2
  63.7 0.1 copy-done.3
  63.8 1.8 shard_map.56.refs_1_
  65.6 18.5 %collective-permute-done.2.refs_0_ = bf16[8,3,16,1152]{3,2,1,0:T(8,128)(2,1)} collective-permute-done((bf16[8,3,16,1152]{3,2,1,0:T(8,128)(2,1)}, bf16[8,3,16,1152]{3,2,1,0:T(8,128)(2,1)}, u32[]{:S(2)}, u32[]{:S(2)}) %collective-permute-start.2) | collective-permute-done | bytes 884768 | tf_op jit(solution)/shard_map/ppermute | solution.py:199
  84.1 2.6 %collective-permute-start.3 = (bf16[8,3,16,1152]{3,2,1,0:T(8,128)(2,1)}, bf16[8,3,16,1152]{3,2,1,0:T(8,128)(2,1)}, u32[]{:S(2)}, u32[]{:S(2)}) collective-permute-start(bf16[8,3,16,1152]{3,2,1,0:T(8,128)(2,1)} %get-tuple-element.228), channel_id=1, source_target_pairs={{0,24},{1,25},{2,26},{3,27},{4,28},{5,29},{6,30},{7,31},{8,16},{9,... | collective-permute-start | bytes 2654216 | tf_op jit(solution)/shard_map/ppermute | solution.py:199
  86.7 0.0 collective-permute-start.4
  86.7 1.8 collective-permute-start.5
  88.5 1.2 shard_map.57
  89.7 70.2 %conditional.4 = (bf16[8,4,2,8,1152]{4,3,2,1,0:T(8,128)(2,1)S(1)}) conditional(s32[]{:T(128)} %bitcast.13, () %tuple.42, (s32[]{:T(128)}, bf16[8,4,3,16,1152]{4,3,2,1,0:T(8,128)(2,1)S(1)}, f32[256,256]{1,0:T(8,128)}, bf16[1152,1152]{1,0:T(8,128)(2,1)}) %tuple.63), branch_computations={%region_2.3_spmd, %region_3.4_spmd} | conditional | bytes 21102656 | solution.py:195
  89.8 0.0 copy-start.1
  89.8 0.0 copy-start.5
  89.8 45.5 %all_to_all.16 = bf16[8,4,3,16,1152]{4,3,2,1,0:T(8,128)(2,1)S(1)} all-to-all(bf16[8,4,3,16,1152]{4,3,2,1,0:T(8,128)(2,1)S(1)} %get-tuple-element.172), channel_id=1, replica_groups={{0,4,1,5,2,6,3,7},{8,12,9,13,10,14,11,15},{16,20,17,21,18,22,19,23},{24..., dimensions={0} | all-to-all | bytes 7077888 | tf_op jit(solution)/shard_map/cond/branch_1_fun/all_to_all | solution.py:202
  135.3 0.0 copy-done.1
  135.3 5.8 %branch_1_fun.8 = bf16[8,4,2,8,1152]{4,3,2,1,0:T(8,128)(2,1)S(1)} custom-call(s32[1]{0:T(128)} %bitcast.5.z_ref, bf16[8,4,3,2,8,1152]{5,4,3,2,1,0:T(8,128)(2,1)S(1)} %bitcast.32, bf16[8,4,3,2,8,1152]{5,4,3,2,1,0:T(8,128)(2,1)S(1)} %bitcast.33, bf16[8,4,3,2,8,1152]{5,4,3,2,1,0:T(8,128)(2,1)S(1)} %bitcast.34, bf16[8,4,3,2,8,1152]{5,4,3,2,1,0:T(8,128)(2,1)S(1)} %bitcast.35, ...), custom_call_target="tpu_custom_call" | custom-call | tf_op jit(solution)/shard_map/cond/branch_1_fun/pallas_call | solution.py:124
  141.1 18.8 %all_to_all.17 = bf16[8,4,2,8,1152]{4,3,2,1,0:T(8,128)(2,1)S(1)} all-to-all(bf16[8,4,2,8,1152]{4,3,2,1,0:T(8,128)(2,1)S(1)} %branch_1_fun.8), channel_id=1, replica_groups={{0,4,1,5,2,6,3,7},{8,12,9,13,10,14,11,15},{16,20,17,21,18,22,19,23},{24..., dimensions={0} | all-to-all | bytes 2359296 | tf_op jit(solution)/shard_map/cond/branch_1_fun/all_to_all | solution.py:202
  159.9 0.0 collective-permute-done.3
  159.9 0.0 collective-permute-done.4
  159.9 1.1 collective-permute-done.5
  161.0 0.1 fusion.21
  161.1 1.6 collective-permute-start.6
  162.7 0.0 collective-permute-start.7
  162.7 2.9 %collective-permute-start.8 = (bf16[128,1152]{1,0:T(8,128)(2,1)S(1)}, bf16[128,1152]{1,0:T(8,128)(2,1)S(1)}, u32[]{:S(2)}, u32[]{:S(2)}) collective-permute-start(bf16[128,1152]{1,0:T(8,128)(2,1)S(1)} %bitcast.49), channel_id=1, source_target_pairs={{0,16},{1,17},{2,18},{3,19},{4,20},{5,21},{6,22},{7,23},{8,24},{9,... | collective-permute-start | bytes 884744 | tf_op jit(solution)/shard_map/ppermute | solution.py:199
  165.5 47.2 %conditional.5 = (bf16[32,16,1152]{2,1,0:T(8,128)(2,1)S(1)}) conditional(s32[]{:T(128)} %bitcast.13, () %tuple.45, (s32[]{:T(128)}, bf16[8,3,16,1152]{3,2,1,0:T(8,128)(2,1)}, bf16[8,3,16,1152]{3,2,1,0:T(8,128)(2,1)}, bf16[8,3,16,1152]{3,2,1,0:T(8,128)(2,1)}, bf16[8,3,16,1152]{3,2,1,0:T(8,128)(2,1)}, /*index=5*/f32[256,256]{1,0:T(8,128)S(1)}, ...), branch_computations={%region_4.5_spmd, %region_5.6_spmd} | conditional | bytes 2359304 | solution.py:195
  165.5 7.1 %branch_1_fun.9 = bf16[4,4,2,2,8,1152]{5,4,3,2,1,0:T(8,128)(2,1)S(1)} custom-call(s32[1]{0:T(128)} %bitcast.7.z_ref, bf16[8,1,3,2,8,1152]{5,4,3,2,1,0:T(8,128)(2,1)} %bitcast.8.refs_0_, bf16[8,1,3,2,8,1152]{5,4,3,2,1,0:T(8,128)(2,1)} %bitcast.9.refs_1_, bf16[8,1,3,2,8,1152]{5,4,3,2,1,0:T(8,128)(2,1)} %bitcast.10.refs_2_, ...), custom_call_target="tpu_custom_call" | custom-call | tf_op jit(solution)/shard_map/cond/branch_1_fun/pallas_call | solution.py:124
  172.6 40.1 %all_to_all.18 = bf16[32,16,1152]{2,1,0:T(8,128)(2,1)S(1)} all-to-all(bf16[32,16,1152]{2,1,0:T(8,128)(2,1)S(1)} %bitcast.36), channel_id=1, replica_groups=mesh['pix'=8,'tm'=4] {'tm','pix'}, dimensions={0} | all-to-all | bytes 2359296 | tf_op jit(solution)/shard_map/cond/branch_1_fun/all_to_all | solution.py:259
  212.8 0.0 collective-permute-done.6
  212.8 0.0 collective-permute-done.7
  212.8 0.0 collective-permute-done.8
  212.8 0.1 broadcast_in_dim.38
  213.1 1.6 pad_maximum_fusion
  (17 shorter events, 0.2 us)
Async XLA Ops:
  0.0 8.8 %copy-start.6 = (s32[8,8]{1,0:T(8,128)S(1)}, s32[8,8]{1,0:T(8,128)}, u32[]{:S(2)}) copy-start(s32[8,8]{1,0:T(8,128)} %param.14) | copy-start | bytes 772
  0.0 10.0 %copy-start = (bf16[1,1,1024,1152]{3,2,1,0:T(8,128)(2,1)S(1)}, bf16[1,1,1024,1152]{3,2,1,0:T(8,128)(2,1)}, u32[]{:S(2)}) copy-start(bf16[1,1,1024,1152]{3,2,1,0:T(8,128)(2,1)} %param.11) | copy-start | bytes 7077892
  3.0 59.8 %collective-permute-start = (bf16[8,3,16,1152]{3,2,1,0:T(8,128)(2,1)}, bf16[8,3,16,1152]{3,2,1,0:T(8,128)(2,1)}, u32[]{:S(2)}, u32[]{:S(2)}) collective-permute-start(bf16[8,3,16,1152]{3,2,1,0:T(8,128)(2,1)} %get-tuple-element.224), channel_id=1, source_target_pairs={{0,24},{1,25},{2,26},{3,27},{4,28},{5,29},{6,30},{7,31},{8,16},{9,... | collective-permute-start | bytes 2654216 | tf_op jit(solution)/shard_map/ppermute | solution.py:199
  8.1 54.7 %collective-permute-start.1 = (bf16[8,3,16,1152]{3,2,1,0:T(8,128)(2,1)}, bf16[8,3,16,1152]{3,2,1,0:T(8,128)(2,1)}, u32[]{:S(2)}, u32[]{:S(2)}) collective-permute-start(bf16[8,3,16,1152]{3,2,1,0:T(8,128)(2,1)} %get-tuple-element.225), channel_id=1, source_target_pairs={{0,8},{1,9},{2,10},{3,11},{4,12},{5,13},{6,14},{7,15},{8,0},{9,1},... | collective-permute-start | bytes 2654216 | tf_op jit(solution)/shard_map/ppermute | solution.py:199
  8.1 76.0 %collective-permute-start.2 = (bf16[8,3,16,1152]{3,2,1,0:T(8,128)(2,1)}, bf16[8,3,16,1152]{3,2,1,0:T(8,128)(2,1)}, u32[]{:S(2)}, u32[]{:S(2)}) collective-permute-start(bf16[8,3,16,1152]{3,2,1,0:T(8,128)(2,1)} %get-tuple-element.226), channel_id=1, source_target_pairs={{0,16},{1,17},{2,18},{3,19},{4,20},{5,21},{6,22},{7,23},{8,24},{9,... | collective-permute-start | bytes 2654216 | tf_op jit(solution)/shard_map/ppermute | solution.py:199
  13.6 46.1 %all-to-all-start.3 = ((bf16[8,4,3,16,1152]{4,3,2,1,0:T(8,128)(2,1)}), bf16[8,4,3,16,1152]{4,3,2,1,0:T(8,128)(2,1)}, u32[]{:S(2)}, u32[]{:S(2)}) async-start(bf16[8,4,3,16,1152]{4,3,2,1,0:T(8,128)(2,1)} %bitcast.46), calls=%async_computation.3 | async-start | bytes 7077888 | tf_op jit(solution)/shard_map/cond/branch_1_fun/all_to_all | solution.py:202
  62.7 0.9 copy-start.2
  62.8 1.0 copy-start.3
  84.1 75.8 %collective-permute-start.3 = (bf16[8,3,16,1152]{3,2,1,0:T(8,128)(2,1)}, bf16[8,3,16,1152]{3,2,1,0:T(8,128)(2,1)}, u32[]{:S(2)}, u32[]{:S(2)}) collective-permute-start(bf16[8,3,16,1152]{3,2,1,0:T(8,128)(2,1)} %get-tuple-element.228), channel_id=1, source_target_pairs={{0,24},{1,25},{2,26},{3,27},{4,28},{5,29},{6,30},{7,31},{8,16},{9,... | collective-permute-start | bytes 2654216 | tf_op jit(solution)/shard_map/ppermute | solution.py:199
  86.7 73.2 %collective-permute-start.4 = (bf16[8,3,16,1152]{3,2,1,0:T(8,128)(2,1)}, bf16[8,3,16,1152]{3,2,1,0:T(8,128)(2,1)}, u32[]{:S(2)}, u32[]{:S(2)}) collective-permute-start(bf16[8,3,16,1152]{3,2,1,0:T(8,128)(2,1)} %get-tuple-element.229), channel_id=1, source_target_pairs={{0,8},{1,9},{2,10},{3,11},{4,12},{5,13},{6,14},{7,15},{8,0},{9,1},... | collective-permute-start | bytes 2654216 | tf_op jit(solution)/shard_map/ppermute | solution.py:199
  86.7 74.3 %collective-permute-start.5 = (bf16[8,3,16,1152]{3,2,1,0:T(8,128)(2,1)}, bf16[8,3,16,1152]{3,2,1,0:T(8,128)(2,1)}, u32[]{:S(2)}, u32[]{:S(2)}) collective-permute-start(bf16[8,3,16,1152]{3,2,1,0:T(8,128)(2,1)} %get-tuple-element.230), channel_id=1, source_target_pairs={{0,16},{1,17},{2,18},{3,19},{4,20},{5,21},{6,22},{7,23},{8,24},{9,... | collective-permute-start | bytes 2654216 | tf_op jit(solution)/shard_map/ppermute | solution.py:199
  89.8 45.5 %copy-start.1 = (bf16[1152,1152]{1,0:T(8,128)(2,1)S(1)}, bf16[1152,1152]{1,0:T(8,128)(2,1)}, u32[]{:S(2)}) copy-start(bf16[1152,1152]{1,0:T(8,128)(2,1)} %get-tuple-element.174.refs_5_) | copy-start | bytes 7962628 | tf_op jit(solution)/shard_map/cond
  89.8 45.5 %copy-start.5 = (f32[256,256]{1,0:T(8,128)S(1)}, f32[256,256]{1,0:T(8,128)}, u32[]{:S(2)}) copy-start(f32[256,256]{1,0:T(8,128)} %get-tuple-element.173.refs_4_) | copy-start | bytes 786436 | tf_op jit(solution)/shard_map/cond
  159.9 5.6 %copy-start.4 = (f32[256,256]{1,0:T(8,128)S(1)}, f32[256,256]{1,0:T(8,128)}, u32[]{:S(2)}) copy-start(f32[256,256]{1,0:T(8,128)} %copy-done.3) | copy-start | bytes 786436
  161.1 51.7 %collective-permute-start.6 = (bf16[128,1152]{1,0:T(8,128)(2,1)S(1)}, bf16[128,1152]{1,0:T(8,128)(2,1)S(1)}, u32[]{:S(2)}, u32[]{:S(2)}) collective-permute-start(bf16[128,1152]{1,0:T(8,128)(2,1)S(1)} %bitcast.51), channel_id=1, source_target_pairs={{0,24},{1,25},{2,26},{3,27},{4,28},{5,29},{6,30},{7,31},{8,16},{9,... | collective-permute-start | bytes 884744 | tf_op jit(solution)/shard_map/ppermute | solution.py:199
  162.7 50.1 %collective-permute-start.7 = (bf16[128,1152]{1,0:T(8,128)(2,1)S(1)}, bf16[128,1152]{1,0:T(8,128)(2,1)S(1)}, u32[]{:S(2)}, u32[]{:S(2)}) collective-permute-start(bf16[128,1152]{1,0:T(8,128)(2,1)S(1)} %bitcast.50), channel_id=1, source_target_pairs={{0,8},{1,9},{2,10},{3,11},{4,12},{5,13},{6,14},{7,15},{8,0},{9,1},... | collective-permute-start | bytes 884744 | tf_op jit(solution)/shard_map/ppermute | solution.py:199
  162.7 50.1 %collective-permute-start.8 = (bf16[128,1152]{1,0:T(8,128)(2,1)S(1)}, bf16[128,1152]{1,0:T(8,128)(2,1)S(1)}, u32[]{:S(2)}, u32[]{:S(2)}) collective-permute-start(bf16[128,1152]{1,0:T(8,128)(2,1)S(1)} %bitcast.49), channel_id=1, source_target_pairs={{0,16},{1,17},{2,18},{3,19},{4,20},{5,21},{6,22},{7,23},{8,24},{9,... | collective-permute-start | bytes 884744 | tf_op jit(solution)/shard_map/ppermute | solution.py:199
